TPU v7x, 128 devices: a whole 4x4x4 slice. The times are simulated.
128 devices in a mesh: dp: 8 (over y, x_hi), head: 16 (over z, x_lo, core).
Axes of the slice: x: 4 (x_hi: 2, x_lo: 2; x = x_hi * 2 + x_lo), y: 4, z: 4, core: 2. Of those that a mesh axis runs over, the one named last changes fastest.
Arguments:
- tokens: bfloat16 [16384, 2048], P(('dp', 'head')), may hold values from -6 to 6
- cotangent: bfloat16 [16384, 2048], P(('dp', 'head')), may hold values from -6 to 6
- doc_spans: int32 [8, 3], P('dp'), may hold values from 1 to 16, 32 in all within a row
- norm1_gain: float32 [2048], replicated, may hold values from 0.5 to 1.5
- q_weight: bfloat16 [2048, 2048], P('dp', 'head'), may hold values from -0.125 to 0.125
- k_weight: bfloat16 [2048, 2048], P('dp', 'head'), may hold values from -0.125 to 0.125
- v_weight: bfloat16 [2048, 2048], P('dp', 'head'), may hold values from -0.125 to 0.125
- gate_out_weight: bfloat16 [2048, 2048], P('dp', 'head'), may hold values from -0.125 to 0.125
- decay_weight: bfloat16 [2048, 16, 2], P('dp', 'head'), may hold values from -0.125 to 0.125
- conv_weight: bfloat16 [3, 4, 2048], P(None, None, ('head', 'dp')), may hold values from -0.796875 to 0.796875
- gate_params: float32 [2, 16], P(None, 'head'), may hold values from -4 to 0
- out_gain: float32 [128], replicated, may hold values from 0.5 to 1.5
- out_weight: bfloat16 [2048, 2048], P('dp', 'head'), may hold values from -0.1875 to 0.1875
- norm2_gain: float32 [2048], replicated, may hold values from 0.5 to 1.5
- gate_weight: bfloat16 [2048, 5632], P('dp', 'head'), may hold values from -0.125 to 0.125
- up_weight: bfloat16 [2048, 5632], P('dp', 'head'), may hold values from -0.125 to 0.125
- down_weight: bfloat16 [2048, 5632], P('dp', 'head'), may hold values from -0.15625 to 0.15625
Outputs:
- block_out: bfloat16 [16384, 2048], P(('dp', 'head'))
- tokens_grad: float32 [16384, 2048], P(('dp', 'head'))
- norm1_gain_grad: float32 [2048], replicated
- q_weight_grad: float32 [2048, 2048], P('dp', 'head')
- k_weight_grad: float32 [2048, 2048], P('dp', 'head')
- v_weight_grad: float32 [2048, 2048], P('dp', 'head')
- gate_out_weight_grad: float32 [2048, 2048], P('dp', 'head')
- decay_weight_grad: float32 [2048, 16, 2], P('dp', 'head')
- conv_weight_grad: float32 [3, 4, 2048], P(None, None, ('head', 'dp'))
- gate_params_grad: float32 [2, 16], P(None, 'head')
- out_gain_grad: float32 [128], replicated
- out_weight_grad: float32 [2048, 2048], P('dp', 'head')
- norm2_gain_grad: float32 [2048], replicated
- gate_weight_grad: float32 [2048, 5632], P('dp', 'head')
- up_weight_grad: float32 [2048, 5632], P('dp', 'head')
- down_weight_grad: float32 [2048, 5632], P('dp', 'head')
Inputs may be any that keep to these rules, and one draw needn't show every extreme that they name: `doc_spans`: each group's 3 lengths sum to 32, and the longest is exactly half of that.
All inputs are finite; a program needn't handle non-finite values.
Results may differ from a plain program's by a relative error of at most 0.033.
Values may be sent and summed in bfloat16 or wider, within the bound.
No kernel may reach another device: no remote copies, remote signals or barrier semaphores. Data moves between devices by JAX's collectives and lax.ppermute only.
A program may use at most 256 MiB of HBM per device.

v0:
```python
from functools import partial

import jax
import jax.numpy as jnp
from jax import lax
from jax.sharding import PartitionSpec as P

HEADS = 16
SPAN = 64


def product(form, left, right):
    return jnp.einsum(
        form, left, right, precision=lax.Precision.HIGHEST, preferred_element_type=jnp.float32
    )


def plain_product(left, right):
    return jnp.dot(left, right, preferred_element_type=jnp.float32)


def against(left, right):
    return lax.dot_general(
        left, right, (((1,), (1,)), ((), ())), preferred_element_type=jnp.float32
    )


def over_rows(left, right):
    return lax.dot_general(
        left, right, (((0,), (0,)), ((), ())), preferred_element_type=jnp.float32
    )


def rms_rows(values, gain):
    return values * lax.rsqrt(jnp.mean(values * values, axis=-1, keepdims=True) + 1e-05) * gain


def doc_masks(doc_lengths, seq_length, block_len, tap_count):
    doc_bounds = jnp.cumsum(doc_lengths)[:-1] * block_len
    positions = jnp.arange(seq_length, dtype=jnp.int32)
    doc_index = jnp.sum((positions[:, None] >= doc_bounds[None, :]).astype(jnp.int32), axis=1)
    same_doc = []
    for offset in range(1, tap_count):
        earlier_doc = jnp.concatenate(
            [jnp.full((offset,), -1, jnp.int32), doc_index[: seq_length - offset]]
        )
        same_doc.append((earlier_doc == doc_index).astype(jnp.float32))
    block_starts = jnp.arange(seq_length // block_len, dtype=jnp.int32) * block_len
    doc_starts = jnp.any(block_starts[:, None] == doc_bounds[None, :], axis=1) | (block_starts == 0)
    carry_mask = 1.0 - doc_starts.astype(jnp.float32)
    return (same_doc, carry_mask)


def short_conv(raw_in, tap_weights, same_doc):
    tap_count = tap_weights.shape[0]
    seq_length = raw_in.shape[0]
    summed = raw_in * tap_weights[tap_count - 1]
    for offset in range(1, tap_count):
        shifted = jnp.concatenate(
            [jnp.zeros((offset, raw_in.shape[1]), raw_in.dtype), raw_in[: seq_length - offset]],
            axis=0,
        )
        summed = (
            summed + shifted * same_doc[offset - 1][:, None] * tap_weights[tap_count - 1 - offset]
        )
    return jax.nn.silu(summed)


def delta_head(queries, keys_in, values_in, beta_gate, decay_log, carry_mask, block_len):
    seq_length, head_width = queries.shape
    block_count = seq_length // block_len
    queries = queries.reshape(block_count, block_len, head_width)
    keys_in = keys_in.reshape(block_count, block_len, head_width)
    values_in = values_in.reshape(block_count, block_len, head_width)
    beta_gate = beta_gate.reshape(block_count, block_len)
    log_decay_sum = jnp.cumsum(decay_log.reshape(block_count, block_len), axis=1)
    positions = jnp.arange(block_len)
    lower_mask = positions[:, None] >= positions[None, :]
    strict_mask = positions[:, None] > positions[None, :]
    log_gap = log_decay_sum[:, :, None] - log_decay_sum[:, None, :]
    decay_mask = jnp.where(lower_mask, jnp.exp(jnp.where(lower_mask, log_gap, 0.0)), 0.0)
    keys_beta = keys_in * beta_gate[:, :, None]
    strict_part = jnp.where(
        strict_mask, product("cip,cjp->cij", keys_beta, keys_in) * decay_mask, 0.0
    )
    identity = jnp.eye(block_len, dtype=jnp.float32)
    inverse = identity - strict_part
    rounds_left = block_len.bit_length() - 2
    nil_power = product("cij,cjk->cik", strict_part, strict_part)
    for doubling in range(rounds_left):
        inverse = product("cij,cjk->cik", inverse, identity + nil_power)
        if doubling + 1 < rounds_left:
            nil_power = product("cij,cjk->cik", nil_power, nil_power)
    fresh_base = product("cij,cjp->cip", inverse, values_in * beta_gate[:, :, None])
    key_weighted = product("cij,cjp->cip", inverse, keys_beta * jnp.exp(log_decay_sum)[:, :, None])
    inner_scores = jnp.where(
        lower_mask, product("cip,cjp->cij", queries, keys_in) * decay_mask, 0.0
    )
    query_faded = queries * jnp.exp(log_decay_sum)[:, :, None]
    key_tail = jnp.exp(log_decay_sum[:, -1:] - log_decay_sum)[:, :, None] * keys_in
    span_decay = jnp.exp(log_decay_sum[:, -1])

    def span_step(state_mat, pieces):
        base_now, weighted_now, scores_now, faded_now, tail_now, decay_now, carry_now = pieces
        state_mat = state_mat * carry_now
        fresh_vals = base_now - product("ij,jk->ik", weighted_now, state_mat)
        span_out = product("ij,jk->ik", faded_now, state_mat) + product(
            "ij,jk->ik", scores_now, fresh_vals
        )
        state_mat = state_mat * decay_now + product("ip,iv->pv", tail_now, fresh_vals)
        return (state_mat, span_out)

    state_start = jnp.zeros((head_width, head_width), jnp.float32)
    _, span_outs = lax.scan(
        jax.checkpoint(span_step),
        state_start,
        (fresh_base, key_weighted, inner_scores, query_faded, key_tail, span_decay, carry_mask),
    )
    return span_outs.reshape(seq_length, head_width)


def token_mixer(
    q_raw, k_raw, v_raw, gate_raw, decay_raw, conv_taps, gate_par, out_gain, doc_lengths, block_len
):
    seq_length = q_raw.shape[0]
    head_count = gate_par.shape[1]
    head_width = q_raw.shape[1] // head_count
    same_doc, carry_mask = doc_masks(doc_lengths, seq_length, block_len, conv_taps.shape[1])
    queries = short_conv(q_raw, conv_taps[0], same_doc).reshape(seq_length, head_count, head_width)
    keys_in = short_conv(k_raw, conv_taps[1], same_doc).reshape(seq_length, head_count, head_width)
    values_in = short_conv(v_raw, conv_taps[2], same_doc).reshape(
        seq_length, head_count, head_width
    )
    queries = (
        queries
        * lax.rsqrt(jnp.sum(queries * queries, axis=-1, keepdims=True) + 1e-06)
        * head_width ** (-0.5)
    )
    keys_in = keys_in * lax.rsqrt(jnp.sum(keys_in * keys_in, axis=-1, keepdims=True) + 1e-06)
    gate_pair = decay_raw.reshape(seq_length, head_count, 2)
    beta_gate = jax.nn.sigmoid(gate_pair[:, :, 1])
    decay_log = -jnp.exp(gate_par[0]) * jax.nn.softplus(gate_pair[:, :, 0] + gate_par[1])
    per_head = jax.vmap(
        partial(delta_head, carry_mask=carry_mask, block_len=block_len),
        in_axes=(1, 1, 1, 1, 1),
        out_axes=1,
    )
    core_out = per_head(queries, keys_in, values_in, beta_gate, decay_log)
    scaled = (
        core_out
        * lax.rsqrt(jnp.mean(core_out * core_out, axis=-1, keepdims=True) + 1e-05)
        * out_gain
    )
    gate_heads = gate_raw.reshape(seq_length, head_count, head_width)
    return (scaled * jax.nn.silu(gate_heads)).reshape(seq_length, head_count * head_width)


def body(
    tokens,
    cotangent,
    doc_spans,
    norm1_gain,
    q_weight,
    k_weight,
    v_weight,
    gate_out_weight,
    decay_weight,
    conv_weight,
    gate_params,
    out_gain,
    out_weight,
    norm2_gain,
    gate_weight,
    up_weight,
    down_weight,
):
    rows_in = tokens.astype(jnp.float32)
    doc_lengths = doc_spans[0]
    w_query, w_key, w_value, w_outgate, w_decay, w_conv, w_out, w_gate, w_up, w_down = (
        lax.all_gather(q_weight, "dp", axis=0, tiled=True),
        lax.all_gather(k_weight, "dp", axis=0, tiled=True),
        lax.all_gather(v_weight, "dp", axis=0, tiled=True),
        lax.all_gather(gate_out_weight, "dp", axis=0, tiled=True),
        lax.all_gather(decay_weight, "dp", axis=0, tiled=True),
        lax.all_gather(conv_weight, "dp", axis=2, tiled=True),
        lax.all_gather(out_weight, "dp", axis=0, tiled=True),
        lax.all_gather(gate_weight, "dp", axis=0, tiled=True),
        lax.all_gather(up_weight, "dp", axis=0, tiled=True),
        lax.all_gather(down_weight, "dp", axis=0, tiled=True),
    )
    model_width = w_query.shape[0]
    decay_flat = w_decay.reshape(model_width, -1)
    normed1 = rms_rows(rows_in, norm1_gain)
    group_one = lax.all_gather(normed1.astype(jnp.bfloat16), "head", axis=0, tiled=True)
    q_raw = plain_product(group_one, w_query)
    k_raw = plain_product(group_one, w_key)
    v_raw = plain_product(group_one, w_value)
    go_raw = plain_product(group_one, w_outgate)
    decay_raw = plain_product(group_one, decay_flat)
    local_mixer = partial(token_mixer, doc_lengths=doc_lengths, block_len=SPAN)
    mixed, mixer_pull = jax.vjp(
        local_mixer,
        q_raw,
        k_raw,
        v_raw,
        go_raw,
        decay_raw,
        w_conv.astype(jnp.float32),
        gate_params,
        out_gain,
    )
    mixed_low = mixed.astype(jnp.bfloat16)
    attn_rows = lax.psum_scatter(
        against(mixed_low, w_out).astype(jnp.bfloat16), "head", scatter_dimension=0, tiled=True
    ).astype(jnp.float32)
    resid = rows_in + attn_rows
    normed2 = rms_rows(resid, norm2_gain)
    group_two = lax.all_gather(normed2.astype(jnp.bfloat16), "head", axis=0, tiled=True)
    gate_pre = plain_product(group_two, w_gate)
    up_pre = plain_product(group_two, w_up)
    hidden_low = (jax.nn.silu(gate_pre) * up_pre).astype(jnp.bfloat16)
    mlp_rows = lax.psum_scatter(
        against(hidden_low, w_down).astype(jnp.bfloat16), "head", scatter_dimension=0, tiled=True
    ).astype(jnp.float32)
    block_out = (resid + mlp_rows).astype(jnp.bfloat16)
    grad_out = cotangent.astype(jnp.float32)
    group_grad = lax.all_gather(cotangent, "head", axis=0, tiled=True)
    hidden_grad = plain_product(group_grad, w_down)
    down_grad = over_rows(group_grad, hidden_low)
    sigmoid_gate = jax.nn.sigmoid(gate_pre)
    gate_grad_low = (
        hidden_grad * up_pre * sigmoid_gate * (1.0 + gate_pre * (1.0 - sigmoid_gate))
    ).astype(jnp.bfloat16)
    up_grad_low = (hidden_grad * gate_pre * sigmoid_gate).astype(jnp.bfloat16)
    group_two = lax.all_gather(
        rms_rows(resid, norm2_gain).astype(jnp.bfloat16), "head", axis=0, tiled=True
    )
    gate_wgrad = over_rows(group_two, gate_grad_low)
    up_wgrad = over_rows(group_two, up_grad_low)
    normed2_grad = lax.psum_scatter(
        (against(gate_grad_low, w_gate) + against(up_grad_low, w_up)).astype(jnp.bfloat16),
        "head",
        scatter_dimension=0,
        tiled=True,
    ).astype(jnp.float32)
    _, norm2_pull = jax.vjp(rms_rows, resid, norm2_gain)
    resid_part, gain2_grad = norm2_pull(normed2_grad)
    resid_grad = grad_out + resid_part
    group_branch = lax.all_gather(resid_grad.astype(jnp.bfloat16), "head", axis=0, tiled=True)
    out_wgrad = over_rows(group_branch, mixed_low)
    mixed_grad = plain_product(group_branch, w_out)
    query_g, key_g, value_g, outgate_g, decay_g, conv_grad, params_grad, outgain_grad = mixer_pull(
        mixed_grad
    )
    grad_lows = [
        piece.astype(jnp.bfloat16) for piece in (query_g, key_g, value_g, outgate_g, decay_g)
    ]
    group_one = lax.all_gather(
        rms_rows(rows_in, norm1_gain).astype(jnp.bfloat16), "head", axis=0, tiled=True
    )
    query_wgrad = over_rows(group_one, grad_lows[0])
    key_wgrad = over_rows(group_one, grad_lows[1])
    value_wgrad = over_rows(group_one, grad_lows[2])
    outgate_wgrad = over_rows(group_one, grad_lows[3])
    decay_wgrad = over_rows(group_one, grad_lows[4]).reshape(w_decay.shape)
    proj_weights = (w_query, w_key, w_value, w_outgate, decay_flat)
    summed = against(grad_lows[0], proj_weights[0])
    for member in range(1, 5):
        summed = summed + against(grad_lows[member], proj_weights[member])
    normed1_grad = lax.psum_scatter(
        summed.astype(jnp.bfloat16), "head", scatter_dimension=0, tiled=True
    ).astype(jnp.float32)
    _, norm1_pull = jax.vjp(rms_rows, rows_in, norm1_gain)
    rows_part, gain1_grad = norm1_pull(normed1_grad)
    tokens_grad = resid_grad + rows_part
    (
        query_sum,
        key_sum,
        value_sum,
        outgate_sum,
        decay_sum,
        conv_sum,
        out_sum,
        gate_sum,
        up_sum,
        down_sum,
    ) = (
        lax.psum_scatter(
            query_wgrad.astype(jnp.bfloat16), "dp", scatter_dimension=0, tiled=True
        ).astype(jnp.float32),
        lax.psum_scatter(
            key_wgrad.astype(jnp.bfloat16), "dp", scatter_dimension=0, tiled=True
        ).astype(jnp.float32),
        lax.psum_scatter(
            value_wgrad.astype(jnp.bfloat16), "dp", scatter_dimension=0, tiled=True
        ).astype(jnp.float32),
        lax.psum_scatter(
            outgate_wgrad.astype(jnp.bfloat16), "dp", scatter_dimension=0, tiled=True
        ).astype(jnp.float32),
        lax.psum_scatter(
            decay_wgrad.astype(jnp.bfloat16), "dp", scatter_dimension=0, tiled=True
        ).astype(jnp.float32),
        lax.psum_scatter(
            conv_grad.astype(jnp.bfloat16), "dp", scatter_dimension=2, tiled=True
        ).astype(jnp.float32),
        lax.psum_scatter(
            out_wgrad.astype(jnp.bfloat16), "dp", scatter_dimension=0, tiled=True
        ).astype(jnp.float32),
        lax.psum_scatter(
            gate_wgrad.astype(jnp.bfloat16), "dp", scatter_dimension=0, tiled=True
        ).astype(jnp.float32),
        lax.psum_scatter(
            up_wgrad.astype(jnp.bfloat16), "dp", scatter_dimension=0, tiled=True
        ).astype(jnp.float32),
        lax.psum_scatter(
            down_grad.astype(jnp.bfloat16), "dp", scatter_dimension=0, tiled=True
        ).astype(jnp.float32),
    )
    local_heads = gate_params.shape[1]
    head_start = lax.axis_index("head") * local_heads
    params_spread = lax.dynamic_update_slice_in_dim(
        jnp.zeros((2, HEADS), jnp.float32), params_grad, head_start, 1
    )
    gain1_total, gain2_total, outgain_total, params_total = lax.psum(
        (gain1_grad, gain2_grad, outgain_grad, params_spread), ("dp", "head")
    )
    params_mine = lax.dynamic_slice_in_dim(params_total, head_start, local_heads, 1)
    return (
        block_out,
        tokens_grad,
        gain1_total,
        query_sum,
        key_sum,
        value_sum,
        outgate_sum,
        decay_sum,
        conv_sum,
        params_mine,
        outgain_total,
        out_sum,
        gain2_total,
        gate_sum,
        up_sum,
        down_sum,
    )


def solution(mesh):
    in_specs = (
        P(("dp", "head"), None),
        P(("dp", "head"), None),
        P("dp", None),
        P(),
        P("dp", "head"),
        P("dp", "head"),
        P("dp", "head"),
        P("dp", "head"),
        P("dp", "head", None),
        P(None, None, ("head", "dp")),
        P(None, "head"),
        P(),
        P("dp", "head"),
        P(),
        P("dp", "head"),
        P("dp", "head"),
        P("dp", "head"),
    )
    out_specs = (
        P(("dp", "head"), None),
        P(("dp", "head"), None),
        P(),
        P("dp", "head"),
        P("dp", "head"),
        P("dp", "head"),
        P("dp", "head"),
        P("dp", "head", None),
        P(None, None, ("head", "dp")),
        P(None, "head"),
        P(),
        P("dp", "head"),
        P(),
        P("dp", "head"),
        P("dp", "head"),
        P("dp", "head"),
    )
    return jax.shard_map(body, mesh=mesh, in_specs=in_specs, out_specs=out_specs, check_vma=False)
```

profile of v0, /device:TPU:1, one launch (start us, length us, event | category | flops | bytes accessed | tf_op | source)
XLA Modules:
  0.0 2608.5 jit_solution(17421069317214233803)
XLA Ops:
  15.1 29.8 %all_gather.47 = bf16[3,4,128]{1,0,2:T(4,128)(2,1)S(1)} all-gather(bf16[3,4,16]{1,0,2:T(4,128)(2,1)S(1)} %copy.159), channel_id=1, replica_groups=mesh['dp'=8,'head'=16] {'dp'}, dimensions={2}, use_global_device_ids=true | all-gather | bytes 3456 | tf_op jit(solution)/shard_map/all_gather | solution.py:185
  65.3 31.2 %all_gather.49 = bf16[2048,128]{1,0:T(8,128)(2,1)} all-gather(bf16[256,128]{1,0:T(8,128)(2,1)} %param.25), channel_id=1, replica_groups=mesh['dp'=8,'head'=16] {'dp'}, dimensions={0}, use_global_device_ids=true | all-gather | bytes 589824 | tf_op jit(solution)/shard_map/all_gather | solution.py:180
  96.6 30.0 %all_gather.46 = bf16[2048,128]{1,0:T(8,128)(2,1)S(1)} all-gather(bf16[256,128]{1,0:T(8,128)(2,1)} %param.26), channel_id=1, replica_groups=mesh['dp'=8,'head'=16] {'dp'}, dimensions={0}, use_global_device_ids=true | all-gather | bytes 589824 | tf_op jit(solution)/shard_map/all_gather | solution.py:181
  126.6 32.4 %all_gather.48 = bf16[2048,128]{1,0:T(8,128)(2,1)} all-gather(bf16[256,128]{1,0:T(8,128)(2,1)} %param.27), channel_id=1, replica_groups=mesh['dp'=8,'head'=16] {'dp'}, dimensions={0}, use_global_device_ids=true | all-gather | bytes 589824 | tf_op jit(solution)/shard_map/all_gather | solution.py:182
  159.0 31.2 %all_gather.50 = bf16[2048,128]{1,0:T(8,128)(2,1)} all-gather(bf16[256,128]{1,0:T(8,128)(2,1)} %param.28), channel_id=1, replica_groups=mesh['dp'=8,'head'=16] {'dp'}, dimensions={0}, use_global_device_ids=true | all-gather | bytes 589824 | tf_op jit(solution)/shard_map/all_gather | solution.py:183
  190.2 32.5 %all_gather.51 = bf16[2048,128]{1,0:T(8,128)(2,1)} all-gather(bf16[256,128]{1,0:T(8,128)(2,1)} %param.33), channel_id=1, replica_groups=mesh['dp'=8,'head'=16] {'dp'}, dimensions={0}, use_global_device_ids=true | all-gather | bytes 589824 | tf_op jit(solution)/shard_map/all_gather | solution.py:186
  281.5 327.5 %while.42 = (s32[]{:T(128)}, f32[1,128,128]{2,1,0:T(8,128)S(1)}, f32[32,1,64,128]{3,2,1,0:T(8,128)}, f32[32,1,128,128]{3,2,1,0:T(8,128)}, f32[32]{0:T(128)}, /*i...) while((s32[]{:T(128)}, f32[1,128,128]{2,1,0:T(8,128)S(1)}, ...), condition=%wide.region_8.9_spmd.clone, body=%wide.region_7.8_spmd.clone.sunk | while | flops 44204032 | bytes 758453 | solution.py:114
  625.0 143.5 %reduce-scatter.19.cloned.1.call-done = bf16[128,2048]{1,0:T(8,128)(2,1)} async-done(((bf16[2048,2048]{1,0:T(8,128)(2,1)}), bf16[128,2048]{1,0:T(8,128)(2,1)}) %reduce-scatter.19.cloned.1.call-update) | async-done | bytes 524304 | tf_op jit(solution)/shard_map/reduce_scatter | solution.py:213
  774.7 50.5 %all-gather.10.cloned.1.call-done = bf16[2048,2048]{1,0:T(8,128)(2,1)} async-done(((bf16[128,2048]{1,0:T(8,128)(2,1)}), bf16[2048,2048]{1,0:T(8,128)(2,1)}) %all-gather.10.cloned.1.call-update) | async-done | bytes 8388624 | tf_op jit(solution)/shard_map/all_gather | solution.py:218
  833.7 41.9 %all-gather.12.cloned.1.call-done = bf16[2048,352]{0,1:T(8,128)(2,1)} async-done(((bf16[256,352]{0,1:T(8,128)(2,1)}), bf16[2048,352]{0,1:T(8,128)(2,1)}) %all-gather.12.cloned.1.call-update) | async-done | bytes 1441808 | tf_op jit(solution)/shard_map/all_gather | solution.py:187
  884.1 40.0 %all-gather.16.cloned.1.call-done = bf16[2048,352]{0,1:T(8,128)(2,1)} async-done(((bf16[256,352]{0,1:T(8,128)(2,1)}), bf16[2048,352]{0,1:T(8,128)(2,1)}) %all-gather.16.cloned.1.call-update) | async-done | bytes 1441808 | tf_op jit(solution)/shard_map/all_gather | solution.py:189
  924.1 52.8 %all-gather.18.cloned.1.call-done = bf16[2048,2048]{1,0:T(8,128)(2,1)} async-done(((bf16[128,2048]{1,0:T(8,128)(2,1)}), bf16[2048,2048]{1,0:T(8,128)(2,1)}) %all-gather.18.cloned.1.call-update) | async-done | bytes 8388624 | tf_op jit(solution)/shard_map/all_gather | solution.py:227
  1006.4 96.8 %reduce-scatter.23.cloned.1.call-done = bf16[128,2048]{1,0:T(8,128)(2,1)} async-done(((bf16[2048,2048]{1,0:T(8,128)(2,1)}), bf16[128,2048]{1,0:T(8,128)(2,1)}) %reduce-scatter.23.cloned.1.call-update) | async-done | bytes 524304 | tf_op jit(solution)/shard_map/reduce_scatter | solution.py:240
  1135.8 25.7 all-gather.20.cloned.1.call-done
  1177.6 627.6 %while.43 = (s32[]{:T(128)}, f32[1,128,128]{1,2,0:T(8,128)}, f32[32,1,64,128]{3,2,1,0:T(8,128)}, f32[32,1,64,128]{3,2,1,0:T(8,128)}, f32[32,1,64,64]{3,2,1,0:T(8...) while((s32[]{:T(128)}, f32[1,128,128]{1,2,0:T(8,128)}, ...), condition=%wide.region_18.19_spmd.clone, body=%wide.region_16.18_spmd.clone.sunk | while | flops 100876288 | bytes 2213171 | solution.py:114
  1980.4 25.5 add_convert_fusion
  2033.6 71.9 %reduce-scatter.35.cloned.1.call-done = bf16[256,128]{1,0:T(8,128)(2,1)} async-done(((bf16[2048,128]{1,0:T(8,128)(2,1)}), bf16[256,128]{1,0:T(8,128)(2,1)}) %reduce-scatter.35.cloned.1.call-update) | async-done | bytes 65552 | tf_op jit(solution)/shard_map/reduce_scatter | solution.py:306
  2107.0 71.4 %reduce-scatter.33.cloned.1.call-done = bf16[256,128]{1,0:T(8,128)(2,1)} async-done(((bf16[2048,128]{1,0:T(8,128)(2,1)}), bf16[256,128]{1,0:T(8,128)(2,1)}) %reduce-scatter.33.cloned.1.call-update) | async-done | bytes 65552 | tf_op jit(solution)/shard_map/reduce_scatter | solution.py:297
  2179.8 72.0 %reduce-scatter.29.cloned.1.call-done = bf16[256,128]{1,0:T(8,128)(2,1)} async-done(((bf16[2048,128]{1,0:T(8,128)(2,1)}), bf16[256,128]{1,0:T(8,128)(2,1)}) %reduce-scatter.29.cloned.1.call-update) | async-done | bytes 65552 | tf_op jit(solution)/shard_map/reduce_scatter | solution.py:291
  2253.3 71.5 %reduce-scatter.31.cloned.1.call-done = bf16[256,128]{1,0:T(8,128)(2,1)} async-done(((bf16[2048,128]{1,0:T(8,128)(2,1)}), bf16[256,128]{1,0:T(8,128)(2,1)}) %reduce-scatter.31.cloned.1.call-update) | async-done | bytes 65552 | tf_op jit(solution)/shard_map/reduce_scatter | solution.py:294
  2326.4 72.0 %reduce-scatter.27.cloned.1.call-done = bf16[256,128]{1,0:T(8,128)(2,1)} async-done(((bf16[2048,128]{1,0:T(8,128)(2,1)}), bf16[256,128]{1,0:T(8,128)(2,1)}) %reduce-scatter.27.cloned.1.call-update) | async-done | bytes 65552 | tf_op jit(solution)/shard_map/reduce_scatter | solution.py:288
  2399.8 97.9 %reduce-scatter.25.cloned.1.call-done = bf16[128,2048]{1,0:T(8,128)(2,1)} async-done(((bf16[2048,2048]{1,0:T(8,128)(2,1)}), bf16[128,2048]{1,0:T(8,128)(2,1)}) %reduce-scatter.25.cloned.1.call-update) | async-done | bytes 524304 | tf_op jit(solution)/shard_map/reduce_scatter | solution.py:270
  2499.3 67.0 %all-reduce.41 = (f32[2048]{0:T(1024)}, f32[2,16]{0,1:T(8,128)S(1)}, f32[128]{0:T(128)}, f32[2048]{0:T(1024)}) all-reduce(f32[2048]{0:T(1024)S(1)} %get-tuple-element.684, f32[2,16]{0,1:T(8,128)S(1)} %dynamic_update_slice.67, f32[128]{0:T(128)S(1)} %copy-done.142, ...), channel_id=1, replica_groups=mesh['dp'=8,'head'=16] {'dp','head'}, use_global_device_ids=true, to_apply=%region_33.34 | all-reduce | flops 4256 | bytes 34048 | tf_op jit(solution)/shard_map/psum | solution.py:324
  2566.9 30.9 %reduce-scatter.21.cloned.1.call-done = bf16[128,2048]{1,0:T(8,128)(2,1)} async-done(((bf16[2048,2048]{1,0:T(8,128)(2,1)}), bf16[128,2048]{1,0:T(8,128)(2,1)}) %reduce-scatter.21.cloned.1.call-update) | async-done | bytes 524304 | tf_op jit(solution)/shard_map/reduce_scatter | solution.py:222
  (1386 shorter events, 1368.2 us)
Async XLA Ops:
  8.0 220.4 %all-gather.8.cloned.1.call-start = ((), (), s32[]{:S(2)}) async-start(), calls=%async_computation.14 | async-start | bytes 8912896 | tf_op jit(solution)/shard_map/all_gather | solution.py:194
  11.4 757.1 %reduce-scatter.19.cloned.1.call-start = ((), (), s32[]{:S(2)}) async-start(), calls=%async_computation.15 | async-start | bytes 8912896 | tf_op jit(solution)/shard_map/reduce_scatter | solution.py:213
  65.3 1060.8 %copy-start.81 = (f32[2048]{0:T(1024)}, f32[2048]{0:T(1024)S(1)}, u32[]{:S(2)}) copy-start(f32[2048]{0:T(1024)S(1)} %get-tuple-element.821) | copy-start | bytes 24580
  65.3 1061.4 %copy-start.83 = (f32[2048]{0:T(1024)}, f32[2048]{0:T(1024)S(1)}, u32[]{:S(2)}) copy-start(f32[2048]{0:T(1024)S(1)} %get-tuple-element.822) | copy-start | bytes 24580
  624.3 150.4 %all-gather.14.cloned.1.call-start = ((), (), s32[]{:S(2)}) async-start(), calls=%async_computation.18 | async-start | bytes 1622016 | tf_op jit(solution)/shard_map/all_gather | solution.py:188
  624.9 200.3 %all-gather.10.cloned.1.call-start = ((), (), s32[]{:S(2)}) async-start(), calls=%async_computation.16 | async-start | bytes 8912896 | tf_op jit(solution)/shard_map/all_gather | solution.py:218
  772.1 103.5 %all-gather.12.cloned.1.call-start = ((), (), s32[]{:S(2)}) async-start(), calls=%async_computation.17 | async-start | bytes 1622016 | tf_op jit(solution)/shard_map/all_gather | solution.py:187
  772.7 151.3 %all-gather.16.cloned.1.call-start = ((), (), s32[]{:S(2)}) async-start(), calls=%async_computation.19 | async-start | bytes 1622016 | tf_op jit(solution)/shard_map/all_gather | solution.py:189
  773.5 203.4 %all-gather.18.cloned.1.call-start = ((), (), s32[]{:S(2)}) async-start(), calls=%async_computation.21 | async-start | bytes 8912896 | tf_op jit(solution)/shard_map/all_gather | solution.py:227
  774.2 329.0 %reduce-scatter.23.cloned.1.call-start = ((), (), s32[]{:S(2)}) async-start(), calls=%async_computation.22 | async-start | bytes 8912896 | tf_op jit(solution)/shard_map/reduce_scatter | solution.py:240
  1006.4 155.1 %all-gather.20.cloned.1.call-start = ((), (), s32[]{:S(2)}) async-start(), calls=%async_computation.23 | async-start | bytes 8912896 | tf_op jit(solution)/shard_map/all_gather | solution.py:249
  1108.4 907.3 %reduce-scatter.41.cloned.1.call-start = ((), (), s32[]{:S(2)}) async-start(), calls=%async_computation.32 | async-start | bytes 1622016 | tf_op jit(solution)/shard_map/reduce_scatter | solution.py:315
  1116.7 900.8 %reduce-scatter.39.cloned.1.call-start = ((), (), s32[]{:S(2)}) async-start(), calls=%async_computation.31 | async-start | bytes 1622016 | tf_op jit(solution)/shard_map/reduce_scatter | solution.py:312
  1125.2 894.0 %reduce-scatter.37.cloned.1.call-start = ((), (), s32[]{:S(2)}) async-start(), calls=%async_computation.30 | async-start | bytes 1622016 | tf_op jit(solution)/shard_map/reduce_scatter | solution.py:309
  1135.8 887.1 %reduce-scatter.45.cloned.1.call-start = ((), (), s32[]{:S(2)}) async-start(), calls=%async_computation.34 | async-start | bytes 36864
  1898.2 133.8 %reduce-scatter.43.cloned.1.call-start = ((), (), s32[]{:S(2)}) async-start(), calls=%async_computation.33 | async-start | bytes 589824
  1903.9 201.5 %reduce-scatter.35.cloned.1.call-start = ((), (), s32[]{:S(2)}) async-start(), calls=%async_computation.29 | async-start | bytes 589824 | tf_op jit(solution)/shard_map/reduce_scatter | solution.py:306
  1910.6 267.7 %reduce-scatter.33.cloned.1.call-start = ((), (), s32[]{:S(2)}) async-start(), calls=%async_computation.28 | async-start | bytes 589824 | tf_op jit(solution)/shard_map/reduce_scatter | solution.py:297
  1925.5 326.3 %reduce-scatter.29.cloned.1.call-start = ((), (), s32[]{:S(2)}) async-start(), calls=%async_computation.26 | async-start | bytes 589824 | tf_op jit(solution)/shard_map/reduce_scatter | solution.py:291
  1947.0 377.8 %reduce-scatter.31.cloned.1.call-start = ((), (), s32[]{:S(2)}) async-start(), calls=%async_computation.27 | async-start | bytes 589824 | tf_op jit(solution)/shard_map/reduce_scatter | solution.py:294
  1965.3 433.0 %reduce-scatter.27.cloned.1.call-start = ((), (), s32[]{:S(2)}) async-start(), calls=%async_computation.25 | async-start | bytes 589824 | tf_op jit(solution)/shard_map/reduce_scatter | solution.py:288
  1980.4 517.3 %reduce-scatter.25.cloned.1.call-start = ((), (), s32[]{:S(2)}) async-start(), calls=%async_computation.24 | async-start | bytes 8912896 | tf_op jit(solution)/shard_map/reduce_scatter | solution.py:270
  2006.0 591.8 %reduce-scatter.21.cloned.1.call-start = ((), (), s32[]{:S(2)}) async-start(), calls=%async_computation.20 | async-start | bytes 8912896 | tf_op jit(solution)/shard_map/reduce_scatter | solution.py:222
  2015.6 582.2 %copy-start.27 = (bf16[128,2048]{1,0:T(8,128)(2,1)S(1)}, bf16[128,2048]{1,0:T(8,128)(2,1)}, u32[]{:S(2)}) copy-start(bf16[128,2048]{1,0:T(8,128)(2,1)} %reduce-scatter.19.cloned.1.call-done) | copy-start | bytes 1572868
  (144 other events, 8579.5 us)
Sparse Core Ops, SparseCore 0:
  11.5 57.6 all-gather.7
  624.5 143.9 reduce-scatter.18
  1006.5 96.6 reduce-scatter.22
Sparse Core Ops, SparseCore 1:
  627.0 93.4 all-gather.13
  772.2 53.0 all-gather.9
  827.3 48.3 all-gather.11
  877.8 46.2 all-gather.15
  925.8 51.0 all-gather.17
  1108.5 53.0 all-gather.19
  1165.1 72.3 reduce-scatter.40
  1240.9 72.7 reduce-scatter.38
  1317.2 72.7 reduce-scatter.36
  1898.3 60.3 reduce-scatter.44
  1962.1 69.9 reduce-scatter.42
  2036.0 69.4 reduce-scatter.34
  2108.9 69.4 reduce-scatter.32
  2182.3 69.4 reduce-scatter.28
  2255.4 69.4 reduce-scatter.30
  2328.8 69.4 reduce-scatter.26
  2400.7 96.9 reduce-scatter.24
  2500.1 97.6 reduce-scatter.20
where the time goes:
time: 2640 us; the launch traced here: 2610 us
  waiting for transfers between devices  949 us (36%)
  matrix products  817 us (31%)
  local copies, waits for them, and re-layouts  384 us (15%)
  blocking collectives  274 us (10%)
  other arithmetic  161 us (6%)
    dot_general x458, matrix products, product(): jnp.einsum(form, left, right, precision=lax.Precision.HIGHEST, preferred_...  602 us
    dynamic_slice x192, local copies, waits for them, and re-layouts, delta_head(): lax.scan(jax.checkpoint(span_step), state_start, (fresh_base, key_weighte...  192 us
    reduce_scatter x1, waiting for transfers between devices, body(): lax.psum_scatter(against(mixed_low, w_out).astype(jnp.bfloat16), 'head',...  143 us
    squeeze x128, local copies, waits for them, and re-layouts, delta_head(): lax.scan(jax.checkpoint(span_step), state_start, (fresh_base, key_weighte...  98.8 us
    reduce_scatter x1, waiting for transfers between devices, body(): lax.psum_scatter(summed.astype(jnp.bfloat16), 'head', scatter_dimension=0...  97.9 us
    reduce_scatter x1, waiting for transfers between devices, body(): lax.psum_scatter((against(gate_grad_low, w_gate) + against(up_grad_low, w...  96.8 us
    dot_general x9, matrix products, against(): lax.dot_general(left, right, (((1,), (1,)), ((), ())), preferred_element_...  92.4 us
    reduce_scatter x1, waiting for transfers between devices, body(): lax.psum_scatter(key_wgrad.astype(jnp.bfloat16), 'dp', scatter_dimension=...  72 us
  transfers between devices with their start and end apart: 21, of which 15 were waited for; matrix products, arithmetic and copies ran while one was open for 35% of the time, Pallas kernels for 0%

commit v1 on v0

v1 whole, which is shorter than its diff:
```python
from functools import partial

import jax
import jax.numpy as jnp
from jax import lax
from jax.experimental import pallas as pl
from jax.experimental.pallas import tpu as pltpu

CHUNK = 128
BATCH = 4
ROWS_A = 80
ROWS_B = 48
GATE_ALONE = 9
VMEM_MAX = 56 * 1024 * 1024


def split(value):
    high = value.astype(jnp.bfloat16)
    return high, (value - high.astype(jnp.float32)).astype(jnp.bfloat16)


def left_pair(value):
    return jnp.concatenate(split(value), axis=1)


def right_pair(value):
    high, low = split(value)
    wide = jnp.concatenate([high, low], axis=1)
    return jnp.concatenate([wide, wide], axis=0)


def right_pair_t(value):
    high, low = split(value)
    return jnp.concatenate(
        [jnp.concatenate([high, high], axis=1), jnp.concatenate([low, low], axis=1)], axis=0
    )


def fold(wide):
    half = wide.shape[1] // 2
    return wide[:, :half] + wide[:, half:]


def mul_pairs(left, right):
    return fold(jnp.dot(left, right, preferred_element_type=jnp.float32))


def mul(left, right):
    return mul_pairs(left_pair(left), right_pair(right))


def mul_t(left, right):
    return fold(
        lax.dot_general(
            left_pair(left),
            right_pair_t(right),
            (((1,), (1,)), ((), ())),
            preferred_element_type=jnp.float32,
        )
    )


def iotas(rows=CHUNK, cols=CHUNK):
    return (
        lax.broadcasted_iota(jnp.int32, (rows, cols), 0),
        lax.broadcasted_iota(jnp.int32, (rows, cols), 1),
    )


def silu_parts(value):
    gate = jax.nn.sigmoid(value)
    return gate, value * gate


def tap_masks(start_first, start_second, row_index):
    keeps = []
    for offset in range(1, 4):
        first = jnp.where(row_index < offset, 1.0 - start_first, 1.0)
        second = jnp.where(
            (row_index >= CHUNK // 2) & (row_index < CHUNK // 2 + offset), 1.0 - start_second, 1.0
        )
        keeps.append(first * second)
    return keeps


def shifted_rows(current, before, keeps):
    joined = jnp.concatenate([before, current], axis=0)
    return [current] + [
        pltpu.roll(joined, offset, 0)[8:] * keeps[offset - 1] for offset in range(1, 4)
    ]


def conv_rows(rows_by_offset, taps):
    total = rows_by_offset[0] * taps[3:4]
    for offset in range(1, 4):
        total = total + rows_by_offset[offset] * taps[3 - offset : 4 - offset]
    return total


def chunk_cols(rows):
    return jnp.transpose(jnp.concatenate([rows, jnp.zeros((CHUNK - 8, CHUNK), jnp.float32)], axis=0))


def decay_matrix(rows, cols, start_second):
    row_index, col_index = iotas()
    gap = cols[:, 0:1] - rows[0:1, :]
    lower = row_index >= col_index
    cross = (row_index >= CHUNK // 2) & (col_index < CHUNK // 2)
    decay = jnp.where(lower, jnp.exp(jnp.where(lower, gap, 0.0)), 0.0)
    return decay * jnp.where(cross, 1.0 - start_second, 1.0)


def head_rows(raw_refs, place_ref, chunk, part):
    def load(start, count):
        rows = pl.ds(pl.multiple_of(start, 8), count)
        return jnp.where(half == 0, raw_refs[0][rows, lanes], raw_refs[1][rows, lanes])

    lanes = slice(None) if part == GATE_ALONE else slice(part * CHUNK, (part + 1) * CHUNK)
    half = place_ref[2, chunk]
    current = jnp.concatenate(
        [load(place_ref[0, chunk], ROWS_A), load(place_ref[1, chunk], ROWS_B)], axis=0
    )
    if part > 2:
        return current
    earlier = jnp.maximum(chunk - 1, 0)
    half = place_ref[2, earlier]
    return current, load(place_ref[1, earlier] + ROWS_B - 8, 8)


def put_rows(out_ref, place_ref, chunk, lanes, value):
    half = place_ref[2, chunk]
    first = pl.ds(pl.multiple_of(place_ref[0, chunk], 16), ROWS_A)
    second = pl.ds(pl.multiple_of(place_ref[1, chunk], 16), ROWS_B)
    out_ref[half, first, lanes] = value[:ROWS_A]
    out_ref[half, second, lanes] = value[ROWS_A:]


def spread_sum(rows, matrix):
    high, rest = split(rows)
    mid = rest
    low = (rows - high.astype(jnp.float32) - mid.astype(jnp.float32)).astype(jnp.bfloat16)
    parts = jnp.concatenate([high, mid, low, jnp.zeros_like(low)], axis=0)
    wide = jnp.dot(parts, matrix.astype(jnp.bfloat16), preferred_element_type=jnp.float32)
    return wide[:8] + wide[8:16] + wide[16:24]


def gate_rows(decay_cols, starts, params_ref):
    row_index, col_index = iotas()
    pair = jnp.transpose(decay_cols)[:8]
    position = col_index[:8]
    kind = row_index[:8]
    carry, same = 1.0 - starts[0], 1.0 - starts[1]
    second = position >= CHUNK // 2
    beta = jax.nn.sigmoid(pair[1:2])
    inside = pair[0:1] + params_ref[1, 0]
    soft = jax.nn.softplus(inside)
    decay_log = -jnp.exp(params_ref[0, 0] + jnp.zeros((8, CHUNK), jnp.float32)) * soft
    total = spread_sum(decay_log, (row_index <= col_index).astype(jnp.float32))
    end = total[:, CHUNK - 1 :]
    gam = jnp.exp(total) * carry * jnp.where(second, same, 1.0)
    tail = jnp.exp(end - total) * jnp.where(second, 1.0, same)
    span = jnp.exp(end) * carry * same
    rows = jnp.where(kind == 0, total, jnp.where(kind == 1, beta, jnp.where(kind == 2, gam, tail)))
    return jnp.where(kind == 4, span, rows)


def convolved(raw_refs, place_ref, starts, taps_ref, chunk, row_index):
    keeps = tap_masks(starts[0], starts[1], row_index)
    pieces = []
    for part in range(3):
        current, before = head_rows(raw_refs, place_ref, chunk, part)
        rows_by_offset = shifted_rows(current, before, keeps)
        pieces.append((rows_by_offset, conv_rows(rows_by_offset, taps_ref[part])))
    return keeps, pieces


def start_flags(starts_ref, chunk):
    return (
        starts_ref[2 * chunk].astype(jnp.float32),
        starts_ref[2 * chunk + 1].astype(jnp.float32),
    )


def normed_qkv(pieces):
    acts = [piece[1] * jax.nn.sigmoid(piece[1]) for piece in pieces]
    q_scale = lax.rsqrt(jnp.sum(acts[0] * acts[0], axis=-1, keepdims=True) + 1e-06)
    k_scale = lax.rsqrt(jnp.sum(acts[1] * acts[1], axis=-1, keepdims=True) + 1e-06)
    return acts[0] * q_scale * CHUNK ** (-0.5), acts[1] * k_scale, acts[2], q_scale, k_scale


def inverse_lower(stricts):
    row_index, col_index = iotas()
    eye = (row_index == col_index).astype(jnp.float32)
    near = row_index // 16 == col_index // 16
    powers = [jnp.where(near, strict, 0.0) for strict in stricts]
    inverses = [eye - power for power in powers]
    powers = [mul(power, power) for power in powers]
    for step in range(3):
        rights = [right_pair(power) for power in powers]
        if step < 2:
            stacks = [
                left_pair(jnp.concatenate([inverse, power], axis=0))
                for inverse, power in zip(inverses, powers)
            ]
            both = [mul_pairs(stack, right) for stack, right in zip(stacks, rights)]
            inverses = [inverse + pair[:CHUNK] for inverse, pair in zip(inverses, both)]
            powers = [pair[CHUNK:] for pair in both]
        else:
            inverses = [
                inverse + mul_pairs(left_pair(inverse), right)
                for inverse, right in zip(inverses, rights)
            ]
    for width in (16, 32, 64):
        beside = (row_index // (2 * width) == col_index // (2 * width)) & (
            row_index // width != col_index // width
        )
        crossed = [
            mul(inverse, jnp.where(beside, strict, 0.0))
            for inverse, strict in zip(inverses, stricts)
        ]
        inverses = [inverse - mul(cross, inverse) for cross, inverse in zip(crossed, inverses)]
    return inverses


def prepare_kernel(place_ref, starts_ref, params_ref, raw0_ref, raw1_ref, taps_ref,
                   rows_out_ref, inv_ref, kkf_ref, p_ref, uw_ref, m_ref, mt_ref, b_ref, r_ref, pu_ref):
    row_index, col_index = iotas()
    diagonal = (row_index == col_index).astype(jnp.float32)
    stricts, kept = [], []
    for member in range(BATCH):
        chunk = pl.program_id(0) * BATCH + member
        starts = start_flags(starts_ref, chunk)
        raw_refs = (raw0_ref, raw1_ref)
        _, pieces = convolved(raw_refs, place_ref, starts, taps_ref, chunk, row_index)
        queries, keys_in, values_in, _, _ = normed_qkv(pieces)
        rows = gate_rows(head_rows(raw_refs, place_ref, chunk, 4), starts, params_ref)
        rows_out_ref[member] = rows
        cols = chunk_cols(rows)
        decay = decay_matrix(rows, cols, starts[1])
        beta, gam, tail = cols[:, 1:2], cols[:, 2:3], cols[:, 3:4]
        scores = mul_t(jnp.concatenate([keys_in, queries], axis=0), keys_in)
        kkf = jnp.where(row_index > col_index, scores[:CHUNK] * decay, 0.0)
        inner = scores[CHUNK:] * decay
        stricts.append(kkf * beta)
        kkf_ref[member] = kkf
        p_ref[member] = inner
        pair = jnp.concatenate([values_in * beta, keys_in * (beta * gam)], axis=1)
        stack = jnp.concatenate([jnp.transpose(keys_in * tail), inner], axis=0)
        kept.append((pair, stack, diagonal * rows[4:5], queries * gam))
    inverses = inverse_lower(stricts)
    joined = [mul(inverse, pair) for inverse, (pair, _, _, _) in zip(inverses, kept)]
    both = [mul(stack, join) for join, (_, stack, _, _) in zip(joined, kept)]
    for member in range(BATCH):
        _, _, span, faded = kept[member]
        inv_ref[member] = inverses[member]
        uw_ref[member] = joined[member]
        state_map = span - both[member][:CHUNK, CHUNK:]
        m_ref[member] = left_pair(state_map)
        mt_ref[member] = left_pair(jnp.transpose(state_map))
        b_ref[member] = both[member][:CHUNK, :CHUNK]
        r_ref[member] = faded - both[member][CHUNK:, CHUNK:]
        pu_ref[member] = both[member][CHUNK:, :CHUNK]


def whole(shape):
    return pl.BlockSpec(shape, lambda *_: (0,) * len(shape))


def per_batch(shape, turned=False, steps=4):
    def place(step, *_):
        return ((steps - 1 - step) if turned else step,) + (0,) * (len(shape) - 1)

    return pl.BlockSpec(shape, place)


def shaped(shape, dtype=jnp.float32):
    return jax.ShapeDtypeStruct(shape, dtype)


def prepare(place, starts, params, raw0, raw1, taps):
    chunks = place.shape[1]
    square = (BATCH, CHUNK, CHUNK)
    wide = (BATCH, CHUNK, 2 * CHUNK)
    kinds = [((BATCH, 8, CHUNK), jnp.float32), (square, jnp.float32), (square, jnp.float32), (square, jnp.float32),
             (wide, jnp.float32), (wide, jnp.bfloat16), (wide, jnp.bfloat16), (square, jnp.float32),
             (square, jnp.float32), (square, jnp.float32)]
    return pl.pallas_call(
        prepare_kernel,
        grid_spec=pltpu.PrefetchScalarGridSpec(
            num_scalar_prefetch=3,
            grid=(chunks // BATCH,),
            in_specs=[whole(raw0.shape), whole(raw1.shape), whole(taps.shape)],
            out_specs=[per_batch(shape) for shape, _ in kinds],
        ),
        out_shape=[shaped((chunks,) + shape[1:], dtype) for shape, dtype in kinds],
        compiler_params=pltpu.CompilerParams(vmem_limit_bytes=VMEM_MAX),
        name="prepare",
    )(place, starts, params, raw0, raw1, taps)


def gate_rows_of(gate_refs, place_ref, chunk):
    return head_rows(gate_refs, place_ref, chunk, GATE_ALONE)


def scan_kernel(place_ref, m_ref, b_ref, r_ref, pu_ref, gate0_ref, gate1_ref, gain_ref,
                state_out_ref, core_ref, mixed_ref, stored_ref, state_ref):
    @pl.when(pl.program_id(0) == 0)
    def _():
        state_ref[...] = jnp.zeros_like(state_ref)

    state = state_ref[...]
    for member in range(BATCH):
        chunk = pl.program_id(0) * BATCH + member
        state_out_ref[member] = state
        pair = right_pair(state)
        core = mul_pairs(left_pair(r_ref[member]), pair) + pu_ref[member]
        state = mul_pairs(m_ref[member], pair) + b_ref[member]
        _, gate = silu_parts(gate_rows_of((gate0_ref, gate1_ref), place_ref, chunk))
        core_ref[member] = core
        scale = lax.rsqrt(jnp.mean(core * core, axis=-1, keepdims=True) + 1e-05)
        mixed = (core * scale * gain_ref[...] * gate).astype(jnp.bfloat16)
        mixed_ref[member] = mixed
        put_rows(stored_ref, place_ref, chunk, slice(None), mixed)
    state_ref[...] = state


def gate_columns(raw):
    return pl.BlockSpec((raw.shape[0], CHUNK), lambda *_: (0, 3))


def scan_states(place, m, b, r, pu, raw0, raw1, gain):
    chunks = m.shape[0]
    square = (BATCH, CHUNK, CHUNK)
    wide = (BATCH, CHUNK, 2 * CHUNK)
    stored = (2, raw0.shape[0], CHUNK)
    return pl.pallas_call(
        scan_kernel,
        grid_spec=pltpu.PrefetchScalarGridSpec(
            num_scalar_prefetch=1,
            grid=(chunks // BATCH,),
            in_specs=[per_batch(wide), per_batch(square), per_batch(square), per_batch(square),
                      gate_columns(raw0), gate_columns(raw1), whole((1, CHUNK))],
            out_specs=[per_batch(square)] * 3 + [whole(stored)],
            scratch_shapes=[pltpu.VMEM((CHUNK, CHUNK), jnp.float32)],
        ),
        out_shape=[shaped((chunks, CHUNK, CHUNK)), shaped((chunks, CHUNK, CHUNK)),
                   shaped((chunks, CHUNK, CHUNK), jnp.bfloat16), shaped(stored, jnp.bfloat16)],
        compiler_params=pltpu.CompilerParams(vmem_limit_bytes=VMEM_MAX),
        name="scan_states",
    )(place, m, b, r, pu, raw0, raw1, gain)


def back_scan_kernel(place_ref, mt_ref, r_ref, core_ref, gate0_ref, gate1_ref, dmixed_ref, gain_ref,
                     dcore_ref, dstate_out_ref, dgate_ref, dgain_ref, dstate_ref):
    step = pl.program_id(0)

    @pl.when(step == 0)
    def _():
        dstate_ref[...] = jnp.zeros_like(dstate_ref)
        dgain_ref[...] = jnp.zeros_like(dgain_ref)

    gain = gain_ref[...]
    dgain = jnp.zeros((8, CHUNK), jnp.float32)
    terms = []
    for member in reversed(range(BATCH)):
        chunk = (pl.num_programs(0) - 1 - step) * BATCH + member
        core = core_ref[member]
        raw_gate = gate_rows_of((gate0_ref, gate1_ref), place_ref, chunk)
        dmixed = dmixed_ref[member].astype(jnp.float32)
        gate, gated = silu_parts(raw_gate)
        scale = lax.rsqrt(jnp.mean(core * core, axis=-1, keepdims=True) + 1e-05)
        unit = core * scale
        dscaled = dmixed * gated
        dgate = dmixed * unit * gain * (gate * (1.0 + raw_gate * (1.0 - gate)))
        dgate_ref[member] = dgate.astype(jnp.bfloat16)
        product = dscaled * unit
        dgain = dgain + jnp.sum(product.reshape(CHUNK // 8, 8, CHUNK), axis=0)
        dunit = dscaled * gain
        dcore = scale * (dunit - unit * jnp.mean(dunit * unit, axis=-1, keepdims=True))
        dcore_ref[member] = dcore
        terms.append((member, mul(jnp.transpose(r_ref[member]), dcore)))
    dgain_ref[...] += dgain
    dstate = dstate_ref[...]
    for member, term in terms:
        dstate_out_ref[member] = dstate
        dstate = mul_pairs(mt_ref[member], right_pair(dstate)) + term
    dstate_ref[...] = dstate


def back_scan(place, mt, r, core, raw0, raw1, dmixed, gain):
    chunks = mt.shape[0]
    square = (BATCH, CHUNK, CHUNK)
    wide = (BATCH, CHUNK, 2 * CHUNK)
    turned = partial(per_batch, turned=True, steps=chunks // BATCH)
    return pl.pallas_call(
        back_scan_kernel,
        grid_spec=pltpu.PrefetchScalarGridSpec(
            num_scalar_prefetch=1,
            grid=(chunks // BATCH,),
            in_specs=[turned(wide), turned(square), turned(square),
                      gate_columns(raw0), gate_columns(raw1), turned(square), whole((1, CHUNK))],
            out_specs=[turned(square), turned(square), turned(square), whole((8, CHUNK))],
            scratch_shapes=[pltpu.VMEM((CHUNK, CHUNK), jnp.float32)],
        ),
        out_shape=[shaped((chunks, CHUNK, CHUNK)), shaped((chunks, CHUNK, CHUNK)),
                   shaped((chunks, CHUNK, CHUNK), jnp.bfloat16), shaped((8, CHUNK))],
        compiler_params=pltpu.CompilerParams(vmem_limit_bytes=VMEM_MAX),
        name="back_scan",
    )(place, mt, r, core, raw0, raw1, dmixed, gain)


def lane_sum(value):
    return jnp.sum(value, axis=1, keepdims=True)


def back_kernel(place_ref, starts_ref, params_ref, raw0_ref, raw1_ref, rows_ref, taps_ref, inv_ref, kkf_ref,
                p_ref, uw_ref, state_ref, dstate_ref, dcore_ref, dgate_ref,
                draw_ref, dtaps_ref, dparams_ref, next_ref):
    step = pl.program_id(0)
    row_index, col_index = iotas()
    lower = row_index >= col_index
    strict = row_index > col_index

    @pl.when(step == 0)
    def _():
        next_ref[...] = jnp.zeros_like(next_ref)
        dtaps_ref[...] = jnp.zeros_like(dtaps_ref)
        dparams_ref[...] = jnp.zeros_like(dparams_ref)

    raw_refs = (raw0_ref, raw1_ref)
    members = range(BATCH)
    setups = []
    for member in members:
        chunk = (pl.num_programs(0) - 1 - step) * BATCH + member
        starts = start_flags(starts_ref, chunk)
        keeps, pieces = convolved(raw_refs, place_ref, starts, taps_ref, chunk, row_index)
        queries, keys_in, values_in, q_scale, k_scale = normed_qkv(pieces)
        rows = rows_ref[member]
        cols = chunk_cols(rows)
        decay = decay_matrix(rows, cols, starts[1])
        setups.append((starts, keeps, pieces, queries, keys_in, values_in, q_scale, k_scale, rows, cols, decay))
    fresh = [
        uw_ref[i][:, :CHUNK] - mul(uw_ref[i][:, CHUNK:], state_ref[i]) for i in members
    ]
    dfresh = [
        mul(jnp.transpose(p_ref[i]), dcore_ref[i])
        + mul(setups[i][4] * setups[i][9][:, 3:4], dstate_ref[i])
        for i in members
    ]
    through = [
        mul_t(jnp.concatenate([dcore_ref[i], dfresh[i]], axis=0), state_ref[i]) for i in members
    ]
    dinner = [jnp.where(lower, mul_t(dcore_ref[i], fresh[i]), 0.0) for i in members]
    dkeys_tail = [mul_t(fresh[i], dstate_ref[i]) for i in members]
    dboth = [
        mul(
            jnp.transpose(inv_ref[i]),
            jnp.concatenate([dfresh[i], -through[i][CHUNK:]], axis=1),
        )
        for i in members
    ]
    dstrict = [jnp.where(strict, -mul_t(dboth[i], uw_ref[i]), 0.0) for i in members]
    stacked, crossed = [], []
    for i in members:
        queries, keys_in, cols, decay = setups[i][3], setups[i][4], setups[i][9], setups[i][10]
        dscores_n = dstrict[i] * decay * cols[:, 1:2]
        dscores = dinner[i] * decay
        stacked.append(
            mul(jnp.concatenate([dscores, dscores_n + jnp.transpose(dscores_n)], axis=0), keys_in)
        )
        crossed.append(mul(jnp.transpose(dscores), queries))
    for i in reversed(members):
        starts, keeps, pieces, queries, keys_in, values_in, q_scale, k_scale, rows, cols, _ = setups[i]
        beta, gam, tail = cols[:, 1:2], cols[:, 2:3], cols[:, 3:4]
        dqueries_faded = through[i][:CHUNK]
        dvalues_beta, dkeys_beta = dboth[i][:, :CHUNK], dboth[i][:, CHUNK:]
        keys_gam = keys_in * gam
        dqueries = stacked[i][:CHUNK] + dqueries_faded * gam
        dkeys = (
            stacked[i][CHUNK:]
            + crossed[i]
            + dkeys_beta * (beta * gam)
            + dkeys_tail[i] * tail
        )
        dvalues = dvalues_beta * beta

        dkkf = dstrict[i] * kkf_ref[i]
        flow = dkkf * beta + dinner[i] * p_ref[i]
        tail_term = lane_sum(dkeys_tail[i] * keys_in * tail)
        dbeta = lane_sum(dkkf + dvalues_beta * values_in + dkeys_beta * keys_gam)
        dsum = (
            lane_sum(flow + (dqueries_faded * queries + dkeys_beta * keys_in * beta) * gam)
            - tail_term
        )
        last = jnp.sum(tail_term) + jnp.sum(state_ref[i] * dstate_ref[i] * rows[4:5, 0:1])
        last_col = jnp.where(row_index[:, :1] == CHUNK - 1, last, 0.0)
        packed = jnp.where(
            col_index == 0, dsum + last_col, jnp.where(col_index == 1, dbeta, 0.0)
        )
        turned = jnp.transpose(packed)[:8]
        flow_rows = jnp.sum(flow, axis=0, keepdims=True)
        kind = row_index[:8]
        dtotal = jnp.where(kind == 0, turned - flow_rows, 0.0)
        dlog = spread_sum(dtotal, lower.astype(jnp.float32))[0:1]
        chunk = (pl.num_programs(0) - 1 - step) * BATCH + i
        pair = jnp.transpose(head_rows(raw_refs, place_ref, chunk, 4))[:8]
        inside = pair[0:1] + params_ref[1, 0]
        rate = -jnp.exp(params_ref[0, 0] + jnp.zeros((1, CHUNK), jnp.float32))
        dinside = dlog * rate * jax.nn.sigmoid(inside)
        beta_row = rows[1:2]
        dbeta_raw = turned[1:2] * beta_row * (1.0 - beta_row)
        drate = dlog * rate * jax.nn.softplus(inside)
        dparams_ref[...] += jnp.where(kind == 0, drate, jnp.where(kind == 1, dinside, 0.0))
        ddecay = jnp.where(kind == 0, dinside, jnp.where(kind == 1, dbeta_raw, 0.0))
        put_rows(draw_ref, place_ref, chunk, slice(3 * CHUNK, 4 * CHUNK), dgate_ref[i])
        put_rows(
            draw_ref, place_ref, chunk, slice(4 * CHUNK, 5 * CHUNK), chunk_cols(ddecay).astype(jnp.bfloat16)
        )

        d_scaled_q = dqueries * CHUNK ** (-0.5)
        gates = [jax.nn.sigmoid(piece[1]) for piece in pieces]
        unit_q, unit_k = pieces[0][1] * gates[0] * q_scale, pieces[1][1] * gates[1] * k_scale
        dact = [
            q_scale * (d_scaled_q - unit_q * lane_sum(d_scaled_q * unit_q)),
            k_scale * (dkeys - unit_k * lane_sum(dkeys * unit_k)),
            dvalues,
        ]
        for part in range(3):
            rows_by_offset, conv = pieces[part]
            gate = gates[part]
            dconv = dact[part] * (gate * (1.0 + conv * (1.0 - gate)))
            taps = taps_ref[part]
            after = next_ref[part]
            draw = dconv * taps[3:4]
            for offset in range(1, 4):
                kept = jnp.concatenate([dconv * keeps[offset - 1], after], axis=0)
                draw = draw + pltpu.roll(kept, CHUNK + 8 - offset, 0)[:CHUNK] * taps[3 - offset : 4 - offset]
            lanes = slice(part * CHUNK, (part + 1) * CHUNK)
            put_rows(draw_ref, place_ref, chunk, lanes, draw.astype(jnp.bfloat16))
            for offset in range(4):
                dtaps_ref[part, 3 - offset : 4 - offset] += jnp.sum(
                    dconv * rows_by_offset[offset], axis=0, keepdims=True
                )
            next_ref[part] = dconv[:8] * (1.0 - starts[0])


def back(place, starts, params, raw0, raw1, rows, taps, inverse, kkf, inner, joined, states, dstates, dcore, dgate):
    chunks = rows.shape[0]
    square = (BATCH, CHUNK, CHUNK)
    wide = (BATCH, CHUNK, 2 * CHUNK)
    turned = partial(per_batch, turned=True, steps=chunks // BATCH)
    draw = (2,) + raw0.shape
    return pl.pallas_call(
        back_kernel,
        grid_spec=pltpu.PrefetchScalarGridSpec(
            num_scalar_prefetch=3,
            grid=(chunks // BATCH,),
            in_specs=[whole(raw0.shape), whole(raw1.shape), turned((BATCH, 8, CHUNK)), whole(taps.shape),
                      turned(square), turned(square), turned(square), turned(wide), turned(square),
                      turned(square), turned(square), turned(square)],
            out_specs=[whole(draw), whole((3, 4, CHUNK)), whole((8, CHUNK))],
            scratch_shapes=[pltpu.VMEM((3, 8, CHUNK), jnp.float32)],
        ),
        out_shape=[shaped(draw, jnp.bfloat16), shaped((3, 4, CHUNK)), shaped((8, CHUNK))],
        compiler_params=pltpu.CompilerParams(vmem_limit_bytes=VMEM_MAX),
        name="back",
    )(place, starts, params, raw0, raw1, rows, taps, inverse, kkf, inner, joined, states, dstates, dcore, dgate)


def document_starts(doc_lengths, block_count):
    bounds = jnp.cumsum(doc_lengths)[:-1]
    blocks = jnp.arange(block_count, dtype=jnp.int32)
    opens = jnp.any(blocks[:, None] == bounds[None, :], axis=1) | (blocks == 0)
    return opens.astype(jnp.int32)


def mixer_forward(place, starts, params, raw0, raw1, taps, out_gain):
    rows, inverse, kkf, inner, joined, m, mt, b, r, pu = prepare(place, starts, params, raw0, raw1, taps)
    states, core, mixed, stored = scan_states(place, m, b, r, pu, raw0, raw1, out_gain)
    return mixed, stored, (rows, inverse, kkf, inner, joined, mt, r, states, core)


def mixer_backward(place, starts, params, raw0, raw1, taps, out_gain, kept, dmixed):
    rows, inverse, kkf, inner, joined, mt, r, states, core = kept
    dcore, dstates, dgate, dgain = back_scan(place, mt, r, core, raw0, raw1, dmixed, out_gain)
    draw, dtaps, dparams = back(
        place, starts, params, raw0, raw1, rows, taps, inverse, kkf, inner, joined, states, dstates, dcore, dgate
    )
    return draw, dtaps, dparams, dgain


from jax.sharding import PartitionSpec as P

LANES = 128
HALF = 384


def exchange_perm(count, shifted, sizes):
    pairs = []
    for target in range(count):
        source, scale, rest = 0, 1, target
        for size, offset in zip(reversed(sizes), reversed(shifted)):
            source += (rest % size + offset) % size * scale
            rest //= size
            scale *= size
        pairs.append((source, target))
    return pairs


def from_head(value, dz=0, dx=0, dc=0):
    return lax.ppermute(value, "head", exchange_perm(16, (dz, dx, dc), (4, 2, 2)))


def from_dp(value, dy=0, dx=0):
    return lax.ppermute(value, "dp", exchange_perm(8, (dy, dx), (4, 2)))


def gather_parts(value, take, cut):
    first, second = value[:cut], value[cut:]
    pair = jnp.concatenate([first, take(first, 0, 1)], axis=0)
    rings = [pair] + [take(pair, k, 0) for k in (1, 2, 3)]
    column = jnp.concatenate([second] + [take(second, k, 0) for k in (1, 2, 3)], axis=0)
    return rings, [column, take(column, 0, 1)]


def take_zx(value, ring, side):
    return from_head(value, dz=ring, dx=side)


def take_yx(value, ring, side):
    return from_dp(value, dy=ring, dx=side)


def gather_zx(value):
    rings, columns = gather_parts(value, take_zx, value.shape[0] * 5 // 8)
    return jnp.concatenate(rings + columns, axis=0)


def gather_dp(value):
    rings, columns = gather_parts(value, take_yx, value.shape[0] // 2)
    return jnp.concatenate(rings + columns, axis=0)


def wide(value):
    return value.astype(jnp.float32)


def narrow(value):
    return value.astype(jnp.bfloat16)


def reduce_parts(value, take, cut):
    rows = value.shape[0] // 8
    rest = rows - cut
    blocks = [value[2 * cut * k : 2 * cut * (k + 1)] for k in range(4)]
    near, far = value[8 * cut : 8 * cut + 4 * rest], value[8 * cut + 4 * rest :]
    summed = wide(blocks[0])
    for k in (1, 2, 3):
        summed = summed + wide(take(blocks[k], -k, 0))
    column = wide(near) + wide(take(far, 0, 1))
    first = (summed[:cut], take(narrow(summed[cut:]), 0, 1))
    second = (column[:rest],) + tuple(
        take(narrow(column[rest * k : rest * (k + 1)]), -k, 0) for k in (1, 2, 3)
    )
    return first, second


def reduce_zx(value):
    first, second = reduce_parts(value, take_zx, value.shape[0] // 8 * 5 // 8)
    return first + second


def reduce_dp(value):
    first, second = reduce_parts(value, take_yx, value.shape[0] // 16)
    return jnp.concatenate(
        [first[0] + wide(first[1]), second[0] + wide(second[1]) + wide(second[2]) + wide(second[3])], axis=0
    )


def ring_sum(value, take, position):
    pieces = [value] + [take(value, k, 0) for k in (1, 2, 3)]
    stacked = jnp.stack(pieces + pieces)
    ordered = lax.dynamic_slice_in_dim(stacked, (4 - position) % 4, 4, 0)
    return (ordered[0] + ordered[1]) + (ordered[2] + ordered[3])


def whole_call(kernel, out_shape, name, scalars, *arrays, scratch=()):
    outs = out_shape if isinstance(out_shape, (list, tuple)) else [out_shape]
    return pl.pallas_call(
        kernel,
        grid_spec=pltpu.PrefetchScalarGridSpec(
            num_scalar_prefetch=len(scalars),
            grid=(1,),
            in_specs=[whole(array.shape) for array in arrays],
            out_specs=[whole(out.shape) for out in outs],
            scratch_shapes=list(scratch),
        ),
        out_shape=list(outs),
        compiler_params=pltpu.CompilerParams(vmem_limit_bytes=VMEM_MAX),
        name=name,
    )(*scalars, *arrays)


def block_lanes(position):
    return slice(position * LANES, (position + 1) * LANES)


def placed_lanes(order_ref, position):
    return pl.ds(pl.multiple_of(order_ref[position] * LANES, LANES), LANES)


def rms_parts(values):
    scale = lax.rsqrt(jnp.mean(values * values, axis=-1, keepdims=True) + 1e-05)
    return scale, values * scale


def rms_back(grad, gain, scale, unit):
    inner = grad * gain
    return scale * (inner - unit * jnp.mean(inner * unit, axis=-1, keepdims=True))


def enter_kernel(order_ref, tokens_ref, cot_ref, gains_ref, normed_ref, rows_ref, grad_ref, gains_out_ref):
    for position in range(16):
        here, there = block_lanes(position), placed_lanes(order_ref, position)
        rows_ref[:, here] = tokens_ref[:, there]
        grad_ref[:, here] = cot_ref[:, there]
        gains_out_ref[:, here] = gains_ref[:, there]
    _, unit = rms_parts(wide(rows_ref[...]))
    normed_ref[...] = narrow(unit * gains_out_ref[0:1])


def attn_kernel(heads_ref, mixed_ref, first0_ref, first1_ref, second0_ref, second1_ref, rows_ref, gains_ref,
                resid_ref, normed_ref, total_ref):
    step = pl.program_id(0)

    @pl.when(step == 0)
    def _():
        total_ref[...] = wide(rows_ref[...])

    pair = jnp.concatenate([mixed_ref[heads_ref[0, step]], mixed_ref[heads_ref[1, step]]], axis=1)
    cut = first0_ref.shape[0]
    weights = jnp.concatenate([first0_ref[...], first1_ref[...]], axis=1)
    total_ref[:, :cut] += against(pair, weights)
    weights = jnp.concatenate([second0_ref[...], second1_ref[...]], axis=1)
    total_ref[:, cut:] += against(pair, weights)

    @pl.when(step == pl.num_programs(0) - 1)
    def _():
        resid = total_ref[...]
        resid_ref[...] = resid
        _, unit = rms_parts(resid)
        normed_ref[...] = narrow(unit * gains_ref[1:2])


def out_weight_specs(cut, rest):
    first = pl.BlockSpec((cut, LANES), lambda step, *_: (step, 0))
    second = pl.BlockSpec((rest, LANES), lambda step, *_: (step % 2 * 4 + step // 2, 0))
    return [first, first, second, second]


def attend(heads, received, out_parts, rows, gains):
    cut, rest = out_parts[0].shape[0] // 8, out_parts[2].shape[0] // 8
    shape = rows.shape
    return pl.pallas_call(
        attn_kernel,
        grid_spec=pltpu.PrefetchScalarGridSpec(
            num_scalar_prefetch=1,
            grid=(8,),
            in_specs=[whole(received.shape)] + out_weight_specs(cut, rest) + [whole(shape), whole(gains.shape)],
            out_specs=[whole(shape), whole(shape)],
            scratch_shapes=[pltpu.VMEM(shape, jnp.float32)],
        ),
        out_shape=[shaped(shape), shaped(shape, jnp.bfloat16)],
        compiler_params=pltpu.CompilerParams(vmem_limit_bytes=VMEM_MAX),
        name="attend",
    )(heads, received, *out_parts, rows, gains)


def total_of(refs):
    first = refs[0][...] + wide(refs[1][...])
    second = refs[2][...] + wide(refs[3][...]) + wide(refs[4][...]) + wide(refs[5][...])
    return jnp.concatenate([first, second], axis=0)


def middle_kernel(heads_ref, *refs):
    pieces, (resid_ref, cot_ref, gains_ref, first0_ref, first1_ref, second0_ref, second1_ref) = refs[:6], refs[6:13]
    dresid_ref, dattn_ref, dgain_ref, dmixed_ref = refs[13:]
    step = pl.program_id(0)

    @pl.when(step == 0)
    def _():
        grad = total_of(pieces)
        scale, unit = rms_parts(resid_ref[...])
        dgain_ref[...] = jnp.sum(grad * unit, axis=0, keepdims=True)
        dresid = wide(cot_ref[...]) + rms_back(grad, gains_ref[1:2], scale, unit)
        dresid_ref[...] = dresid
        dattn_ref[...] = narrow(dresid)

    cut = first0_ref.shape[0]
    dattn = dattn_ref[...]
    weights = jnp.concatenate([first0_ref[...], first1_ref[...]], axis=1)
    total = plain_product(dattn[:, :cut], weights)
    weights = jnp.concatenate([second0_ref[...], second1_ref[...]], axis=1)
    total = narrow(total + plain_product(dattn[:, cut:], weights))
    dmixed_ref[heads_ref[0, step]] = total[:, :LANES]
    dmixed_ref[heads_ref[1, step]] = total[:, LANES:]


def middle(heads, pieces, resid, cot, gains, out_parts):
    cut, rest = out_parts[0].shape[0] // 8, out_parts[2].shape[0] // 8
    shape = resid.shape
    mixed_shape = (16, shape[0], LANES)
    return pl.pallas_call(
        middle_kernel,
        grid_spec=pltpu.PrefetchScalarGridSpec(
            num_scalar_prefetch=1,
            grid=(8,),
            in_specs=[whole(piece.shape) for piece in pieces]
            + [whole(shape), whole(shape), whole(gains.shape)]
            + out_weight_specs(cut, rest),
            out_specs=[whole(shape), whole(shape), whole((1, shape[1])), whole(mixed_shape)],
        ),
        out_shape=[shaped(shape), shaped(shape, jnp.bfloat16), shaped((1, shape[1])),
                   shaped(mixed_shape, jnp.bfloat16)],
        compiler_params=pltpu.CompilerParams(vmem_limit_bytes=VMEM_MAX),
        name="middle",
    )(heads, *pieces, resid, cot, gains, *out_parts)


def leave_kernel(order_ref, *refs):
    pieces, (resid_ref, out_ref) = refs[:6], refs[6:]
    total = narrow(resid_ref[...] + total_of(pieces))
    for position in range(16):
        out_ref[:, placed_lanes(order_ref, position)] = total[:, block_lanes(position)]


def finish_kernel(order_ref, *refs):
    pieces, (rows_ref, dresid_ref, gains_ref, out_ref) = refs[:6], refs[6:]
    scale, unit = rms_parts(wide(rows_ref[...]))
    total = dresid_ref[...] + rms_back(total_of(pieces), gains_ref[0:1], scale, unit)
    for position in range(16):
        out_ref[:, placed_lanes(order_ref, position)] = total[:, block_lanes(position)]


def feed_kernel(normed_ref, cot_ref, gu0_ref, down0_ref, gu1_ref, down1_ref,
                out_ref, dnormed_ref, hidden_ref, dpre_ref):
    normed, cot = normed_ref[...], cot_ref[...]
    out, dnormed = 0.0, 0.0
    for half, (gu_ref, down_ref) in enumerate(((gu0_ref, down0_ref), (gu1_ref, down1_ref))):
        pre = plain_product(normed, gu_ref[...])
        gate, up = pre[:, :HALF], pre[:, HALF:]
        dhidden = plain_product(cot, down_ref[...])
        sigmoid = jax.nn.sigmoid(gate)
        act = gate * sigmoid
        hidden = narrow(act * up)
        dgate = narrow(dhidden * up * sigmoid * (1.0 + gate * (1.0 - sigmoid)))
        dpre = jnp.concatenate([dgate, narrow(dhidden * act)], axis=1)
        hidden_ref[:, half * HALF : (half + 1) * HALF] = hidden
        dpre_ref[:, 2 * half * HALF : 2 * (half + 1) * HALF] = dpre
        out = out + against(hidden, down_ref[...])
        dnormed = dnormed + against(dpre, gu_ref[...])
    out_ref[...] = narrow(out)
    dnormed_ref[...] = narrow(dnormed)


def feed(normed, cot, own, other):
    rows, width = normed.shape
    step = 256
    row_block = pl.BlockSpec((step, width), lambda i: (i, 0))
    gate_up = pl.BlockSpec((width, 2 * HALF), lambda i: (0, 0))
    down = pl.BlockSpec((width, HALF), lambda i: (0, 2))
    return pl.pallas_call(
        feed_kernel,
        grid=(rows // step,),
        in_specs=[row_block, row_block, gate_up, down, gate_up, down],
        out_specs=[row_block, row_block, pl.BlockSpec((step, 2 * HALF), lambda i: (i, 0)),
                   pl.BlockSpec((step, 4 * HALF), lambda i: (i, 0))],
        out_shape=[shaped((rows, width), jnp.bfloat16), shaped((rows, width), jnp.bfloat16),
                   shaped((rows, 2 * HALF), jnp.bfloat16), shaped((rows, 4 * HALF), jnp.bfloat16)],
        compiler_params=pltpu.CompilerParams(vmem_limit_bytes=VMEM_MAX),
        name="feed",
    )(normed, cot, own, own, other, other)


def plain_product(left, right):
    return jnp.dot(left, right, preferred_element_type=jnp.float32)


def against(left, right):
    return lax.dot_general(left, right, (((1,), (1,)), ((), ())), preferred_element_type=jnp.float32)


def over_rows(left, right):
    return lax.dot_general(left, right, (((0,), (0,)), ((), ())), preferred_element_type=jnp.float32)


def tables():
    head, group = lax.axis_index("head"), lax.axis_index("dp")
    ring, side, core = head // 4, head // 2 % 2, head % 2
    chunk = jnp.arange(16, dtype=jnp.int32)
    dz, dx, dc = (chunk // 4 - ring) % 4, (chunk // 2 + side) % 2, (chunk + core) % 2
    place = jnp.stack([ROWS_A * (2 * dz + dx), 8 * ROWS_A + ROWS_B * (4 * dx + dz), dc]).astype(jnp.int32)
    step = jnp.arange(8, dtype=jnp.int32)
    chip = ((step // 2 + ring) % 4) * 2 + (step + side) % 2
    heads = jnp.stack([2 * chip + core, 2 * chip + 1 - core]).astype(jnp.int32)
    up, over = group // 2, group % 2
    early = ((step // 2 + up) % 4) * 2 + (step + over) % 2
    late = ((step + up) % 4) * 2 + (step // 4 + over) % 2
    order = jnp.concatenate([2 * early, 2 * late + 1]).astype(jnp.int32)
    return place, heads, order


def body(
    tokens,
    cotangent,
    doc_spans,
    norm1_gain,
    q_weight,
    k_weight,
    v_weight,
    gate_out_weight,
    decay_weight,
    conv_weight,
    gate_params,
    out_gain,
    out_weight,
    norm2_gain,
    gate_weight,
    up_weight,
    down_weight,
):
    place, heads, order = tables()
    core = lax.axis_index("head") % 2
    starts = document_starts(doc_spans[0], 32)
    out_gain_row = out_gain[None, :]
    rows_shape = tokens.shape

    pad = lambda weight, columns: jnp.pad(weight, ((0, 0), (0, columns - weight.shape[1])))
    pack_one = jnp.concatenate(
        [q_weight, k_weight, v_weight, gate_out_weight, pad(decay_weight[:, 0], LANES), out_weight], axis=1
    )
    pack_two = jnp.concatenate([pad(gate_weight, HALF), pad(up_weight, HALF), pad(down_weight, HALF)], axis=1)
    taps = wide(lax.all_gather(conv_weight, "dp", axis=2, tiled=True))

    normed1, rows, cot, gains = whole_call(
        enter_kernel,
        [shaped(rows_shape, jnp.bfloat16)] * 3 + [shaped((2, rows_shape[1]))],
        "enter",
        (order,),
        tokens,
        cotangent,
        jnp.stack([norm1_gain, norm2_gain]),
    )
    mine_one = gather_dp(pack_one)
    weights_in = mine_one[:, : 5 * LANES]
    normed1_own = gather_zx(normed1)
    normed1_other = from_head(normed1_own, dc=1)
    raw0 = plain_product(normed1_own, weights_in)
    raw1 = plain_product(normed1_other, weights_in)

    weights_other = from_head(weights_in, dc=1)
    out_rings, out_columns = gather_parts(mine_one[:, 5 * LANES :], take_zx, 1280)
    out_first, out_second = jnp.concatenate(out_rings, axis=0), jnp.concatenate(out_columns, axis=0)
    out_parts = (out_first, from_head(out_first, dc=1), out_second, from_head(out_second, dc=1))
    mine_two = gather_dp(pack_two)
    other_two = from_head(mine_two, dc=1)
    cot_own = gather_zx(cot)

    mixed, stored, kept = mixer_forward(place, starts, gate_params, raw0, raw1, taps, out_gain_row)
    received = lax.all_to_all(mixed, "head", 0, 0, tiled=False)
    resid, normed2 = attend(heads, received, out_parts, rows, gains)
    normed2_own = gather_zx(normed2)
    fed, dnormed2, hidden, dpre = feed(normed2_own, cot_own, mine_two, other_two)

    dnormed2_pieces = reduce_zx(dnormed2)
    dresid, dattn, dgain2, dmixed = middle(heads, dnormed2_pieces, resid, cot, gains, out_parts)
    dmixed_mine = lax.all_to_all(dmixed, "head", 0, 0, tiled=False)

    (block_out,) = whole_call(
        leave_kernel, shaped(rows_shape, jnp.bfloat16), "leave", (order,), *reduce_zx(fed), resid
    )
    gate_up_grad = narrow(over_rows(normed2_own, dpre))
    down_grad = narrow(over_rows(cot_own, hidden))
    feed_own = jnp.concatenate([gate_up_grad[:, : 2 * HALF], down_grad[:, :HALF]], axis=1)
    feed_other = jnp.concatenate([gate_up_grad[:, 2 * HALF :], down_grad[:, HALF:]], axis=1)
    feed_grad = narrow(wide(feed_own) + wide(from_head(feed_other, dc=1)))
    feed_total = reduce_dp(feed_grad)

    dattn_own = gather_zx(dattn)
    mixed_pair = jnp.concatenate([stored[0], from_head(stored[1], dc=1)], axis=1)
    out_both = narrow(over_rows(dattn_own, mixed_pair))
    out_grad = narrow(wide(out_both[:, :LANES]) + wide(from_head(out_both[:, LANES:], dc=1)))

    draw, dtaps, dparams, dgain_out = mixer_backward(
        place, starts, gate_params, raw0, raw1, taps, out_gain_row, kept, dmixed_mine
    )
    draw_far = from_head(draw[1], dc=1)
    dnormed1 = against(draw[0], weights_in) + against(draw_far, weights_other)
    gain1_part = jnp.sum(dnormed1 * wide(normed1_own), axis=0) / gains[0]
    dnormed1_pieces = reduce_zx(narrow(dnormed1))

    in_grad = narrow(over_rows(normed1_own, draw[0]) + over_rows(normed1_other, draw[1]))
    one_total = reduce_dp(jnp.concatenate([in_grad, out_grad], axis=1))

    place_gain = lambda value: value.reshape(16, LANES)[inverse_order(order)]
    small = jnp.concatenate(
        [
            place_gain(gain1_part),
            place_gain(dgain2[0]),
            dgain_out,
            dparams,
            dtaps.reshape(12, LANES),
            jnp.zeros((4, LANES), jnp.float32),
        ],
        axis=0,
    )
    small = ring_sum(small, take_yx, lax.axis_index("dp") // 2)
    small = small + from_dp(small, dx=1)
    shared = small[:40]
    shared = ring_sum(shared, take_zx, lax.axis_index("head") // 4)
    shared = shared + from_head(shared, dx=1)
    shared = shared + from_head(shared, dc=1)
    gain1_total = shared[:16].reshape(-1)
    gain2_total = shared[16:32].reshape(-1)
    out_gain_total = jnp.sum(shared[32:40], axis=0)
    params_total = jnp.sum(small[40:48], axis=1)[:2, None]
    taps_total = lax.dynamic_slice_in_dim(
        small[48:60].reshape(3, 4, LANES), lax.axis_index("dp") * 16, 16, 2
    )

    (tokens_grad,) = whole_call(
        finish_kernel, shaped(rows_shape), "finish", (order,), *dnormed1_pieces, rows, dresid, gains
    )
    hidden_units = gate_weight.shape[1]
    return (
        block_out,
        tokens_grad,
        gain1_total,
        one_total[:, :LANES],
        one_total[:, LANES : 2 * LANES],
        one_total[:, 2 * LANES : 3 * LANES],
        one_total[:, 3 * LANES : 4 * LANES],
        one_total[:, 4 * LANES : 4 * LANES + 2][:, None, :],
        taps_total,
        params_total,
        out_gain_total,
        one_total[:, 5 * LANES :],
        gain2_total,
        feed_total[:, :hidden_units],
        feed_total[:, HALF : HALF + hidden_units],
        feed_total[:, 2 * HALF : 2 * HALF + hidden_units],
    )


def inverse_order(order):
    return jnp.argmax(order[None, :] == jnp.arange(16, dtype=jnp.int32)[:, None], axis=1)


def solution(mesh):
    rows, weight = P(("dp", "head"), None), P("dp", "head")
    weight3, taps = P("dp", "head", None), P(None, None, ("head", "dp"))
    params = P(None, "head")
    in_specs = (
        rows, rows, P("dp", None), P(), weight, weight, weight, weight, weight3, taps, params, P(),
        weight, P(), weight, weight, weight,
    )
    out_specs = (
        rows, rows, P(), weight, weight, weight, weight, weight3, taps, params, P(),
        weight, P(), weight, weight, weight,
    )
    return jax.shard_map(body, mesh=mesh, in_specs=in_specs, out_specs=out_specs, check_vma=False)
```

time: 2640 us -> 860 us (0.33); the launches traced: 2610 us -> 857 us
  matrix products: 817 us -> 51.5 us
  waiting for transfers between devices: 949 us -> 327 us
  local copies, waits for them, and re-layouts: 384 us -> 90.4 us
  blocking collectives: 274 us -> 28.2 us
  starting transfers between devices: 1.99 us -> 196 us
  Pallas kernels: 0 us -> 118 us
  other arithmetic: 161 us -> 43.9 us
    reduce_scatter x12 -> x0, waiting for transfers between devices: 728 us -> none  [the longest x1 143 us: body(): lax.psum_scatter(against(mixed_low, w_out).astype(jnp.bfloat16), 'head',...]
    dot_general x458 -> x0, matrix products: 602 us -> none  [product(): jnp.einsum(form, left, right, precision=lax.Precision.HIGHEST, preferred_...]
    ppermute x0 -> x114, waiting for transfers between devices: none -> 326 us  [the longest x78 251 us: from_head(): lax.ppermute(value, 'head', exchange_perm(16, (dz, dx, dc), (4, 2, 2)))]
    all_gather x7 -> x0, waiting for transfers between devices: 211 us -> none  [the longest x1 52.8 us: body(): group_grad = lax.all_gather(cotangent, 'head', axis=0, tiled=True)]
    dynamic_slice x193 -> x1, local copies, waits for them, and re-layouts: 192 us -> 0.67 us  [body(): lax.dynamic_slice_in_dim(small[48:60].reshape(3, 4, LANES), lax.axis_inde...]
    ppermute x0 -> x114, starting transfers between devices: none -> 181 us  [the longest x78 134 us: from_head(): lax.ppermute(value, 'head', exchange_perm(16, (dz, dx, dc), (4, 2, 2)))]
    all_gather x7 -> x1, blocking collectives: 207 us -> 28.2 us  [body(): taps = wide(lax.all_gather(conv_weight, 'dp', axis=2, tiled=True))]
    pallas_call x0 -> x10, Pallas kernels: none -> 118 us  [the longest x1 28.2 us: feed(): pl.pallas_call(feed_kernel, grid=(rows // step,), in_specs=[row_block, ro...]
  transfers between devices with their start and end apart: 21 -> 116, of which waited for: 15 -> 46; matrix products, arithmetic and copies ran while one was open for 35% -> 18% of each run, Pallas kernels for 0% -> 10%
where the time goes in v1:
time: 860 us; the launch traced here: 857 us
  waiting for transfers between devices  327 us (38%)
  starting transfers between devices  196 us (23%)
  Pallas kernels  118 us (14%)
  local copies, waits for them, and re-layouts  90.4 us (11%)
  matrix products  51.5 us (6%)
  other arithmetic  43.9 us (5%)
  blocking collectives  28.2 us (3%)
    ppermute x78, waiting for transfers between devices, from_head(): lax.ppermute(value, 'head', exchange_perm(16, (dz, dx, dc), (4, 2, 2)))  251 us
    ppermute x78, starting transfers between devices, from_head(): lax.ppermute(value, 'head', exchange_perm(16, (dz, dx, dc), (4, 2, 2)))  134 us
    ppermute x36, waiting for transfers between devices, from_dp(): return lax.ppermute(value, 'dp', exchange_perm(8, (dy, dx), (4, 2)))  74.5 us
    ppermute x36, starting transfers between devices, from_dp(): return lax.ppermute(value, 'dp', exchange_perm(8, (dy, dx), (4, 2)))  47.1 us
    unnamed x201, local copies, waits for them, and re-layouts  42.3 us
    pallas_call x1, Pallas kernels, feed(): pl.pallas_call(feed_kernel, grid=(rows // step,), in_specs=[row_block, ro...  28.2 us
    all_gather x1, blocking collectives, body(): taps = wide(lax.all_gather(conv_weight, 'dp', axis=2, tiled=True))  28.2 us
    pallas_call x1, Pallas kernels, back(): pl.pallas_call(back_kernel, grid_spec=pltpu.PrefetchScalarGridSpec(num_sc...  25.3 us
  transfers between devices with their start and end apart: 116, of which 46 were waited for; matrix products, arithmetic and copies ran while one was open for 18% of the time, Pallas kernels for 10%

profile of v1, /device:TPU:1, one launch (start us, length us, event | category | flops | bytes accessed | tf_op | source)
XLA Modules:
  0.0 856.5 jit_solution(2122201096859836878)
XLA Ops:
  26.0 28.2 %all_gather.3 = bf16[3,4,128]{1,0,2:T(4,128)(2,1)S(1)} all-gather(bf16[3,4,16]{1,0,2:T(4,128)(2,1)S(1)} %copy.58), channel_id=1, replica_groups=mesh['dp'=8,'head'=16] {'dp'}, dimensions={2}, use_global_device_ids=true | all-gather | bytes 3456 | tf_op jit(solution)/shard_map/all_gather | solution.py:943
  75.4 26.8 %collective-permute-done.12 = bf16[128,768]{1,0:T(8,128)(2,1)S(1)} collective-permute-done((bf16[128,768]{1,0:T(8,128)(2,1)S(1)}, bf16[128,768]{1,0:T(8,128)(2,1)S(1)}, u32[]{:S(2)}, u32[]{:S(2)}) %collective-permute-start.12) | collective-permute-done | bytes 196640 | tf_op jit(solution)/shard_map/ppermute | solution.py:615
  122.5 20.5 %collective-permute-done.1 = bf16[160,2048]{1,0:T(8,128)(2,1)S(1)} collective-permute-done((bf16[160,2048]{1,0:T(8,128)(2,1)S(1)}, bf16[160,2048]{1,0:T(8,128)(2,1)S(1)}, u32[]{:S(2)}, u32[]{:S(2)}) %collective-permute-start.1) | collective-permute-done | bytes 655392 | tf_op jit(solution)/shard_map/ppermute | solution.py:611
  143.1 14.1 %collective-permute-done.3 = bf16[160,2048]{1,0:T(8,128)(2,1)S(1)} collective-permute-done((bf16[160,2048]{1,0:T(8,128)(2,1)S(1)}, bf16[160,2048]{1,0:T(8,128)(2,1)S(1)}, u32[]{:S(2)}, u32[]{:S(2)}) %collective-permute-start.3) | collective-permute-done | bytes 655392 | tf_op jit(solution)/shard_map/ppermute | solution.py:611
  168.7 13.6 %collective-permute-start.38 = (bf16[160,2048]{1,0:T(8,128)(2,1)S(1)}, bf16[160,2048]{1,0:T(8,128)(2,1)S(1)}, u32[]{:S(2)}, u32[]{:S(2)}) collective-permute-start(bf16[160,2048]{1,0:T(8,128)(2,1)S(1)} %pad_maximum_fusion.12), channel_id=1, source_target_pairs={{12,0},{13,1},{14,2},{15,3},{0,4},{1,5},{2,6},{3,7},{4,8},{5,9},{6... | collective-permute-start | bytes 1966088 | tf_op jit(solution)/shard_map/ppermute | solution.py:611
  187.0 29.3 %collective-permute-done.7 = bf16[192,2048]{1,0:T(8,128)(2,1)S(1)} collective-permute-done((bf16[192,2048]{1,0:T(8,128)(2,1)S(1)}, bf16[192,2048]{1,0:T(8,128)(2,1)S(1)}, u32[]{:S(2)}, u32[]{:S(2)}) %collective-permute-start.7) | collective-permute-done | bytes 786464 | tf_op jit(solution)/shard_map/ppermute | solution.py:611
  216.4 10.8 %collective-permute-start.16 = (bf16[1024,2048]{1,0:T(8,128)(2,1)S(1)}, bf16[1024,2048]{1,0:T(8,128)(2,1)S(1)}, u32[]{:S(2)}, u32[]{:S(2)}) collective-permute-start(bf16[1024,2048]{1,0:T(8,128)(2,1)S(1)} %constant_dynamic-update-slice_fusion), channel_id=1, source_target_pairs={{1,0},{0,1},{3,2},{2,3},{5,4},{4,5},{7,6},{6,7},{9,8},{8,9},{11,10... | collective-permute-start | bytes 12582920 | tf_op jit(solution)/shard_map/ppermute | solution.py:611
  235.0 19.1 %collective-permute-done.22 = bf16[768,128]{1,0:T(8,128)(2,1)S(1)} collective-permute-done((bf16[768,128]{1,0:T(8,128)(2,1)S(1)}, bf16[768,128]{1,0:T(8,128)(2,1)S(1)}, u32[]{:S(2)}, u32[]{:S(2)}) %collective-permute-start.22) | collective-permute-done | bytes 196640 | tf_op jit(solution)/shard_map/ppermute | solution.py:611
  260.6 11.8 %collective-permute-done.19 = bf16[2560,128]{1,0:T(8,128)(2,1)S(1)} collective-permute-done((bf16[2560,128]{1,0:T(8,128)(2,1)S(1)}, bf16[2560,128]{1,0:T(8,128)(2,1)S(1)}, u32[]{:S(2)}, u32[]{:S(2)}) %collective-permute-start.19) | collective-permute-done | bytes 655392 | tf_op jit(solution)/shard_map/ppermute | solution.py:611
  272.4 16.0 %collective-permute-done.20 = bf16[2560,128]{1,0:T(8,128)(2,1)S(1)} collective-permute-done((bf16[2560,128]{1,0:T(8,128)(2,1)S(1)}, bf16[2560,128]{1,0:T(8,128)(2,1)S(1)}, u32[]{:S(2)}, u32[]{:S(2)}) %collective-permute-start.20) | collective-permute-done | bytes 655392 | tf_op jit(solution)/shard_map/ppermute | solution.py:611
  312.5 18.2 %prepare.1 = (f32[16,8,128]{2,1,0:T(8,128)}, f32[16,128,128]{2,1,0:T(8,128)}, f32[16,128,128]{2,1,0:T(8,128)}, f32[16,128,128]{2,1,0:T(8,128)}, f32[16,128,256]{...) custom-call(s32[3,16]{1,0:T(4,128)} %pad_add_fusion.place_ref, ...), custom_call_target="tpu_custom_call" | custom-call | tf_op jit(solution)/shard_map/prepare/pallas_call | solution.py:287
  355.6 10.0 %attend.1 = (f32[128,2048]{1,0:T(8,128)}, bf16[128,2048]{1,0:T(8,128)(2,1)}) custom-call(s32[2,8]{1,0:T(2,128)} %pad_add_fusion.1.heads_ref, bf16[16,128,128]{2,1,0:T(8,128)(2,1)} %copy-done.12, bf16[10240,128]{1,0:T(8,128)(2,1)} %copy-done.2, bf16[10240,128]{1,0:T(8,128)(2,1)} %collective-permute-done.21.first1_ref.refs_10_, ...), custom_call_target="tpu_custom_call" | custom-call | tf_op jit(solution)/shard_map/attend/pallas_call | solution.py:764
  395.2 15.6 %collective-permute-done.30 = bf16[160,2048]{1,0:T(8,128)(2,1)S(1)} collective-permute-done((bf16[160,2048]{1,0:T(8,128)(2,1)S(1)}, bf16[160,2048]{1,0:T(8,128)(2,1)S(1)}, u32[]{:S(2)}, u32[]{:S(2)}) %collective-permute-start.30) | collective-permute-done | bytes 655392 | tf_op jit(solution)/shard_map/ppermute | solution.py:611
  426.4 15.6 %collective-permute-done.34 = bf16[192,2048]{1,0:T(8,128)(2,1)S(1)} collective-permute-done((bf16[192,2048]{1,0:T(8,128)(2,1)S(1)}, bf16[192,2048]{1,0:T(8,128)(2,1)S(1)}, u32[]{:S(2)}, u32[]{:S(2)}) %collective-permute-start.34) | collective-permute-done | bytes 786464 | tf_op jit(solution)/shard_map/ppermute | solution.py:611
  444.0 28.2 %feed.1 = (bf16[1024,2048]{1,0:T(8,128)(2,1)}, bf16[1024,2048]{1,0:T(8,128)(2,1)}, bf16[1024,768]{1,0:T(8,128)(2,1)}, bf16[1024,1536]{1,0:T(8,128)(2,1)}) custom-call(bf16[1024,2048]{1,0:T(8,128)(2,1)} %copy-done.4, bf16[1024,2048]{1,0:T(8,128)(2,1)} %constant_dynamic-update-slice_fusion.53.cot_ref, ...), custom_call_target="tpu_custom_call" | custom-call | tf_op jit(solution)/shard_map/feed/pallas_call | solution.py:872
  472.3 9.8 %convolution_convert_fusion = bf16[2048,1536]{0,1:T(8,128)(2,1)S(1)} fusion(bf16[1024,2048]{1,0:T(8,128)(2,1)} %copy-done.4, bf16[1024,1536]{1,0:T(8,128)(2,1)} %get-tuple-element.86), kind=kOutput, calls=%fused_computation.4 | convolution fusion | flops 6445596672 | bytes 13631488 | tf_op jit(solution)/shard_map/dot_general | solution.py:894
  505.2 11.7 %collective-permute-done.61 = bf16[160,2048]{1,0:T(8,128)(2,1)S(1)} collective-permute-done((bf16[160,2048]{1,0:T(8,128)(2,1)S(1)}, bf16[160,2048]{1,0:T(8,128)(2,1)S(1)}, u32[]{:S(2)}, u32[]{:S(2)}) %collective-permute-start.61) | collective-permute-done | bytes 655392 | tf_op jit(solution)/shard_map/ppermute | solution.py:611
  530.8 14.2 %collective-permute-done.53 = bf16[160,2048]{1,0:T(8,128)(2,1)S(1)} collective-permute-done((bf16[160,2048]{1,0:T(8,128)(2,1)S(1)}, bf16[160,2048]{1,0:T(8,128)(2,1)S(1)}, u32[]{:S(2)}, u32[]{:S(2)}) %collective-permute-start.53) | collective-permute-done | bytes 655392 | tf_op jit(solution)/shard_map/ppermute | solution.py:611
  566.6 10.5 %middle.1 = (f32[128,2048]{1,0:T(8,128)}, bf16[128,2048]{1,0:T(8,128)(2,1)}, f32[1,2048]{1,0:T(1,128)}, bf16[16,128,128]{2,1,0:T(8,128)(2,1)}) custom-call(s32[2,8]{1,0:T(2,128)} %pad_add_fusion.1.heads_ref, f32[80,2048]{1,0:T(8,128)} %slice.488.refs_0_, bf16[80,2048]{1,0:T(8,128)(2,1)} %copy-done.23, f32[48,2048]{1,0:T(8,128)} %slice.490.refs_2_, ...), custom_call_target="tpu_custom_call" | custom-call | tf_op jit(solution)/shard_map/middle/pallas_call | solution.py:813
  613.1 25.3 %back.1 = (bf16[2,1024,640]{2,1,0:T(8,128)(2,1)}, f32[3,4,128]{2,1,0:T(4,128)}, f32[8,128]{1,0:T(8,128)}) custom-call(s32[3,16]{1,0:T(4,128)} %pad_add_fusion.place_ref, s32[32]{0:T(128)} %or_convert_fusion.starts_ref, f32[2,1]{1,0:T(2,128)} %copy.60.params_ref, f32[1024,640]{1,0:T(8,128)} %fusion.60.raw0_ref.gate0_ref, ...), custom_call_target="tpu_custom_call" | custom-call | tf_op jit(solution)/shard_map/back/pallas_call | solution.py:553
  669.6 9.1 %fusion.84 = f32[1024,2048]{1,0:T(8,128)} fusion(bf16[1024,640]{1,0:T(8,128)(2,1)} %collective-permute-done.68, bf16[2048,640]{1,0:T(8,128)(2,1)} %collective-permute-done.69), kind=kOutput, calls=%fused_computation.325 | convolution fusion | flops 2684354560 | bytes 12320768 | tf_op jit(solution)/shard_map/dot_general | solution.py:890
  705.3 8.2 collective-permute-done.83
  740.5 9.1 %collective-permute-done.72 = bf16[160,2048]{1,0:T(8,128)(2,1)S(1)} collective-permute-done((bf16[160,2048]{1,0:T(8,128)(2,1)}, bf16[160,2048]{1,0:T(8,128)(2,1)S(1)}, u32[]{:S(2)}, u32[]{:S(2)}) %collective-permute-start.72) | collective-permute-done | bytes 655392 | tf_op jit(solution)/shard_map/ppermute | solution.py:611
  820.7 9.3 %collective-permute-done.107 = bf16[256,1152]{0,1:T(8,128)(2,1)} collective-permute-done((bf16[256,1152]{0,1:T(8,128)(2,1)}, bf16[256,1152]{0,1:T(8,128)(2,1)}, u32[]{:S(2)}, u32[]{:S(2)}) %collective-permute-start.107) | collective-permute-done | bytes 589856 | tf_op jit(solution)/shard_map/ppermute | solution.py:615
  (556 shorter events, 469.5 us)
Async XLA Ops:
  5.1 51.8 %collective-permute-start.47 = (bf16[128,1152]{1,0:T(8,128)(2,1)S(1)}, bf16[128,1152]{1,0:T(8,128)(2,1)S(1)}, u32[]{:S(2)}, u32[]{:S(2)}) collective-permute-start(bf16[128,1152]{1,0:T(8,128)(2,1)S(1)} %get-tuple-element.194), channel_id=1, source_target_pairs={{32,0},{48,16},{64,32},{80,48},{96,64},{112,80},{0,96},{16,112},{3... | collective-permute-start | bytes 884744 | tf_op jit(solution)/shard_map/ppermute | solution.py:615
  8.7 49.4 %collective-permute-start.48 = (bf16[128,1152]{1,0:T(8,128)(2,1)S(1)}, bf16[128,1152]{1,0:T(8,128)(2,1)}, u32[]{:S(2)}, u32[]{:S(2)}) collective-permute-start(bf16[128,1152]{1,0:T(8,128)(2,1)S(1)} %get-tuple-element.194), channel_id=1, source_target_pairs={{64,0},{80,16},{96,32},{112,48},{0,64},{16,80},{32,96},{48,112},{6... | collective-permute-start | bytes 884744 | tf_op jit(solution)/shard_map/ppermute | solution.py:615
  9.0 51.5 %collective-permute-start.49 = (bf16[128,1152]{1,0:T(8,128)(2,1)S(1)}, bf16[128,1152]{1,0:T(8,128)(2,1)S(1)}, u32[]{:S(2)}, u32[]{:S(2)}) collective-permute-start(bf16[128,1152]{1,0:T(8,128)(2,1)S(1)} %get-tuple-element.194), channel_id=1, source_target_pairs={{96,0},{112,16},{0,32},{16,48},{32,64},{48,80},{64,96},{80,112},{9... | collective-permute-start | bytes 884744 | tf_op jit(solution)/shard_map/ppermute | solution.py:615
  16.0 49.2 %collective-permute-start.35 = (bf16[80,2048]{1,0:T(8,128)(2,1)S(1)}, bf16[80,2048]{1,0:T(8,128)(2,1)S(1)}, u32[]{:S(2)}, u32[]{:S(2)}) collective-permute-start(bf16[80,2048]{1,0:T(8,128)(2,1)S(1)} %get-tuple-element.205), channel_id=1, source_target_pairs={{2,0},{3,1},{0,2},{1,3},{6,4},{7,5},{4,6},{5,7},{10,8},{11,9},{8,1... | collective-permute-start | bytes 983048 | tf_op jit(solution)/shard_map/ppermute | solution.py:611
  65.3 48.7 %collective-permute-start.44 = (bf16[256,1152]{1,0:T(8,128)(2,1)S(1)}, bf16[256,1152]{1,0:T(8,128)(2,1)S(1)}, u32[]{:S(2)}, u32[]{:S(2)}) collective-permute-start(bf16[256,1152]{1,0:T(8,128)(2,1)S(1)} %pad_maximum_fusion.14), channel_id=1, source_target_pairs={{32,0},{48,16},{64,32},{80,48},{96,64},{112,80},{0,96},{16,112},{3... | collective-permute-start | bytes 1769480 | tf_op jit(solution)/shard_map/ppermute | solution.py:615
  67.9 47.4 %collective-permute-start.45 = (bf16[256,1152]{1,0:T(8,128)(2,1)S(1)}, bf16[256,1152]{1,0:T(8,128)(2,1)S(1)}, u32[]{:S(2)}, u32[]{:S(2)}) collective-permute-start(bf16[256,1152]{1,0:T(8,128)(2,1)S(1)} %pad_maximum_fusion.14), channel_id=1, source_target_pairs={{64,0},{80,16},{96,32},{112,48},{0,64},{16,80},{32,96},{48,112},{6... | collective-permute-start | bytes 1769480 | tf_op jit(solution)/shard_map/ppermute | solution.py:615
  71.0 47.3 %collective-permute-start.46 = (bf16[256,1152]{1,0:T(8,128)(2,1)S(1)}, bf16[256,1152]{1,0:T(8,128)(2,1)S(1)}, u32[]{:S(2)}, u32[]{:S(2)}) collective-permute-start(bf16[256,1152]{1,0:T(8,128)(2,1)S(1)} %pad_maximum_fusion.14), channel_id=1, source_target_pairs={{96,0},{112,16},{0,32},{16,48},{32,64},{48,80},{64,96},{80,112},{9... | collective-permute-start | bytes 1769480 | tf_op jit(solution)/shard_map/ppermute | solution.py:615
  102.2 82.5 %collective-permute-start.36 = (bf16[160,2048]{1,0:T(8,128)(2,1)S(1)}, bf16[160,2048]{1,0:T(8,128)(2,1)S(1)}, u32[]{:S(2)}, u32[]{:S(2)}) collective-permute-start(bf16[160,2048]{1,0:T(8,128)(2,1)S(1)} %pad_maximum_fusion.12), channel_id=1, source_target_pairs={{4,0},{5,1},{6,2},{7,3},{8,4},{9,5},{10,6},{11,7},{12,8},{13,9},{1... | collective-permute-start | bytes 1966088 | tf_op jit(solution)/shard_map/ppermute | solution.py:611
  110.3 116.8 %collective-permute-start.37 = (bf16[160,2048]{1,0:T(8,128)(2,1)S(1)}, bf16[160,2048]{1,0:T(8,128)(2,1)S(1)}, u32[]{:S(2)}, u32[]{:S(2)}) collective-permute-start(bf16[160,2048]{1,0:T(8,128)(2,1)S(1)} %pad_maximum_fusion.12), channel_id=1, source_target_pairs={{8,0},{9,1},{10,2},{11,3},{12,4},{13,5},{14,6},{15,7},{0,8},{1,9},... | collective-permute-start | bytes 1966088 | tf_op jit(solution)/shard_map/ppermute | solution.py:611
  168.7 59.4 %collective-permute-start.38 = (bf16[160,2048]{1,0:T(8,128)(2,1)S(1)}, bf16[160,2048]{1,0:T(8,128)(2,1)S(1)}, u32[]{:S(2)}, u32[]{:S(2)}) collective-permute-start(bf16[160,2048]{1,0:T(8,128)(2,1)S(1)} %pad_maximum_fusion.12), channel_id=1, source_target_pairs={{12,0},{13,1},{14,2},{15,3},{0,4},{1,5},{2,6},{3,7},{4,8},{5,9},{6... | collective-permute-start | bytes 1966088 | tf_op jit(solution)/shard_map/ppermute | solution.py:611
  182.3 49.9 %collective-permute-start.15 = (bf16[512,768]{1,0:T(8,128)(2,1)S(1)}, bf16[512,768]{1,0:T(8,128)(2,1)S(1)}, u32[]{:S(2)}, u32[]{:S(2)}) collective-permute-start(bf16[512,768]{1,0:T(8,128)(2,1)S(1)} %pad_maximum_fusion.4), channel_id=1, source_target_pairs={{16,0},{0,16},{48,32},{32,48},{80,64},{64,80},{112,96},{96,112},{1... | collective-permute-start | bytes 2359304 | tf_op jit(solution)/shard_map/ppermute | solution.py:615
  216.4 89.2 %collective-permute-start.16 = (bf16[1024,2048]{1,0:T(8,128)(2,1)S(1)}, bf16[1024,2048]{1,0:T(8,128)(2,1)S(1)}, u32[]{:S(2)}, u32[]{:S(2)}) collective-permute-start(bf16[1024,2048]{1,0:T(8,128)(2,1)S(1)} %constant_dynamic-update-slice_fusion), channel_id=1, source_target_pairs={{1,0},{0,1},{3,2},{2,3},{5,4},{4,5},{7,6},{6,7},{9,8},{8,9},{11,10... | collective-permute-start | bytes 12582920 | tf_op jit(solution)/shard_map/ppermute | solution.py:611
  254.2 95.4 %collective-permute-start.50 = (bf16[512,1152]{1,0:T(8,128)(2,1)}, bf16[512,1152]{1,0:T(8,128)(2,1)}, u32[]{:S(2)}, u32[]{:S(2)}) collective-permute-start(bf16[512,1152]{1,0:T(8,128)(2,1)} %pad_maximum_fusion.1), channel_id=1, source_target_pairs={{16,0},{0,16},{48,32},{32,48},{80,64},{64,80},{112,96},{96,112},{1... | collective-permute-start | bytes 3538952 | tf_op jit(solution)/shard_map/ppermute | solution.py:615
  288.5 65.3 %collective-permute-start.21 = (bf16[10240,128]{1,0:T(8,128)(2,1)S(1)}, bf16[10240,128]{1,0:T(8,128)(2,1)}, u32[]{:S(2)}, u32[]{:S(2)}) collective-permute-start(bf16[10240,128]{1,0:T(8,128)(2,1)S(1)} %constant_dynamic-update-slice_fusion.33.first0_ref.refs_9_), channel_id=1, source_target_pairs={{1,0},{0,1},{3,2},{2,3},{5,4},{4,5},{7,6},{6,7},{9,8},{8,9},{11,10... | collective-permute-start | bytes 7864328 | tf_op jit(solution)/shard_map/ppermute | solution.py:611
  298.3 54.2 %collective-permute-start.26 = (bf16[6144,128]{1,0:T(8,128)(2,1)}, bf16[6144,128]{1,0:T(8,128)(2,1)}, u32[]{:S(2)}, u32[]{:S(2)}) collective-permute-start(bf16[6144,128]{1,0:T(8,128)(2,1)} %constant_dynamic-update-slice_fusion.38.second0_ref.refs_11_), channel_id=1, source_target_pairs={{1,0},{0,1},{3,2},{2,3},{5,4},{4,5},{7,6},{6,7},{9,8},{8,9},{11,10... | collective-permute-start | bytes 4718600 | tf_op jit(solution)/shard_map/ppermute | solution.py:611
  352.6 89.4 %collective-permute-start.51 = (bf16[2048,1152]{1,0:T(8,128)(2,1)}, bf16[2048,1152]{1,0:T(8,128)(2,1)}, u32[]{:S(2)}, u32[]{:S(2)}) collective-permute-start(bf16[2048,1152]{1,0:T(8,128)(2,1)} %constant_dynamic-update-slice_fusion.63.gu0_ref.down0_ref), channel_id=1, source_target_pairs={{1,0},{0,1},{3,2},{2,3},{5,4},{4,5},{7,6},{6,7},{9,8},{8,9},{11,10... | collective-permute-start | bytes 14155784 | tf_op jit(solution)/shard_map/ppermute | solution.py:611
  369.0 46.7 %collective-permute-start.42 = (bf16[192,2048]{1,0:T(8,128)(2,1)S(1)}, bf16[192,2048]{1,0:T(8,128)(2,1)S(1)}, u32[]{:S(2)}, u32[]{:S(2)}) collective-permute-start(bf16[192,2048]{1,0:T(8,128)(2,1)S(1)} %pad_maximum_fusion.7), channel_id=1, source_target_pairs={{2,0},{3,1},{0,2},{1,3},{6,4},{7,5},{4,6},{5,7},{10,8},{11,9},{8,1... | collective-permute-start | bytes 2359304 | tf_op jit(solution)/shard_map/ppermute | solution.py:611
  494.7 50.3 %collective-permute-start.53 = (bf16[160,2048]{1,0:T(8,128)(2,1)S(1)}, bf16[160,2048]{1,0:T(8,128)(2,1)S(1)}, u32[]{:S(2)}, u32[]{:S(2)}) collective-permute-start(bf16[160,2048]{1,0:T(8,128)(2,1)S(1)} %get-tuple-element.163), channel_id=1, source_target_pairs={{8,0},{9,1},{10,2},{11,3},{12,4},{13,5},{14,6},{15,7},{0,8},{1,9},... | collective-permute-start | bytes 1966088 | tf_op jit(solution)/shard_map/ppermute | solution.py:611
  501.5 47.0 %collective-permute-start.54 = (bf16[160,2048]{1,0:T(8,128)(2,1)S(1)}, bf16[160,2048]{1,0:T(8,128)(2,1)S(1)}, u32[]{:S(2)}, u32[]{:S(2)}) collective-permute-start(bf16[160,2048]{1,0:T(8,128)(2,1)S(1)} %get-tuple-element.162), channel_id=1, source_target_pairs={{4,0},{5,1},{6,2},{7,3},{8,4},{9,5},{10,6},{11,7},{12,8},{13,9},{1... | collective-permute-start | bytes 1966088 | tf_op jit(solution)/shard_map/ppermute | solution.py:611
  549.7 47.2 %collective-permute-start.55 = (bf16[80,2048]{1,0:T(8,128)(2,1)}, bf16[80,2048]{1,0:T(8,128)(2,1)}, u32[]{:S(2)}, u32[]{:S(2)}) collective-permute-start(bf16[80,2048]{1,0:T(8,128)(2,1)} %slice.657), channel_id=1, source_target_pairs={{2,0},{3,1},{0,2},{1,3},{6,4},{7,5},{4,6},{5,7},{10,8},{11,9},{8,1... | collective-permute-start | bytes 983048 | tf_op jit(solution)/shard_map/ppermute | solution.py:611
  595.9 73.7 %collective-permute-start.69 = (bf16[2048,640]{1,0:T(8,128)(2,1)}, bf16[2048,640]{1,0:T(8,128)(2,1)}, u32[]{:S(2)}, u32[]{:S(2)}) collective-permute-start(bf16[2048,640]{1,0:T(8,128)(2,1)} %slice.478), channel_id=1, source_target_pairs={{1,0},{0,1},{3,2},{2,3},{5,4},{4,5},{7,6},{6,7},{9,8},{8,9},{11,10... | collective-permute-start | bytes 7864328 | tf_op jit(solution)/shard_map/ppermute | solution.py:611
  658.0 67.6 %collective-permute-start.95 = (bf16[1024,128]{1,0:T(8,128)(2,1)}, bf16[1024,128]{1,0:T(8,128)(2,1)}, u32[]{:S(2)}, u32[]{:S(2)}) collective-permute-start(bf16[1024,128]{1,0:T(8,128)(2,1)} %get-tuple-element.198), channel_id=1, source_target_pairs={{1,0},{0,1},{3,2},{2,3},{5,4},{4,5},{7,6},{6,7},{9,8},{8,9},{11,10... | collective-permute-start | bytes 786440 | tf_op jit(solution)/shard_map/ppermute | solution.py:611
  662.7 134.2 %collective-permute-start.105 = (bf16[2048,1152]{0,1:T(8,128)(2,1)}, bf16[2048,1152]{0,1:T(8,128)(2,1)}, u32[]{:S(2)}, u32[]{:S(2)}) collective-permute-start(bf16[2048,1152]{0,1:T(8,128)(2,1)} %pad_maximum_fusion), channel_id=1, source_target_pairs={{1,0},{0,1},{3,2},{2,3},{5,4},{4,5},{7,6},{6,7},{9,8},{8,9},{11,10... | collective-permute-start | bytes 14155784 | tf_op jit(solution)/shard_map/ppermute | solution.py:611
  666.9 55.3 %collective-permute-start.94 = (bf16[192,2048]{1,0:T(8,128)(2,1)}, bf16[192,2048]{1,0:T(8,128)(2,1)}, u32[]{:S(2)}, u32[]{:S(2)}) collective-permute-start(bf16[192,2048]{1,0:T(8,128)(2,1)} %pad_maximum_fusion.8), channel_id=1, source_target_pairs={{2,0},{3,1},{0,2},{1,3},{6,4},{7,5},{4,6},{5,7},{10,8},{11,9},{8,1... | collective-permute-start | bytes 2359304 | tf_op jit(solution)/shard_map/ppermute | solution.py:611
  (150 other events, 2656.8 us)

commit v2 on v1

--- a/solution.py
+++ b/solution.py
@@ -8,10 +8,14 @@
 
 CHUNK = 128
 BATCH = 4
-ROWS_A = 80
-ROWS_B = 48
+ROWS_A = 64
+ROWS_B = 64
 GATE_ALONE = 9
 VMEM_MAX = 56 * 1024 * 1024
+
+
+def spends(microseconds):
+    return pl.CostEstimate(flops=int(microseconds * 1e6), bytes_accessed=1 << 10, transcendentals=0)
 
 
 def split(value):
@@ -294,6 +298,7 @@
         ),
         out_shape=[shaped((chunks,) + shape[1:], dtype) for shape, dtype in kinds],
         compiler_params=pltpu.CompilerParams(vmem_limit_bytes=VMEM_MAX),
+        cost_estimate=spends(18),
         name="prepare",
     )(place, starts, params, raw0, raw1, taps)
 
@@ -303,7 +308,7 @@
 
 
 def scan_kernel(place_ref, m_ref, b_ref, r_ref, pu_ref, gate0_ref, gate1_ref, gain_ref,
-                state_out_ref, core_ref, mixed_ref, stored_ref, state_ref):
+                state_out_ref, core_ref, mixed_ref, state_ref):
     @pl.when(pl.program_id(0) == 0)
     def _():
         state_ref[...] = jnp.zeros_like(state_ref)
@@ -320,7 +325,6 @@
         scale = lax.rsqrt(jnp.mean(core * core, axis=-1, keepdims=True) + 1e-05)
         mixed = (core * scale * gain_ref[...] * gate).astype(jnp.bfloat16)
         mixed_ref[member] = mixed
-        put_rows(stored_ref, place_ref, chunk, slice(None), mixed)
     state_ref[...] = state
 
 
@@ -332,7 +336,6 @@
     chunks = m.shape[0]
     square = (BATCH, CHUNK, CHUNK)
     wide = (BATCH, CHUNK, 2 * CHUNK)
-    stored = (2, raw0.shape[0], CHUNK)
     return pl.pallas_call(
         scan_kernel,
         grid_spec=pltpu.PrefetchScalarGridSpec(
@@ -340,12 +343,13 @@
             grid=(chunks // BATCH,),
             in_specs=[per_batch(wide), per_batch(square), per_batch(square), per_batch(square),
                       gate_columns(raw0), gate_columns(raw1), whole((1, CHUNK))],
-            out_specs=[per_batch(square)] * 3 + [whole(stored)],
+            out_specs=[per_batch(square)] * 3,
             scratch_shapes=[pltpu.VMEM((CHUNK, CHUNK), jnp.float32)],
         ),
         out_shape=[shaped((chunks, CHUNK, CHUNK)), shaped((chunks, CHUNK, CHUNK)),
-                   shaped((chunks, CHUNK, CHUNK), jnp.bfloat16), shaped(stored, jnp.bfloat16)],
+                   shaped((chunks, CHUNK, CHUNK), jnp.bfloat16)],
         compiler_params=pltpu.CompilerParams(vmem_limit_bytes=VMEM_MAX),
+        cost_estimate=spends(7),
         name="scan_states",
     )(place, m, b, r, pu, raw0, raw1, gain)
 
@@ -405,6 +409,7 @@
         out_shape=[shaped((chunks, CHUNK, CHUNK)), shaped((chunks, CHUNK, CHUNK)),
                    shaped((chunks, CHUNK, CHUNK), jnp.bfloat16), shaped((8, CHUNK))],
         compiler_params=pltpu.CompilerParams(vmem_limit_bytes=VMEM_MAX),
+        cost_estimate=spends(7),
         name="back_scan",
     )(place, mt, r, core, raw0, raw1, dmixed, gain)
 
@@ -415,7 +420,7 @@
 
 def back_kernel(place_ref, starts_ref, params_ref, raw0_ref, raw1_ref, rows_ref, taps_ref, inv_ref, kkf_ref,
                 p_ref, uw_ref, state_ref, dstate_ref, dcore_ref, dgate_ref,
-                draw_ref, dtaps_ref, dparams_ref, next_ref):
+                draw0_ref, draw1_ref, dtaps_ref, dparams_ref, next_ref, draw_ref):
     step = pl.program_id(0)
     row_index, col_index = iotas()
     lower = row_index >= col_index
@@ -543,6 +548,11 @@
                 )
             next_ref[part] = dconv[:8] * (1.0 - starts[0])
 
+    @pl.when(step == pl.num_programs(0) - 1)
+    def _():
+        draw0_ref[...] = draw_ref[0]
+        draw1_ref[...] = draw_ref[1]
+
 
 def back(place, starts, params, raw0, raw1, rows, taps, inverse, kkf, inner, joined, states, dstates, dcore, dgate):
     chunks = rows.shape[0]
@@ -558,11 +568,12 @@
             in_specs=[whole(raw0.shape), whole(raw1.shape), turned((BATCH, 8, CHUNK)), whole(taps.shape),
                       turned(square), turned(square), turned(square), turned(wide), turned(square),
                       turned(square), turned(square), turned(square)],
-            out_specs=[whole(draw), whole((3, 4, CHUNK)), whole((8, CHUNK))],
-            scratch_shapes=[pltpu.VMEM((3, 8, CHUNK), jnp.float32)],
+            out_specs=[whole(raw0.shape), whole(raw0.shape), whole((3, 4, CHUNK)), whole((8, CHUNK))],
+            scratch_shapes=[pltpu.VMEM((3, 8, CHUNK), jnp.float32), pltpu.VMEM(draw, jnp.bfloat16)],
         ),
-        out_shape=[shaped(draw, jnp.bfloat16), shaped((3, 4, CHUNK)), shaped((8, CHUNK))],
+        out_shape=[shaped(raw0.shape, jnp.bfloat16)] * 2 + [shaped((3, 4, CHUNK)), shaped((8, CHUNK))],
         compiler_params=pltpu.CompilerParams(vmem_limit_bytes=VMEM_MAX),
+        cost_estimate=spends(24),
         name="back",
     )(place, starts, params, raw0, raw1, rows, taps, inverse, kkf, inner, joined, states, dstates, dcore, dgate)
 
@@ -574,25 +585,29 @@
     return opens.astype(jnp.int32)
 
 
-def mixer_forward(place, starts, params, raw0, raw1, taps, out_gain):
-    rows, inverse, kkf, inner, joined, m, mt, b, r, pu = prepare(place, starts, params, raw0, raw1, taps)
-    states, core, mixed, stored = scan_states(place, m, b, r, pu, raw0, raw1, out_gain)
-    return mixed, stored, (rows, inverse, kkf, inner, joined, mt, r, states, core)
-
-
-def mixer_backward(place, starts, params, raw0, raw1, taps, out_gain, kept, dmixed):
-    rows, inverse, kkf, inner, joined, mt, r, states, core = kept
-    dcore, dstates, dgate, dgain = back_scan(place, mt, r, core, raw0, raw1, dmixed, out_gain)
-    draw, dtaps, dparams = back(
+def mixer_forward(place, prepared, raw0, raw1, out_gain):
+    rows, inverse, kkf, inner, joined, m, mt, b, r, pu = prepared
+    states, core, mixed = scan_states(place, m, b, r, pu, raw0, raw1, out_gain)
+    return mixed, (rows, inverse, kkf, inner, joined, mt, r, states, core)
+
+
+def mixer_backward_scan(place, raw0, raw1, out_gain, kept, dmixed):
+    mt, r, core = kept[5], kept[6], kept[8]
+    return back_scan(place, mt, r, core, raw0, raw1, dmixed, out_gain)
+
+
+def mixer_backward(place, starts, params, raw0, raw1, taps, kept, dstates, dcore, dgate):
+    rows, inverse, kkf, inner, joined, _, _, states, _ = kept
+    return back(
         place, starts, params, raw0, raw1, rows, taps, inverse, kkf, inner, joined, states, dstates, dcore, dgate
     )
-    return draw, dtaps, dparams, dgain
 
 
 from jax.sharding import PartitionSpec as P
 
 LANES = 128
 HALF = 384
+GROUP = 256
 
 
 def exchange_perm(count, shifted, sizes):
@@ -615,12 +630,21 @@
     return lax.ppermute(value, "dp", exchange_perm(8, (dy, dx), (4, 2)))
 
 
-def gather_parts(value, take, cut):
+def after(value, *earlier):
+    return lax.optimization_barrier((value,) + earlier)[0]
+
+
+def gather_turn(value, cut, beside=()):
     first, second = value[:cut], value[cut:]
-    pair = jnp.concatenate([first, take(first, 0, 1)], axis=0)
-    rings = [pair] + [take(pair, k, 0) for k in (1, 2, 3)]
-    column = jnp.concatenate([second] + [take(second, k, 0) for k in (1, 2, 3)], axis=0)
-    return rings, [column, take(column, 0, 1)]
+    arrived = [take_zx(first, 0, 1)] + [take_zx(second, k, 0) for k in (1, 2, 3)]
+    arrived = lax.optimization_barrier(tuple(arrived) + tuple(beside))
+    pair = jnp.concatenate([first, arrived[0]], axis=0)
+    column = jnp.concatenate([second, *arrived[1:4]], axis=0)
+    return lax.optimization_barrier((pair, column))
+
+
+def gather_end(pair, column):
+    return [pair] + [take_zx(pair, k, 0) for k in (1, 2, 3)], [column, take_zx(column, 0, 1)]
 
 
 def take_zx(value, ring, side):
@@ -631,16 +655,6 @@
     return from_dp(value, dy=ring, dx=side)
 
 
-def gather_zx(value):
-    rings, columns = gather_parts(value, take_zx, value.shape[0] * 5 // 8)
-    return jnp.concatenate(rings + columns, axis=0)
-
-
-def gather_dp(value):
-    rings, columns = gather_parts(value, take_yx, value.shape[0] // 2)
-    return jnp.concatenate(rings + columns, axis=0)
-
-
 def wide(value):
     return value.astype(jnp.float32)
 
@@ -649,39 +663,126 @@
     return value.astype(jnp.bfloat16)
 
 
-def reduce_parts(value, take, cut):
-    rows = value.shape[0] // 8
-    rest = rows - cut
-    blocks = [value[2 * cut * k : 2 * cut * (k + 1)] for k in range(4)]
-    near, far = value[8 * cut : 8 * cut + 4 * rest], value[8 * cut + 4 * rest :]
-    summed = wide(blocks[0])
+def sum_rows(pieces, rows):
+    total = wide(pieces[0][rows])
+    for piece in pieces[1:]:
+        total = total + wide(piece[rows])
+    return total
+
+
+def reduce_arrivals(rounds, far, beside=()):
+    arrived = [take_zx(rounds[k - 1], -k, 0) for k in (1, 2, 3)] + [take_zx(far, 0, 1)]
+    return lax.optimization_barrier(tuple(arrived) + tuple(beside))[:4]
+
+
+def turn_sum_kernel(*refs):
+    rounds, sides, outs = refs[:4], refs[4:6], refs[6:]
+    cut = rounds[0].shape[0] // 2
+    early, late = slice(0, cut), slice(cut, None)
+    total = wide(rounds[0][...])
+    for ref in rounds[1:]:
+        total = total + wide(ref[...])
+    outs[0][...] = total[early]
+    outs[1][...] = narrow(total[late])
+    total = wide(sides[0][...]) + wide(sides[1][...])
+    rest = total.shape[0] // 4
+    outs[2][...] = total[:rest]
     for k in (1, 2, 3):
-        summed = summed + wide(take(blocks[k], -k, 0))
-    column = wide(near) + wide(take(far, 0, 1))
-    first = (summed[:cut], take(narrow(summed[cut:]), 0, 1))
-    second = (column[:rest],) + tuple(
-        take(narrow(column[rest * k : rest * (k + 1)]), -k, 0) for k in (1, 2, 3)
-    )
-    return first, second
-
-
-def reduce_zx(value):
-    first, second = reduce_parts(value, take_zx, value.shape[0] // 8 * 5 // 8)
-    return first + second
-
-
-def reduce_dp(value):
-    first, second = reduce_parts(value, take_yx, value.shape[0] // 16)
-    return jnp.concatenate(
-        [first[0] + wide(first[1]), second[0] + wide(second[1]) + wide(second[2]) + wide(second[3])], axis=0
-    )
-
-
-def ring_sum(value, take, position):
-    pieces = [value] + [take(value, k, 0) for k in (1, 2, 3)]
-    stacked = jnp.stack(pieces + pieces)
-    ordered = lax.dynamic_slice_in_dim(stacked, (4 - position) % 4, 4, 0)
-    return (ordered[0] + ordered[1]) + (ordered[2] + ordered[3])
+        outs[2 + k][...] = narrow(total[rest * k : rest * (k + 1)])
+
+
+def reduce_parts(first, near, arrived):
+    width = first.shape[1]
+    cut, rest = (first.shape[0] // 2, width), (near.shape[0] // 4, width)
+    outs = [shaped(cut), shaped(cut, jnp.bfloat16), shaped(rest)] + [shaped(rest, jnp.bfloat16)] * 3
+    return whole_call(turn_sum_kernel, outs, "turn_sum", (), first, *arrived[:3], near, arrived[3])
+
+
+def side_sum_kernel(near_ref, crossed_ref, *out_refs):
+    for k, out_ref in enumerate(out_refs):
+        for half in range(2):
+            rows = slice(ROWS_A * (4 * half + k), ROWS_A * (4 * half + k + 1))
+            total = wide(near_ref[rows]) + wide(crossed_ref[rows])
+            out_ref[ROWS_A * half : ROWS_A * (half + 1)] = total if k == 0 else narrow(total)
+
+
+def ring_sum_kernel(over_ref, *refs):
+    arrived, (kept_ref, sent_ref) = refs[:4], refs[4:]
+    half = kept_ref.shape[0]
+    for target, side in ((kept_ref, over_ref[0]), (sent_ref, 1 - over_ref[0])):
+        rows = pl.ds(pl.multiple_of(side * half, 16), half)
+        total = wide(arrived[0][rows])
+        for ref in arrived[1:]:
+            total = total + wide(ref[rows])
+        target[...] = total.astype(target.dtype)
+
+
+def reduce_end(parts):
+    return (parts[0], take_zx(parts[1], 0, 1), parts[2]) + tuple(
+        take_zx(parts[2 + k], -k, 0) for k in (1, 2, 3)
+    )
+
+
+RINGS = [[0, 2, 4, 6], [1, 3, 5, 7]]
+
+
+def spread_kernel(over_ref, *refs):
+    over, out_ref = over_ref[0], refs[-1]
+    count = (len(refs) - 1) // 2
+    for place in range(count):
+        lanes = slice(place * HALF, (place + 1) * HALF)
+        out_ref[0, over, :, lanes] = refs[place][...]
+        out_ref[0, 1 - over, :, lanes] = refs[count + place][...]
+
+
+def spread_pair(value, mate):
+    rows, columns = value.shape
+    count = columns // HALF
+    blocks = [held((rows, HALF), lambda *_, place=place: (0, place)) for place in range(count)]
+    return pl.pallas_call(
+        spread_kernel,
+        grid_spec=pltpu.PrefetchScalarGridSpec(
+            num_scalar_prefetch=1,
+            grid=(4,),
+            in_specs=blocks * 2,
+            out_specs=pl.BlockSpec((1, 2, rows, columns), lambda turn, *_: (turn, 0, 0, 0)),
+        ),
+        out_shape=shaped((4, 2, rows, columns), value.dtype),
+        compiler_params=pltpu.CompilerParams(vmem_limit_bytes=VMEM_MAX),
+        cost_estimate=spends(3),
+        name="spread_pair",
+    )((lax.axis_index("dp") % 2)[None].astype(jnp.int32), *[value] * count, *[mate] * count)
+
+
+def round_ring(spread):
+    everything = lax.all_to_all(spread, "dp", 0, 0, tiled=False, axis_index_groups=RINGS)
+    return everything.reshape(8 * spread.shape[2], spread.shape[3])
+
+
+def ring_blocks(value):
+    up = lax.axis_index("dp") // 2
+    rows = value.shape[0] // 4
+    blocks = [lax.dynamic_slice_in_dim(value, (up + k) % 4 * rows, rows, 0) for k in range(4)]
+    return lax.optimization_barrier(tuple(blocks))
+
+
+def ring_arrivals(blocks):
+    return [blocks[0]] + [take_yx(blocks[k], -k, 0) for k in (1, 2, 3)]
+
+
+def ring_parts(arrived):
+    over = (lax.axis_index("dp") % 2)[None].astype(jnp.int32)
+    half = (arrived[0].shape[0] // 2, arrived[0].shape[1])
+    return whole_call(ring_sum_kernel, [shaped(half), shaped(half, jnp.bfloat16)], "ring_sum", (over,), *arrived)
+
+
+def exchange_ring(value):
+    return lax.all_to_all(value, "dp", 0, 0, tiled=False, axis_index_groups=RINGS)
+
+
+def sum_all(value, axis, count):
+    spread = jnp.broadcast_to(value, (count,) + value.shape)
+    return jnp.sum(lax.all_to_all(spread, axis, 0, 0, tiled=False), axis=0)
 
 
 def whole_call(kernel, out_shape, name, scalars, *arrays, scratch=()):
@@ -697,16 +798,9 @@
         ),
         out_shape=list(outs),
         compiler_params=pltpu.CompilerParams(vmem_limit_bytes=VMEM_MAX),
+        cost_estimate=spends(3),
         name=name,
     )(*scalars, *arrays)
-
-
-def block_lanes(position):
-    return slice(position * LANES, (position + 1) * LANES)
-
-
-def placed_lanes(order_ref, position):
-    return pl.ds(pl.multiple_of(order_ref[position] * LANES, LANES), LANES)
 
 
 def rms_parts(values):
@@ -719,18 +813,171 @@
     return scale * (inner - unit * jnp.mean(inner * unit, axis=-1, keepdims=True))
 
 
-def enter_kernel(order_ref, tokens_ref, cot_ref, gains_ref, normed_ref, rows_ref, grad_ref, gains_out_ref):
-    for position in range(16):
-        here, there = block_lanes(position), placed_lanes(order_ref, position)
-        rows_ref[:, here] = tokens_ref[:, there]
-        grad_ref[:, here] = cot_ref[:, there]
-        gains_out_ref[:, here] = gains_ref[:, there]
-    _, unit = rms_parts(wide(rows_ref[...]))
-    normed_ref[...] = narrow(unit * gains_out_ref[0:1])
-
-
-def attn_kernel(heads_ref, mixed_ref, first0_ref, first1_ref, second0_ref, second1_ref, rows_ref, gains_ref,
-                resid_ref, normed_ref, total_ref):
+def enter_kernel(tokens_ref, gain_ref, normed_ref):
+    _, unit = rms_parts(wide(tokens_ref[...]))
+    normed_ref[...] = narrow(unit * gain_ref[...])
+
+
+def project_kernel(own_ref, other_ref, weights_ref, own_out_ref, other_out_ref):
+    step = pl.program_id(0)
+    half = pl.num_programs(0) // 2
+
+    @pl.when(step < half)
+    def _():
+        own_out_ref[...] = plain_product(own_ref[...], weights_ref[...])
+
+    @pl.when(step >= half)
+    def _():
+        other_out_ref[...] = plain_product(other_ref[...], weights_ref[...])
+
+
+def project(own, other, weights, columns):
+    count, width = own.shape
+    step = 512
+    half = count // step
+
+    def early(size):
+        return pl.BlockSpec((step, size), lambda i: (jnp.minimum(i, half - 1), 0))
+
+    def late(size):
+        return pl.BlockSpec((step, size), lambda i: (jnp.maximum(i - half, 0), 0))
+
+    return pl.pallas_call(
+        project_kernel,
+        grid=(2 * half,),
+        in_specs=[early(width), late(width), held((width, columns))],
+        out_specs=[early(columns), late(columns)],
+        out_shape=[shaped((count, columns))] * 2,
+        compiler_params=pltpu.CompilerParams(vmem_limit_bytes=VMEM_MAX),
+        cost_estimate=spends(5),
+        name="project",
+    )(own, other, weights)
+
+
+def unproject_kernel(own_ref, far_ref, weights_ref, far_weights_ref, *piece_refs):
+    step = pl.program_id(0)
+    total = against(own_rows(own_ref, step), weights_ref[...]) + against(
+        own_rows(far_ref, step), far_weights_ref[...]
+    )
+    put_pieces(narrow(total), piece_refs, step)
+
+
+def unproject(own, far, weights, far_weights, piece_shapes):
+    used = held((weights.shape[0], own.shape[1]))
+    return pl.pallas_call(
+        unproject_kernel,
+        grid=(4,),
+        in_specs=[held(own.shape), held(far.shape), used, used],
+        out_specs=[whole(shape) for shape in piece_shapes],
+        out_shape=[shaped(shape, jnp.bfloat16) for shape in piece_shapes],
+        compiler_params=pltpu.CompilerParams(vmem_limit_bytes=VMEM_MAX),
+        cost_estimate=spends(8),
+        name="unproject",
+    )(own, far, weights, far_weights)
+
+
+def feed_grad_kernel(*refs):
+    own_ref, far_ref = refs[8:]
+    gate_up, down = 0.0, 0.0
+    for normed_ref, cot_ref, dpre_ref, hidden_ref in (refs[:4], refs[4:8]):
+        gate_up = gate_up + over_rows(normed_ref[...], dpre_ref[...])
+        down = down + over_rows(cot_ref[...], hidden_ref[...])
+    gate_up, down = narrow(gate_up), narrow(down)
+    own_ref[:, : 2 * HALF] = gate_up[:, : 2 * HALF]
+    far_ref[:, : 2 * HALF] = gate_up[:, 2 * HALF :]
+    own_ref[:, 2 * HALF :] = down[:, :HALF]
+    far_ref[:, 2 * HALF :] = down[:, HALF:]
+
+
+def feed_grads(*parts):
+    arrays, specs = [], []
+    width = parts[0][2].shape[1]
+    for hidden, dpre, normed, cot in parts:
+        rows = pl.BlockSpec((normed.shape[0], GROUP), lambda i: (0, i))
+        arrays += [normed, cot, dpre, hidden]
+        specs += [rows, rows, held(dpre.shape), held(hidden.shape)]
+    out = pl.BlockSpec((GROUP, 3 * HALF), lambda i: (i, 0))
+    return pl.pallas_call(
+        feed_grad_kernel,
+        grid=(width // GROUP,),
+        in_specs=specs,
+        out_specs=[out, out],
+        out_shape=[shaped((width, 3 * HALF), jnp.bfloat16)] * 2,
+        compiler_params=pltpu.CompilerParams(vmem_limit_bytes=VMEM_MAX),
+        cost_estimate=spends(12),
+        name="feed_grads",
+    )(*arrays)
+
+
+def in_grad_kernel(own_ref, other_ref, draw0_ref, draw1_ref, weights_ref, gain_ref, out_ref, part_ref):
+    grad = narrow(over_rows(own_ref[...], draw0_ref[...]) + over_rows(other_ref[...], draw1_ref[...]))
+    out_ref[0] = grad
+    product = wide(grad) * wide(weights_ref[...])
+    lanes = product[:, :LANES]
+    for start in range(LANES, product.shape[1], LANES):
+        lanes = lanes + product[:, start : start + LANES]
+    part = jnp.sum(jnp.transpose(lanes), axis=0, keepdims=True) / gain_ref[...]
+    part_ref[0] = jnp.broadcast_to(part, part_ref.shape[1:])
+
+
+def in_grads(own, other, draw0, draw1, weights, gain):
+    count, width = own.shape
+    used = draw0.shape[1]
+    rows = pl.BlockSpec((count, GROUP), lambda i: (0, i))
+    grad, part = pl.pallas_call(
+        in_grad_kernel,
+        grid=(width // GROUP,),
+        in_specs=[rows, rows, held(draw0.shape), held(draw1.shape),
+                  pl.BlockSpec((GROUP, used), lambda i: (i, 0)), pl.BlockSpec((1, GROUP), lambda i: (0, i))],
+        out_specs=[pl.BlockSpec((1, GROUP, used), lambda i: (i // 2, i % 2, 0)),
+                   pl.BlockSpec((1, 8, GROUP), lambda i: (i, 0, 0))],
+        out_shape=[shaped((4, 2 * GROUP, used), jnp.bfloat16), shaped((width // GROUP, 8, GROUP))],
+        compiler_params=pltpu.CompilerParams(vmem_limit_bytes=VMEM_MAX),
+        cost_estimate=spends(8),
+        name="in_grads",
+    )(own, other, draw0, draw1, weights, gain)
+    return grad, part[:, 0]
+
+
+def out_grad_kernel(rows_ref, mixed_ref, out_ref):
+    out_ref[0] = narrow(over_rows(rows_ref[...], mixed_ref[...]))
+
+
+def out_grads(rows, mixed):
+    count, width = rows.shape
+    return pl.pallas_call(
+        out_grad_kernel,
+        grid=(width // GROUP,),
+        in_specs=[pl.BlockSpec((count, GROUP), lambda i: (0, i)), held(mixed.shape)],
+        out_specs=pl.BlockSpec((1, GROUP, mixed.shape[1]), lambda i: (i, 0, 0)),
+        out_shape=shaped((width // GROUP, GROUP, mixed.shape[1]), jnp.bfloat16),
+        compiler_params=pltpu.CompilerParams(vmem_limit_bytes=VMEM_MAX),
+        cost_estimate=spends(6),
+        name="out_grads",
+    )(rows, mixed)
+
+
+def own_rows(ref, step):
+    first = pl.ds(pl.multiple_of(step * 2 * ROWS_A, 16), 2 * ROWS_A)
+    near = pl.ds(pl.multiple_of(8 * ROWS_A + step * ROWS_B, 16), ROWS_B)
+    far = pl.ds(pl.multiple_of(8 * ROWS_A + 4 * ROWS_B + step * ROWS_B, 16), ROWS_B)
+    return jnp.concatenate([ref[first], ref[near], ref[far]], axis=0)
+
+
+def put_pieces(total, piece_refs, step):
+    side = pl.ds(pl.multiple_of(step * ROWS_B, 16), ROWS_B)
+    for k in range(4):
+
+        @pl.when(step == k)
+        def _(k=k):
+            piece_refs[k][...] = total[: 2 * ROWS_A]
+
+    piece_refs[4][side] = total[2 * ROWS_A : 2 * ROWS_A + ROWS_B]
+    piece_refs[5][side] = total[2 * ROWS_A + ROWS_B :]
+
+
+def attn_kernel(heads_ref, mixed_ref, *refs):
+    weight_refs, (rows_ref, gain_ref, resid_ref, normed_ref, total_ref) = refs[:4], refs[4:]
     step = pl.program_id(0)
 
     @pl.when(step == 0)
@@ -738,42 +985,41 @@
         total_ref[...] = wide(rows_ref[...])
 
     pair = jnp.concatenate([mixed_ref[heads_ref[0, step]], mixed_ref[heads_ref[1, step]]], axis=1)
-    cut = first0_ref.shape[0]
-    weights = jnp.concatenate([first0_ref[...], first1_ref[...]], axis=1)
-    total_ref[:, :cut] += against(pair, weights)
-    weights = jnp.concatenate([second0_ref[...], second1_ref[...]], axis=1)
-    total_ref[:, cut:] += against(pair, weights)
+    cut = weight_refs[0].shape[0]
+    total_ref[:, :cut] += against(pair, jnp.concatenate([weight_refs[0][...], weight_refs[1][...]], axis=1))
+    total_ref[:, cut:] += against(pair, jnp.concatenate([weight_refs[2][...], weight_refs[3][...]], axis=1))
 
     @pl.when(step == pl.num_programs(0) - 1)
     def _():
         resid = total_ref[...]
         resid_ref[...] = resid
         _, unit = rms_parts(resid)
-        normed_ref[...] = narrow(unit * gains_ref[1:2])
-
-
-def out_weight_specs(cut, rest):
-    first = pl.BlockSpec((cut, LANES), lambda step, *_: (step, 0))
-    second = pl.BlockSpec((rest, LANES), lambda step, *_: (step % 2 * 4 + step // 2, 0))
+        normed_ref[...] = narrow(unit * gain_ref[...])
+
+
+def out_weight_specs(out_parts):
+    rows = out_parts[0].shape[0] // 16
+    first = pl.BlockSpec((rows, LANES), lambda step, *_: (step % 4 * 2 + step // 4, 0))
+    second = pl.BlockSpec((rows, LANES), lambda step, *_: (8 + step, 0))
     return [first, first, second, second]
 
 
-def attend(heads, received, out_parts, rows, gains):
-    cut, rest = out_parts[0].shape[0] // 8, out_parts[2].shape[0] // 8
+def attend(heads, received, out_parts, rows, gain):
     shape = rows.shape
     return pl.pallas_call(
         attn_kernel,
         grid_spec=pltpu.PrefetchScalarGridSpec(
             num_scalar_prefetch=1,
             grid=(8,),
-            in_specs=[whole(received.shape)] + out_weight_specs(cut, rest) + [whole(shape), whole(gains.shape)],
+            in_specs=[whole(received.shape)] + out_weight_specs(out_parts) + [whole(shape), whole(gain.shape)],
             out_specs=[whole(shape), whole(shape)],
             scratch_shapes=[pltpu.VMEM(shape, jnp.float32)],
         ),
         out_shape=[shaped(shape), shaped(shape, jnp.bfloat16)],
         compiler_params=pltpu.CompilerParams(vmem_limit_bytes=VMEM_MAX),
+        cost_estimate=spends(10),
         name="attend",
-    )(heads, received, *out_parts, rows, gains)
+    )(heads, received, *out_parts, *out_parts, rows, gain)
 
 
 def total_of(refs):
@@ -783,7 +1029,7 @@
 
 
 def middle_kernel(heads_ref, *refs):
-    pieces, (resid_ref, cot_ref, gains_ref, first0_ref, first1_ref, second0_ref, second1_ref) = refs[:6], refs[6:13]
+    pieces, (resid_ref, cot_ref, gain_ref), weight_refs = refs[:6], refs[6:9], refs[9:13]
     dresid_ref, dattn_ref, dgain_ref, dmixed_ref = refs[13:]
     step = pl.program_id(0)
 
@@ -792,22 +1038,21 @@
         grad = total_of(pieces)
         scale, unit = rms_parts(resid_ref[...])
         dgain_ref[...] = jnp.sum(grad * unit, axis=0, keepdims=True)
-        dresid = wide(cot_ref[...]) + rms_back(grad, gains_ref[1:2], scale, unit)
+        dresid = wide(cot_ref[...]) + rms_back(grad, gain_ref[...], scale, unit)
         dresid_ref[...] = dresid
         dattn_ref[...] = narrow(dresid)
 
-    cut = first0_ref.shape[0]
+    cut = weight_refs[0].shape[0]
     dattn = dattn_ref[...]
-    weights = jnp.concatenate([first0_ref[...], first1_ref[...]], axis=1)
+    weights = jnp.concatenate([weight_refs[0][...], weight_refs[1][...]], axis=1)
     total = plain_product(dattn[:, :cut], weights)
-    weights = jnp.concatenate([second0_ref[...], second1_ref[...]], axis=1)
+    weights = jnp.concatenate([weight_refs[2][...], weight_refs[3][...]], axis=1)
     total = narrow(total + plain_product(dattn[:, cut:], weights))
     dmixed_ref[heads_ref[0, step]] = total[:, :LANES]
     dmixed_ref[heads_ref[1, step]] = total[:, LANES:]
 
 
-def middle(heads, pieces, resid, cot, gains, out_parts):
-    cut, rest = out_parts[0].shape[0] // 8, out_parts[2].shape[0] // 8
+def middle(heads, pieces, resid, cot, gain, out_parts):
     shape = resid.shape
     mixed_shape = (16, shape[0], LANES)
     return pl.pallas_call(
@@ -816,37 +1061,57 @@
             num_scalar_prefetch=1,
             grid=(8,),
             in_specs=[whole(piece.shape) for piece in pieces]
-            + [whole(shape), whole(shape), whole(gains.shape)]
-            + out_weight_specs(cut, rest),
+            + [whole(shape), whole(shape), whole(gain.shape)]
+            + out_weight_specs(out_parts),
             out_specs=[whole(shape), whole(shape), whole((1, shape[1])), whole(mixed_shape)],
         ),
         out_shape=[shaped(shape), shaped(shape, jnp.bfloat16), shaped((1, shape[1])),
                    shaped(mixed_shape, jnp.bfloat16)],
         compiler_params=pltpu.CompilerParams(vmem_limit_bytes=VMEM_MAX),
+        cost_estimate=spends(10),
         name="middle",
-    )(heads, *pieces, resid, cot, gains, *out_parts)
-
-
-def leave_kernel(order_ref, *refs):
-    pieces, (resid_ref, out_ref) = refs[:6], refs[6:]
-    total = narrow(resid_ref[...] + total_of(pieces))
-    for position in range(16):
-        out_ref[:, placed_lanes(order_ref, position)] = total[:, block_lanes(position)]
-
-
-def finish_kernel(order_ref, *refs):
-    pieces, (rows_ref, dresid_ref, gains_ref, out_ref) = refs[:6], refs[6:]
+    )(heads, *pieces, resid, cot, gain, *out_parts, *out_parts)
+
+
+def leave_kernel(*refs):
+    total = refs[0][...] + refs[4][...]
+    for ref in refs[1:4]:
+        total = total + wide(ref[...])
+    refs[5][...] = narrow(total)
+
+
+def finish_kernel(*refs):
+    pieces, (rows_ref, dresid_ref, gain_ref, out_ref) = refs[:6], refs[6:]
     scale, unit = rms_parts(wide(rows_ref[...]))
-    total = dresid_ref[...] + rms_back(total_of(pieces), gains_ref[0:1], scale, unit)
-    for position in range(16):
-        out_ref[:, placed_lanes(order_ref, position)] = total[:, block_lanes(position)]
-
-
-def feed_kernel(normed_ref, cot_ref, gu0_ref, down0_ref, gu1_ref, down1_ref,
-                out_ref, dnormed_ref, hidden_ref, dpre_ref):
-    normed, cot = normed_ref[...], cot_ref[...]
+    out_ref[...] = dresid_ref[...] + rms_back(total_of(pieces), gain_ref[...], scale, unit)
+
+
+def feed_kernel(halves, count, joins, heads_ref, *refs):
+    normed_refs, refs = refs[:count], refs[count:]
+    cot_refs, refs = refs[: len(halves)], refs[len(halves) :]
+    weight_refs, refs = refs[:4], refs[4:]
+    earlier_refs, refs = refs[: 2 * joins], refs[2 * joins :]
+    fed_refs, dnormed_refs, refs = refs[:2], refs[2 : 2 + count], refs[2 + count :]
+    hidden_ref, dpre_ref, normed_out_ref, cot_out_ref, normed_ref, cot_ref, out_ref, grad_ref = refs
+    step, last = pl.program_id(0), pl.num_programs(0) - 1
+    size = hidden_ref.shape[0]
+
+    @pl.when(step == 0)
+    def _():
+        start = 0
+        for ref in normed_refs:
+            normed_ref[start : start + ref.shape[0]] = ref[...]
+            start += ref.shape[0]
+        for place, ref in enumerate(cot_refs):
+            cot_ref[ROWS_A * place : ROWS_A * (place + 1)] = ref[...]
+
+    rows = pl.ds(pl.multiple_of(step * size, 16), size)
+    normed, cot = normed_ref[rows], cot_ref[rows]
+    normed_out_ref[...] = normed
+    cot_out_ref[...] = cot
     out, dnormed = 0.0, 0.0
-    for half, (gu_ref, down_ref) in enumerate(((gu0_ref, down0_ref), (gu1_ref, down1_ref))):
+    for half in range(2):
+        gu_ref, down_ref = weight_refs[2 * half], weight_refs[2 * half + 1]
         pre = plain_product(normed, gu_ref[...])
         gate, up = pre[:, :HALF], pre[:, HALF:]
         dhidden = plain_product(cot, down_ref[...])
@@ -859,27 +1124,94 @@
         dpre_ref[:, 2 * half * HALF : 2 * (half + 1) * HALF] = dpre
         out = out + against(hidden, down_ref[...])
         dnormed = dnormed + against(dpre, gu_ref[...])
-    out_ref[...] = narrow(out)
-    dnormed_ref[...] = narrow(dnormed)
-
-
-def feed(normed, cot, own, other):
-    rows, width = normed.shape
-    step = 256
-    row_block = pl.BlockSpec((step, width), lambda i: (i, 0))
-    gate_up = pl.BlockSpec((width, 2 * HALF), lambda i: (0, 0))
-    down = pl.BlockSpec((width, HALF), lambda i: (0, 2))
+    out_ref[rows] = narrow(out)
+    grad_ref[rows] = narrow(dnormed)
+
+    @pl.when(step == last)
+    def _():
+        start = 0
+        for ref in dnormed_refs:
+            ref[...] = grad_ref[start : start + ref.shape[0]]
+            start += ref.shape[0]
+        if joins:
+            near_ref, far_ref = fed_refs
+            near_ref[:ROWS_A] = earlier_refs[0][:ROWS_A]
+            far_ref[:ROWS_A] = earlier_refs[0][ROWS_A:]
+            for k in (1, 2, 3):
+                base = 2 * ROWS_A * (k - 1)
+                near_ref[ROWS_A * k : ROWS_A * (k + 1)] = out_ref[base : base + ROWS_A]
+                far_ref[ROWS_A * k : ROWS_A * (k + 1)] = out_ref[base + ROWS_A : base + 2 * ROWS_A]
+            near_ref[4 * ROWS_A :] = earlier_refs[1][...]
+            far_ref[4 * ROWS_A :] = out_ref[6 * ROWS_A :]
+        else:
+            fed_refs[0][...] = out_ref[: 2 * ROWS_A]
+            fed_refs[1][...] = out_ref[2 * ROWS_A :]
+
+
+def held(shape, place=None):
+    place = place or (lambda *_: (0,) * len(shape))
+    return pl.BlockSpec(shape, place, pipeline_mode=pl.Buffered(1))
+
+
+def feed(heads, pieces, halves, cot, own, other, steps, earlier=()):
+    width = cot.shape[1]
+    shapes = [piece.shape for piece in pieces]
+    count = sum(shape[0] for shape in shapes)
+    size = count // steps
+    gate_up = held((width, 2 * HALF))
+    down = held((width, HALF), lambda *_: (0, 2))
+
+    def half_block(slot, half):
+        return held((ROWS_A, width), lambda i, heads_ref: (2 * heads_ref[0, slot] + half, 0))
+
+    fed_shapes = [(8 * ROWS_A, width)] * 2 if earlier else shapes
+    row_widths = (2 * HALF, 4 * HALF, width, width)
+    outs = pl.pallas_call(
+        partial(feed_kernel, tuple(halves), len(pieces), bool(earlier)),
+        grid_spec=pltpu.PrefetchScalarGridSpec(
+            num_scalar_prefetch=1,
+            grid=(steps,),
+            in_specs=[held(shape) for shape in shapes]
+            + [half_block(*half) for half in halves]
+            + [gate_up, down, gate_up, down]
+            + [held(piece.shape) for piece in earlier],
+            out_specs=[whole(shape) for shape in fed_shapes + shapes]
+            + [pl.BlockSpec((size, part), lambda i, *_: (i, 0)) for part in row_widths],
+            scratch_shapes=[pltpu.VMEM((count, width), jnp.bfloat16)] * 4,
+        ),
+        out_shape=[shaped(shape, jnp.bfloat16) for shape in fed_shapes + shapes]
+        + [shaped((count, part), jnp.bfloat16) for part in row_widths],
+        compiler_params=pltpu.CompilerParams(vmem_limit_bytes=VMEM_MAX),
+        cost_estimate=spends(28),
+        name="feed",
+    )(heads, *pieces, *[cot] * len(halves), own, own, other, other, *earlier)
+    return outs[:2], outs[2 : 2 + len(shapes)], outs[2 + len(shapes) :]
+
+
+def join_kernel(*refs):
+    sources, target, sems = refs[:-2], refs[-2], refs[-1]
+    copies, start = [], 0
+    for place, ref in enumerate(sources):
+        copies.append(pltpu.make_async_copy(ref, target.at[pl.ds(start, ref.shape[0])], sems.at[place]))
+        copies[-1].start()
+        start += ref.shape[0]
+    for copy in copies:
+        copy.wait()
+
+
+def join(pieces):
+    anywhere = pl.BlockSpec(memory_space=pl.ANY)
+    rows = sum(piece.shape[0] for piece in pieces)
     return pl.pallas_call(
-        feed_kernel,
-        grid=(rows // step,),
-        in_specs=[row_block, row_block, gate_up, down, gate_up, down],
-        out_specs=[row_block, row_block, pl.BlockSpec((step, 2 * HALF), lambda i: (i, 0)),
-                   pl.BlockSpec((step, 4 * HALF), lambda i: (i, 0))],
-        out_shape=[shaped((rows, width), jnp.bfloat16), shaped((rows, width), jnp.bfloat16),
-                   shaped((rows, 2 * HALF), jnp.bfloat16), shaped((rows, 4 * HALF), jnp.bfloat16)],
+        join_kernel,
+        in_specs=[anywhere] * len(pieces),
+        out_specs=pl.BlockSpec(memory_space=pltpu.VMEM),
+        out_shape=shaped((rows, pieces[0].shape[1]), pieces[0].dtype),
+        scratch_shapes=[pltpu.SemaphoreType.DMA((len(pieces),))],
         compiler_params=pltpu.CompilerParams(vmem_limit_bytes=VMEM_MAX),
-        name="feed",
-    )(normed, cot, own, own, other, other)
+        cost_estimate=spends(3),
+        name="join",
+    )(*pieces)
 
 
 def plain_product(left, right):
@@ -895,19 +1227,15 @@
 
 
 def tables():
-    head, group = lax.axis_index("head"), lax.axis_index("dp")
+    head = lax.axis_index("head")
     ring, side, core = head // 4, head // 2 % 2, head % 2
     chunk = jnp.arange(16, dtype=jnp.int32)
     dz, dx, dc = (chunk // 4 - ring) % 4, (chunk // 2 + side) % 2, (chunk + core) % 2
     place = jnp.stack([ROWS_A * (2 * dz + dx), 8 * ROWS_A + ROWS_B * (4 * dx + dz), dc]).astype(jnp.int32)
     step = jnp.arange(8, dtype=jnp.int32)
-    chip = ((step // 2 + ring) % 4) * 2 + (step + side) % 2
+    chip = ((step + ring) % 4) * 2 + (step // 4 + side) % 2
     heads = jnp.stack([2 * chip + core, 2 * chip + 1 - core]).astype(jnp.int32)
-    up, over = group // 2, group % 2
-    early = ((step // 2 + up) % 4) * 2 + (step + over) % 2
-    late = ((step + up) % 4) * 2 + (step // 4 + over) % 2
-    order = jnp.concatenate([2 * early, 2 * late + 1]).astype(jnp.int32)
-    return place, heads, order
+    return place, heads
 
 
 def body(
@@ -929,84 +1257,113 @@
     up_weight,
     down_weight,
 ):
-    place, heads, order = tables()
-    core = lax.axis_index("head") % 2
+    place, heads = tables()
     starts = document_starts(doc_spans[0], 32)
     out_gain_row = out_gain[None, :]
+    gain1_row, gain2_row = norm1_gain[None, :], norm2_gain[None, :]
     rows_shape = tokens.shape
-
-    pad = lambda weight, columns: jnp.pad(weight, ((0, 0), (0, columns - weight.shape[1])))
-    pack_one = jnp.concatenate(
-        [q_weight, k_weight, v_weight, gate_out_weight, pad(decay_weight[:, 0], LANES), out_weight], axis=1
-    )
-    pack_two = jnp.concatenate([pad(gate_weight, HALF), pad(up_weight, HALF), pad(down_weight, HALF)], axis=1)
-    taps = wide(lax.all_gather(conv_weight, "dp", axis=2, tiled=True))
-
-    normed1, rows, cot, gains = whole_call(
-        enter_kernel,
-        [shaped(rows_shape, jnp.bfloat16)] * 3 + [shaped((2, rows_shape[1]))],
-        "enter",
-        (order,),
-        tokens,
-        cotangent,
-        jnp.stack([norm1_gain, norm2_gain]),
-    )
-    mine_one = gather_dp(pack_one)
-    weights_in = mine_one[:, : 5 * LANES]
-    normed1_own = gather_zx(normed1)
+    width = rows_shape[1]
+
+    def pad(weight, columns):
+        return jnp.pad(weight, ((0, 0), (0, columns - weight.shape[1])))
+
+    (normed1,) = whole_call(enter_kernel, shaped(rows_shape, jnp.bfloat16), "enter", (), tokens, gain1_row)
+
+    packed = (conv_weight, decay_weight, q_weight, k_weight, v_weight, gate_out_weight, out_weight)
+    conv_now, decay_now, *square_now = lax.optimization_barrier(packed + (normed1,))[:7]
+    taps_block = jnp.pad(conv_now.reshape(12, 16), ((0, GROUP - 12), (0, 0)))
+    side_block = pad(jnp.concatenate([decay_now[:, 0], taps_block], axis=1), LANES)
+    pack_one = jnp.concatenate(square_now[:4] + [side_block] + square_now[4:], axis=1)
+    wide_now = lax.optimization_barrier((gate_weight, up_weight, down_weight, normed1))[:3]
+    pack_two = jnp.concatenate([pad(weight, HALF) for weight in wide_now], axis=1)
+    cut, used = pack_one.shape[1], 5 * LANES
+
+    mate_one = take_yx(pack_one, 0, 1)
+    pair, column = gather_turn(normed1, ROWS_A, beside=(mate_one,))
+    pair, column, mate_one = lax.optimization_barrier((pair, column, mate_one))
+    mate_two = take_yx(after(pack_two, mate_one), 0, 1)
+    mine_one = round_ring(spread_pair(pack_one, mate_one))
+    rings, columns = gather_end(pair, column)
+    rings, columns, mine_one, mate_two = lax.optimization_barrier((rings, columns, mine_one, mate_two))
+    spread_two = spread_pair(pack_two, mate_two)
+    normed1_own = join(rings + columns)
     normed1_other = from_head(normed1_own, dc=1)
-    raw0 = plain_product(normed1_own, weights_in)
-    raw1 = plain_product(normed1_other, weights_in)
-
-    weights_other = from_head(weights_in, dc=1)
-    out_rings, out_columns = gather_parts(mine_one[:, 5 * LANES :], take_zx, 1280)
-    out_first, out_second = jnp.concatenate(out_rings, axis=0), jnp.concatenate(out_columns, axis=0)
-    out_parts = (out_first, from_head(out_first, dc=1), out_second, from_head(out_second, dc=1))
-    mine_two = gather_dp(pack_two)
+    raw0, raw1 = project(normed1_own, normed1_other, mine_one, used)
+    taps = mine_one.reshape(8, GROUP, cut)[:, :12, 4 * LANES + 2 : 4 * LANES + 18]
+    taps = wide(taps.transpose(1, 0, 2).reshape(3, 4, LANES))
+
+    mine_two = round_ring(spread_two)
+
+    out_turn = gather_turn(after(mine_one[:, used:], normed1_own), width // 2, beside=(raw0,))
+    raw0, raw1, out_turn = lax.optimization_barrier((raw0, raw1, out_turn))
+    out_rings, out_columns = gather_end(*out_turn)
+    prepared = prepare(place, starts, gate_params, raw0, raw1, taps)
+    mixed, kept = mixer_forward(place, prepared, raw0, raw1, out_gain_row)
+    mixed, mine_two, out_rings, out_columns = lax.optimization_barrier((mixed, mine_two, out_rings, out_columns))
+    cot_group = lax.all_gather(after(cotangent, mixed), "head", axis=0, tiled=True)
+    received = lax.all_to_all(mixed, "head", 0, 0, tiled=False)
+    out_own = join(out_rings + out_columns)
+    out_parts = (out_own, from_head(out_own, dc=1))
     other_two = from_head(mine_two, dc=1)
-    cot_own = gather_zx(cot)
-
-    mixed, stored, kept = mixer_forward(place, starts, gate_params, raw0, raw1, taps, out_gain_row)
-    received = lax.all_to_all(mixed, "head", 0, 0, tiled=False)
-    resid, normed2 = attend(heads, received, out_parts, rows, gains)
-    normed2_own = gather_zx(normed2)
-    fed, dnormed2, hidden, dpre = feed(normed2_own, cot_own, mine_two, other_two)
-
-    dnormed2_pieces = reduce_zx(dnormed2)
-    dresid, dattn, dgain2, dmixed = middle(heads, dnormed2_pieces, resid, cot, gains, out_parts)
+    received, other_two = lax.optimization_barrier((received, other_two))
+    resid, normed2 = attend(heads, received, out_parts, tokens, gain2_row)
+    pair, column = gather_turn(normed2, ROWS_A)
+    rings, columns = gather_end(pair, column)
+    near_halves = [(0, 0), (4, 0)] + [(k, 1) for k in range(4)]
+    far_halves = [half for k in (1, 2, 3) for half in ((k, 0), (4 + k, 0))] + [(4 + k, 1) for k in range(4)]
+    fed_early, (dpair, dnear), kept_near = feed(
+        heads, [pair, column], near_halves, cot_group, mine_two, other_two, 1
+    )
+    rings, columns, dpair = lax.optimization_barrier((rings, columns, dpair))
+    (fed_near, fed_far), (*drings, dfar), kept_far = feed(
+        heads, rings[1:] + columns[1:], far_halves, cot_group, mine_two, other_two, 2, fed_early
+    )
+
+    parts = reduce_parts(dpair, dnear, reduce_arrivals(drings, dfar))
+    feed_own, feed_other = feed_grads(kept_near, kept_far)
+    parts, feed_own, feed_other = lax.optimization_barrier((parts, feed_own, feed_other))
+    feed_grad = narrow(wide(feed_own) + wide(from_head(feed_other, dc=1)))
+    dnormed2_pieces = reduce_end(parts)
+    feed_blocks = ring_blocks(feed_grad)
+    resid_then = after(resid, feed_blocks)
+    feed_blocks = lax.optimization_barrier((feed_blocks, dnormed2_pieces))[0]
+    dresid, dattn, dgain2, dmixed = middle(heads, dnormed2_pieces, resid_then, cotangent, gain2_row, out_parts)
     dmixed_mine = lax.all_to_all(dmixed, "head", 0, 0, tiled=False)
-
-    (block_out,) = whole_call(
-        leave_kernel, shaped(rows_shape, jnp.bfloat16), "leave", (order,), *reduce_zx(fed), resid
-    )
-    gate_up_grad = narrow(over_rows(normed2_own, dpre))
-    down_grad = narrow(over_rows(cot_own, hidden))
-    feed_own = jnp.concatenate([gate_up_grad[:, : 2 * HALF], down_grad[:, :HALF]], axis=1)
-    feed_other = jnp.concatenate([gate_up_grad[:, 2 * HALF :], down_grad[:, HALF:]], axis=1)
-    feed_grad = narrow(wide(feed_own) + wide(from_head(feed_other, dc=1)))
-    feed_total = reduce_dp(feed_grad)
-
-    dattn_own = gather_zx(dattn)
-    mixed_pair = jnp.concatenate([stored[0], from_head(stored[1], dc=1)], axis=1)
-    out_both = narrow(over_rows(dattn_own, mixed_pair))
-    out_grad = narrow(wide(out_both[:, :LANES]) + wide(from_head(out_both[:, LANES:], dc=1)))
-
-    draw, dtaps, dparams, dgain_out = mixer_backward(
-        place, starts, gate_params, raw0, raw1, taps, out_gain_row, kept, dmixed_mine
-    )
-    draw_far = from_head(draw[1], dc=1)
-    dnormed1 = against(draw[0], weights_in) + against(draw_far, weights_other)
-    gain1_part = jnp.sum(dnormed1 * wide(normed1_own), axis=0) / gains[0]
-    dnormed1_pieces = reduce_zx(narrow(dnormed1))
-
-    in_grad = narrow(over_rows(normed1_own, draw[0]) + over_rows(normed1_other, draw[1]))
-    one_total = reduce_dp(jnp.concatenate([in_grad, out_grad], axis=1))
-
-    place_gain = lambda value: value.reshape(16, LANES)[inverse_order(order)]
+    dcore, dstates, dgate, dgain_out = mixer_backward_scan(place, raw0, raw1, out_gain_row, kept, dmixed_mine)
+
+    feed_arrived = ring_arrivals(feed_blocks)
+    fed_crossed = take_zx(after(fed_far, dcore), 0, 1)
+    dattn_group = lax.all_gather(dattn, "head", axis=0, tiled=True)
+    weights_other = from_head(after(mine_one, dmixed), dc=1)
+
+    draw0, draw1, dtaps, dparams = mixer_backward(
+        place, starts, gate_params, raw0, raw1, taps, kept, dstates, dcore, dgate
+    )
+    draw0, draw1, weights_other, feed_arrived = lax.optimization_barrier((draw0, draw1, weights_other, feed_arrived))
+    draw_far = from_head(draw1, dc=1)
+    in_grad, gain1_part = in_grads(normed1_own, normed1_other, draw0, draw1, mine_one, gain1_row)
+    in_arrived = exchange_ring(in_grad)
+    draw_far = after(draw_far, in_grad)
+    dnormed1 = unproject(draw0, draw_far, mine_one, weights_other, [dpair.shape] * 4 + [dnear.shape] * 2)
+    dnormed1, feed_arrived, dattn_then = lax.optimization_barrier((dnormed1, feed_arrived, dattn_group))
+    feed_kept, feed_sent = ring_parts(feed_arrived)
+    out_grad = out_grads(dattn_then, mixed.reshape(dattn_group.shape[0], LANES))
+    arrived = reduce_arrivals(
+        dnormed1[1:4], dnormed1[5], beside=(feed_kept, feed_sent, out_grad, fed_crossed)
+    )
+    dnormed1_pieces = reduce_end(reduce_parts(dnormed1[0], dnormed1[4], arrived))
+    fed_crossed, feed_sent = lax.optimization_barrier((fed_crossed, feed_sent, arrived))[:2]
+    half_rows = (ROWS_A + ROWS_B, width)
+    fed_sums = whole_call(
+        side_sum_kernel, [shaped(half_rows)] + [shaped(half_rows, jnp.bfloat16)] * 3, "side_sum", (), fed_near, fed_crossed
+    )
+    fed_pieces = [fed_sums[0]] + [take_zx(fed_sums[k], -k, 0) for k in (1, 2, 3)]
+    in_kept, in_sent = ring_parts(list(after(in_arrived, *arrived)))
+    one_total = in_kept + wide(take_yx(in_sent, 0, 1))
     small = jnp.concatenate(
         [
-            place_gain(gain1_part),
-            place_gain(dgain2[0]),
+            gain1_part.reshape(16, LANES),
+            dgain2.reshape(16, LANES),
             dgain_out,
             dparams,
             dtaps.reshape(12, LANES),
@@ -1014,12 +1371,20 @@
         ],
         axis=0,
     )
-    small = ring_sum(small, take_yx, lax.axis_index("dp") // 2)
-    small = small + from_dp(small, dx=1)
-    shared = small[:40]
-    shared = ring_sum(shared, take_zx, lax.axis_index("head") // 4)
-    shared = shared + from_head(shared, dx=1)
-    shared = shared + from_head(shared, dc=1)
+    high, rest = split(small)
+    small_rows = jnp.concatenate([high, rest, narrow(small - wide(high) - wide(rest))], axis=0)
+    sent = jnp.concatenate(
+        [out_grad, jnp.broadcast_to(small_rows, (8,) + small_rows.shape)], axis=1
+    )
+    got = lax.all_to_all(after(sent, in_arrived, *arrived), "dp", 0, 0, tiled=False)
+    out_total = jnp.sum(wide(got[:, :GROUP]), axis=0)
+    pieces = wide(got[:, GROUP:]).reshape(8, 3, small.shape[0], LANES)
+    small = jnp.sum(pieces[:, 0] + pieces[:, 1] + pieces[:, 2], axis=0)
+    shared = sum_all(small[:40], "head", 16)
+    fed_pieces, shared = lax.optimization_barrier((fed_pieces, shared))
+    (block_out,) = whole_call(leave_kernel, shaped(rows_shape, jnp.bfloat16), "leave", (), *fed_pieces, resid)
+    feed_total = feed_kept + wide(take_yx(feed_sent, 0, 1))
+
     gain1_total = shared[:16].reshape(-1)
     gain2_total = shared[16:32].reshape(-1)
     out_gain_total = jnp.sum(shared[32:40], axis=0)
@@ -1027,9 +1392,8 @@
     taps_total = lax.dynamic_slice_in_dim(
         small[48:60].reshape(3, 4, LANES), lax.axis_index("dp") * 16, 16, 2
     )
-
     (tokens_grad,) = whole_call(
-        finish_kernel, shaped(rows_shape), "finish", (order,), *dnormed1_pieces, rows, dresid, gains
+        finish_kernel, shaped(rows_shape), "finish", (), *dnormed1_pieces, tokens, dresid, gain1_row
     )
     hidden_units = gate_weight.shape[1]
     return (
@@ -1044,16 +1408,12 @@
         taps_total,
         params_total,
         out_gain_total,
-        one_total[:, 5 * LANES :],
+        out_total,
         gain2_total,
         feed_total[:, :hidden_units],
         feed_total[:, HALF : HALF + hidden_units],
         feed_total[:, 2 * HALF : 2 * HALF + hidden_units],
     )
-
-
-def inverse_order(order):
-    return jnp.argmax(order[None, :] == jnp.arange(16, dtype=jnp.int32)[:, None], axis=1)
 
 
 def solution(mesh):

time: 860 us -> 552 us (0.64)
  waiting for transfers between devices: 327 us -> 140 us
  Pallas kernels: 118 us -> 228 us
  starting transfers between devices: 196 us -> 89.6 us
  local copies, waits for them, and re-layouts: 90.4 us -> 28.9 us
  matrix products: 51.5 us -> 0 us
  other arithmetic: 43.9 us -> 19.6 us
  between operations: 2.28 us -> 15.1 us
    ppermute x78 -> x50, waiting for transfers between devices: 251 us -> 106 us  [from_head(): lax.ppermute(value, 'head', exchange_perm(16, (dz, dx, dc), (4, 2, 2)))]
    pallas_call x1 -> x11, Pallas kernels: 28.2 us -> 123 us  [the longest x2 40.8 us: feed(): pl.pallas_call(partial(feed_kernel, tuple(halves), len(pieces), bool(earl...]
    ppermute x78 -> x50, starting transfers between devices: 134 us -> 45.8 us  [from_head(): lax.ppermute(value, 'head', exchange_perm(16, (dz, dx, dc), (4, 2, 2)))]
    ppermute x36 -> x7, waiting for transfers between devices: 74.5 us -> 10.4 us  [from_dp(): return lax.ppermute(value, 'dp', exchange_perm(8, (dy, dx), (4, 2)))]
    dot_general x9 -> x0, matrix products: 51.5 us -> none  [the longest x5 25.1 us: over_rows(): lax.dot_general(left, right, (((0,), (0,)), ((), ())), preferred_element_...]
    ppermute x36 -> x7, starting transfers between devices: 47.1 us -> 15.1 us  [from_dp(): return lax.ppermute(value, 'dp', exchange_perm(8, (dy, dx), (4, 2)))]
    unnamed x201 -> x80, local copies, waits for them, and re-layouts: 42.3 us -> 11.6 us
    slice x40 -> x9, local copies, waits for them, and re-layouts: 34.8 us -> 4.65 us  [the longest x3 2.86 us: gather_turn(): first, second = (value[:cut], value[cut:])]
  transfers between devices with their start and end apart: 116 -> 65, of which waited for: 46 -> 25; matrix products, arithmetic and copies ran while one was open for 18% -> 6% of each run, Pallas kernels for 10% -> 32%
where the time goes in v2:
time: 552 us; the launch traced here: 542 us
  Pallas kernels  228 us (41%)
  waiting for transfers between devices  140 us (25%)
  starting transfers between devices  89.6 us (16%)
  local copies, waits for them, and re-layouts  28.9 us (5%)
  blocking collectives  21.2 us (4%)
  other arithmetic  19.6 us (4%)
  between operations  15.1 us (3%)
    ppermute x50, waiting for transfers between devices, from_head(): lax.ppermute(value, 'head', exchange_perm(16, (dz, dx, dc), (4, 2, 2)))  106 us
    ppermute x50, starting transfers between devices, from_head(): lax.ppermute(value, 'head', exchange_perm(16, (dz, dx, dc), (4, 2, 2)))  45.8 us
    pallas_call x2, Pallas kernels, feed(): pl.pallas_call(partial(feed_kernel, tuple(halves), len(pieces), bool(earl...  40.8 us
    pallas_call x8, Pallas kernels, whole_call(): pl.pallas_call(kernel, grid_spec=pltpu.PrefetchScalarGridSpec(num_scalar_...  26.6 us
    pallas_call x1, Pallas kernels, back(): pl.pallas_call(back_kernel, grid_spec=pltpu.PrefetchScalarGridSpec(num_sc...  25.2 us
    all_to_all x1, blocking collectives, body(): dmixed_mine = lax.all_to_all(dmixed, 'head', 0, 0, tiled=False)  21.2 us
    pallas_call x1, Pallas kernels, prepare(): pl.pallas_call(prepare_kernel, grid_spec=pltpu.PrefetchScalarGridSpec(num...  18.1 us
    pallas_call x1, Pallas kernels, feed_grads(): pl.pallas_call(feed_grad_kernel, grid=(width // GROUP,), in_specs=specs,...  18 us
  transfers between devices with their start and end apart: 65, of which 25 were waited for; matrix products, arithmetic and copies ran while one was open for 6% of the time, Pallas kernels for 32%

profile of v2, /device:TPU:1, one launch (start us, length us, event | category | flops | bytes accessed | tf_op | source)
XLA Modules:
  0.0 542.1 jit_solution(4605472465944177229)
XLA Ops:
  24.7 9.1 %collective-permute-done.1 = bf16[64,2048]{1,0:T(8,128)(2,1)S(1)} collective-permute-done((bf16[64,2048]{1,0:T(8,128)(2,1)S(1)}, bf16[64,2048]{1,0:T(8,128)(2,1)S(1)}, u32[]{:S(2)}, u32[]{:S(2)}) %collective-permute-start.1) | collective-permute-done | bytes 262176 | tf_op jit(solution)/shard_map/ppermute | solution.py:626
  55.8 10.5 %collective-permute-done.5.refs_1_ = bf16[128,2048]{1,0:T(8,128)(2,1)S(1)} collective-permute-done((bf16[128,2048]{1,0:T(8,128)(2,1)}, bf16[128,2048]{1,0:T(8,128)(2,1)S(1)}, u32[]{:S(2)}, u32[]{:S(2)}) %collective-permute-start.5) | collective-permute-done | bytes 524320 | tf_op jit(solution)/shard_map/ppermute | solution.py:626
  66.9 14.2 %collective-permute-done.7.refs_3_ = bf16[128,2048]{1,0:T(8,128)(2,1)S(1)} collective-permute-done((bf16[128,2048]{1,0:T(8,128)(2,1)}, bf16[128,2048]{1,0:T(8,128)(2,1)S(1)}, u32[]{:S(2)}, u32[]{:S(2)}) %collective-permute-start.7) | collective-permute-done | bytes 524320 | tf_op jit(solution)/shard_map/ppermute | solution.py:626
  104.8 11.9 %project.1 = (f32[1024,640]{1,0:T(8,128)}, f32[1024,640]{1,0:T(8,128)}) custom-call(bf16[1024,2048]{1,0:T(8,128)(2,1)} %join.2.own_ref, bf16[1024,2048]{1,0:T(8,128)(2,1)} %collective-permute-done.10.other_ref, bf16[2048,768]{1,0:T(8,128)(2,1)} %bitcast.35), custom_call_target="tpu_custom_call" | custom-call | flops 5000000 | bytes 1024 | tf_op jit(solution)/shard_map/project/pallas_call | solution.py:845
  129.9 18.1 %prepare.1 = (f32[16,8,128]{2,1,0:T(8,128)}, f32[16,128,128]{2,1,0:T(8,128)}, f32[16,128,128]{2,1,0:T(8,128)}, f32[16,128,128]{2,1,0:T(8,128)}, f32[16,128,256]{...) custom-call(s32[3,16]{1,0:T(4,128)} %pad_add_fusion.place_ref, ...), custom_call_target="tpu_custom_call" | custom-call | flops 18000000 | bytes 1024 | tf_op jit(solution)/shard_map/prepare/pallas_call | solution.py:291
  148.0 7.0 %scan_states.1 = (f32[16,128,128]{2,1,0:T(8,128)}, f32[16,128,128]{2,1,0:T(8,128)}, bf16[16,128,128]{2,1,0:T(8,128)(2,1)}) custom-call(s32[3,16]{1,0:T(4,128)} %pad_add_fusion.place_ref, bf16[16,128,256]{2,1,0:T(8,128)(2,1)} %get-tuple-element.247.m_ref, f32[16,128,128]{2,1,0:T(8,128)} %get-tuple-element.248.b_ref, ...), custom_call_target="tpu_custom_call" | custom-call | flops 7000000 | bytes 1024 | tf_op jit(solution)/shard_map/scan_states/pallas_call | solution.py:339
  167.6 15.4 %all-to-all-done.2.mixed_ref = bf16[16,128,128]{2,1,0:T(8,128)(2,1)} async-done(((bf16[16,128,128]{2,1,0:T(8,128)(2,1)}), bf16[16,128,128]{2,1,0:T(8,128)(2,1)}, u32[]{:S(2)}, u32[]{:S(2)}) %all-to-all-start.2) | async-done | bytes 524320 | tf_op jit(solution)/shard_map/all_to_all | solution.py:1304
  183.0 10.3 %attend.1 = (f32[128,2048]{1,0:T(8,128)}, bf16[128,2048]{1,0:T(8,128)(2,1)}) custom-call(s32[2,8]{1,0:T(2,128)} %pad_add_fusion.1.heads_ref, bf16[16,128,128]{2,1,0:T(8,128)(2,1)} %all-to-all-done.2.mixed_ref, bf16[16384,128]{1,0:T(8,128)(2,1)} %join.3.refs_0_.refs_2_.refs_9_.refs_11_, ...), custom_call_target="tpu_custom_call" | custom-call | flops 10000000 | bytes 1024 | tf_op jit(solution)/shard_map/attend/pallas_call | solution.py:1009
  196.0 12.0 %collective-permute-done.21 = bf16[64,2048]{1,0:T(8,128)(2,1)S(1)} collective-permute-done((bf16[64,2048]{1,0:T(8,128)(2,1)S(1)}, bf16[64,2048]{1,0:T(8,128)(2,1)S(1)}, u32[]{:S(2)}, u32[]{:S(2)}) %collective-permute-start.21) | collective-permute-done | bytes 262176 | tf_op jit(solution)/shard_map/ppermute | solution.py:626
  209.7 8.0 %collective-permute-done.24 = bf16[64,2048]{1,0:T(8,128)(2,1)S(1)} collective-permute-done((bf16[64,2048]{1,0:T(8,128)(2,1)S(1)}, bf16[64,2048]{1,0:T(8,128)(2,1)S(1)}, u32[]{:S(2)}, u32[]{:S(2)}) %collective-permute-start.24) | collective-permute-done | bytes 262176 | tf_op jit(solution)/shard_map/ppermute | solution.py:626
  226.1 15.2 %feed.2 = (bf16[128,2048]{1,0:T(8,128)(2,1)}, bf16[256,2048]{1,0:T(8,128)(2,1)}, bf16[128,2048]{1,0:T(8,128)(2,1)}, bf16[256,2048]{1,0:T(8,128)(2,1)}, bf16[384,...) custom-call(s32[2,8]{1,0:T(2,128)} %pad_add_fusion.1.heads_ref, ...), custom_call_target="tpu_custom_call" | custom-call | flops 28000000 | bytes 1024 | tf_op jit(solution)/shard_map/feed/pallas_call | solution.py:1169
  241.3 10.3 %collective-permute-done.27.refs_2_ = bf16[128,2048]{1,0:T(8,128)(2,1)} collective-permute-done((bf16[128,2048]{1,0:T(8,128)(2,1)}, bf16[128,2048]{1,0:T(8,128)(2,1)}, u32[]{:S(2)}, u32[]{:S(2)}) %collective-permute-start.27) | collective-permute-done | bytes 524320 | tf_op jit(solution)/shard_map/ppermute | solution.py:626
  251.7 25.6 %feed.3 = (bf16[512,2048]{1,0:T(8,128)(2,1)}, bf16[512,2048]{1,0:T(8,128)(2,1)}, bf16[128,2048]{1,0:T(8,128)(2,1)}, bf16[128,2048]{1,0:T(8,128)(2,1)}, bf16[128,...) custom-call(s32[2,8]{1,0:T(2,128)} %pad_add_fusion.1.heads_ref, ...), custom_call_target="tpu_custom_call" | custom-call | flops 28000000 | bytes 1024 | tf_op jit(solution)/shard_map/feed/pallas_call | solution.py:1169
  280.4 18.0 %feed_grads.1 = (bf16[2048,1152]{1,0:T(8,128)(2,1)}, bf16[2048,1152]{1,0:T(8,128)(2,1)}) custom-call(bf16[384,2048]{1,0:T(8,128)(2,1)} %get-tuple-element.300.refs_0_, bf16[384,2048]{1,0:T(8,128)(2,1)} %get-tuple-element.301.refs_1_, bf16[384,1536]{1,0:T(8,128)(2,1)} %get-tuple-element.302.refs_2_, bf16[384,768]{1,0:T(8,128)(2,1)} %get-tuple-element.303.refs_3_, ...), custom_call_target="tpu_custom_call" | custom-call | flops 12000000 | bytes 1024 | tf_op jit(solution)/shard_map/feed_grads/pallas_call | solution.py:900
  328.0 10.6 %middle.1 = (f32[128,2048]{1,0:T(8,128)}, bf16[128,2048]{1,0:T(8,128)(2,1)}, f32[1,2048]{1,0:T(1,128)}, bf16[16,128,128]{2,1,0:T(8,128)(2,1)}) custom-call(s32[2,8]{1,0:T(2,128)} %pad_add_fusion.1.heads_ref, f32[64,2048]{1,0:T(8,128)} %get-tuple-element.310.refs_0_, bf16[64,2048]{1,0:T(8,128)(2,1)} %copy-done.20, f32[64,2048]{1,0:T(8,128)} %get-tuple-element.312.refs_2_, ...), custom_call_target="tpu_custom_call" | custom-call | flops 10000000 | bytes 1024 | tf_op jit(solution)/shard_map/middle/pallas_call | solution.py:1058
  344.3 21.2 %all_to_all.35.dmixed_ref = bf16[16,128,128]{2,1,0:T(8,128)(2,1)} all-to-all(bf16[16,128,128]{2,1,0:T(8,128)(2,1)} %get-tuple-element.324), channel_id=1, replica_groups=mesh['dp'=8,'head'=16] {'head'}, dimensions={0} | all-to-all | bytes 1048576 | tf_op jit(solution)/shard_map/all_to_all | solution.py:1331
  365.5 7.3 %back_scan.1 = (f32[16,128,128]{2,1,0:T(8,128)}, f32[16,128,128]{2,1,0:T(8,128)}, bf16[16,128,128]{2,1,0:T(8,128)(2,1)}, f32[8,128]{1,0:T(8,128)}) custom-call(s32[3,16]{1,0:T(4,128)} %pad_add_fusion.place_ref, bf16[16,128,256]{2,1,0:T(8,128)(2,1)} %get-tuple-element.282.mt_ref, f32[16,128,128]{2,1,0:T(8,128)} %get-tuple-element.249.r_ref, ...), custom_call_target="tpu_custom_call" | custom-call | flops 7000000 | bytes 1024 | tf_op jit(solution)/shard_map/back_scan/pallas_call | solution.py:399
  372.9 25.2 %back.1 = (bf16[1024,640]{1,0:T(8,128)(2,1)}, bf16[1024,640]{1,0:T(8,128)(2,1)}, f32[3,4,128]{2,1,0:T(4,128)}, f32[8,128]{1,0:T(8,128)}) custom-call(s32[3,16]{1,0:T(4,128)} %pad_add_fusion.place_ref, s32[32]{0:T(128)} %or_convert_fusion.starts_ref, f32[2,1]{1,0:T(2,128)} %copy.73.params_ref, f32[1024,640]{1,0:T(8,128)} %get-tuple-element.245.raw0_ref.gate0_ref, ...), custom_call_target="tpu_custom_call" | custom-call | flops 24000000 | bytes 1024 | tf_op jit(solution)/shard_map/back/pallas_call | solution.py:563
  399.2 13.4 %in_grads.1 = (bf16[4,512,640]{2,1,0:T(8,128)(2,1)}, f32[8,8,256]{2,1,0:T(8,128)}) custom-call(bf16[1024,2048]{1,0:T(8,128)(2,1)} %join.2.own_ref, bf16[1024,2048]{1,0:T(8,128)(2,1)} %collective-permute-done.10.other_ref, bf16[1024,640]{1,0:T(8,128)(2,1)} %get-tuple-element.342.draw0_ref.own_ref, bf16[1024,640]{1,0:T(8,128)(2,1)} %get-tuple-element.343.draw1_ref, ...), custom_call_target="tpu_custom_call" | custom-call | flops 8000000 | bytes 1024 | tf_op jit(solution)/shard_map/in_grads/pallas_call | solution.py:927
  416.3 13.1 %unproject.1 = (bf16[128,2048]{1,0:T(8,128)(2,1)}, bf16[128,2048]{1,0:T(8,128)(2,1)}, bf16[128,2048]{1,0:T(8,128)(2,1)}, bf16[128,2048]{1,0:T(8,128)(2,1)}, bf16...) custom-call(bf16[1024,640]{1,0:T(8,128)(2,1)} %get-tuple-element.342.draw0_ref.own_ref, ...), custom_call_target="tpu_custom_call" | custom-call | flops 8000000 | bytes 1024 | tf_op jit(solution)/shard_map/unproject/pallas_call | solution.py:867
  437.9 8.5 %out_grads.1 = bf16[8,256,128]{2,1,0:T(8,128)(2,1)} custom-call(bf16[2048,2048]{1,0:T(8,128)(2,1)} %all-gather.5.cloned.1.call-done.rows_ref, bf16[2048,128]{1,0:T(8,128)(2,1)} %bitcast.40), custom_call_target="tpu_custom_call" | custom-call | flops 6000000 | bytes 1024 | tf_op jit(solution)/shard_map/out_grads/pallas_call | solution.py:948
  446.7 9.2 %collective-permute-done.44.refs_1_ = bf16[128,2048]{1,0:T(8,128)(2,1)S(1)} collective-permute-done((bf16[128,2048]{1,0:T(8,128)(2,1)}, bf16[128,2048]{1,0:T(8,128)(2,1)S(1)}, u32[]{:S(2)}, u32[]{:S(2)}) %collective-permute-start.44) | collective-permute-done | bytes 524320 | tf_op jit(solution)/shard_map/ppermute | solution.py:626
  456.4 12.8 %collective-permute-done.47.refs_5_ = bf16[256,2048]{1,0:T(8,128)(2,1)} collective-permute-done((bf16[256,2048]{1,0:T(8,128)(2,1)}, bf16[256,2048]{1,0:T(8,128)(2,1)}, u32[]{:S(2)}, u32[]{:S(2)}) %collective-permute-start.47) | collective-permute-done | bytes 1048608 | tf_op jit(solution)/shard_map/ppermute | solution.py:626
  515.1 7.8 %all-to-all-start.6 = ((f32[16,40,128]{2,1,0:T(8,128)}), f32[16,40,128]{2,1,0:T(8,128)S(1)}, u32[]{:S(2)}, u32[]{:S(2)}) async-start(f32[16,40,128]{2,1,0:T(8,128)} %broadcast_in_dim.38), calls=%async_computation.6 | async-start | bytes 655360 | tf_op jit(solution)/shard_map/all_to_all | solution.py:785
  (274 shorter events, 212.3 us)
Async XLA Ops:
  43.8 42.1 %all-to-all-start = ((bf16[4,2,256,768]{3,2,1,0:T(8,128)(2,1)}), bf16[4,2,256,768]{3,2,1,0:T(8,128)(2,1)S(1)}, u32[]{:S(2)}, u32[]{:S(2)}) async-start(bf16[4,2,256,768]{3,2,1,0:T(8,128)(2,1)} %spread_pair.2), calls=%async_computation | async-start | bytes 6291456 | tf_op jit(solution)/shard_map/all_to_all | solution.py:758
  48.2 37.8 %collective-permute-start.8 = (bf16[256,2048]{1,0:T(8,128)(2,1)}, bf16[256,2048]{1,0:T(8,128)(2,1)}, u32[]{:S(2)}, u32[]{:S(2)}) collective-permute-start(bf16[256,2048]{1,0:T(8,128)(2,1)} %pad_maximum_fusion.refs_4_), channel_id=1, source_target_pairs={{2,0},{3,1},{0,2},{1,3},{6,4},{7,5},{4,6},{5,7},{10,8},{11,9},{8,1... | collective-permute-start | bytes 3145736 | tf_op jit(solution)/shard_map/ppermute | solution.py:626
  52.5 32.6 %collective-permute-start.9 = (bf16[256,1152]{1,0:T(8,128)(2,1)S(1)}, bf16[256,1152]{1,0:T(8,128)(2,1)S(1)}, u32[]{:S(2)}, u32[]{:S(2)}) collective-permute-start(bf16[256,1152]{1,0:T(8,128)(2,1)S(1)} %fusion.5.refs_0_.refs_1_.refs_2_), channel_id=1, source_target_pairs={{16,0},{0,16},{48,32},{32,48},{80,64},{64,80},{112,96},{96,112},{1... | collective-permute-start | bytes 1769480 | tf_op jit(solution)/shard_map/ppermute | solution.py:630
  97.5 59.7 %all-to-all-start.1 = ((bf16[4,2,256,1152]{3,2,1,0:T(8,128)(2,1)}), bf16[4,2,256,1152]{3,2,1,0:T(8,128)(2,1)}, u32[]{:S(2)}, u32[]{:S(2)}) async-start(bf16[4,2,256,1152]{3,2,1,0:T(8,128)(2,1)} %spread_pair.3), calls=%async_computation.1 | async-start | bytes 9437184 | tf_op jit(solution)/shard_map/all_to_all | solution.py:758
  102.5 123.6 %all-gather.3.cloned.1.call-start = ((), (), s32[]{:S(2)}) async-start(), calls=%async_computation.7 | async-start | bytes 8912896 | tf_op jit(solution)/shard_map/all_gather | solution.py:1303
  123.0 34.2 %collective-permute-start.18 = (bf16[4096,128]{1,0:T(8,128)(2,1)}, bf16[4096,128]{1,0:T(8,128)(2,1)}, u32[]{:S(2)}, u32[]{:S(2)}) collective-permute-start(bf16[4096,128]{1,0:T(8,128)(2,1)} %pad_maximum_fusion.1.refs_4_), channel_id=1, source_target_pairs={{2,0},{3,1},{0,2},{1,3},{6,4},{7,5},{4,6},{5,7},{10,8},{11,9},{8,1... | collective-permute-start | bytes 3145736 | tf_op jit(solution)/shard_map/ppermute | solution.py:626
  125.4 31.8 %collective-permute-start.15 = (bf16[2048,128]{1,0:T(8,128)(2,1)}, bf16[2048,128]{1,0:T(8,128)(2,1)}, u32[]{:S(2)}, u32[]{:S(2)}) collective-permute-start(bf16[2048,128]{1,0:T(8,128)(2,1)} %pad_maximum_fusion.5.refs_0_), channel_id=1, source_target_pairs={{4,0},{5,1},{6,2},{7,3},{8,4},{9,5},{10,6},{11,7},{12,8},{13,9},{1... | collective-permute-start | bytes 1572872 | tf_op jit(solution)/shard_map/ppermute | solution.py:626
  125.9 31.4 %collective-permute-start.16 = (bf16[2048,128]{1,0:T(8,128)(2,1)}, bf16[2048,128]{1,0:T(8,128)(2,1)}, u32[]{:S(2)}, u32[]{:S(2)}) collective-permute-start(bf16[2048,128]{1,0:T(8,128)(2,1)} %pad_maximum_fusion.5.refs_0_), channel_id=1, source_target_pairs={{8,0},{9,1},{10,2},{11,3},{12,4},{13,5},{14,6},{15,7},{0,8},{1,9},... | collective-permute-start | bytes 1572872 | tf_op jit(solution)/shard_map/ppermute | solution.py:626
  127.0 30.2 %collective-permute-start.17 = (bf16[2048,128]{1,0:T(8,128)(2,1)}, bf16[2048,128]{1,0:T(8,128)(2,1)}, u32[]{:S(2)}, u32[]{:S(2)}) collective-permute-start(bf16[2048,128]{1,0:T(8,128)(2,1)} %pad_maximum_fusion.5.refs_0_), channel_id=1, source_target_pairs={{12,0},{13,1},{14,2},{15,3},{0,4},{1,5},{2,6},{3,7},{4,8},{5,9},{6... | collective-permute-start | bytes 1572872 | tf_op jit(solution)/shard_map/ppermute | solution.py:626
  167.0 262.4 %all-gather.5.cloned.1.call-start = ((), (), s32[]{:S(2)}) async-start(), calls=%async_computation.8 | async-start | bytes 8912896 | tf_op jit(solution)/shard_map/all_gather | solution.py:1336
  219.5 32.1 %collective-permute-start.28 = (bf16[256,2048]{1,0:T(8,128)(2,1)}, bf16[256,2048]{1,0:T(8,128)(2,1)}, u32[]{:S(2)}, u32[]{:S(2)}) collective-permute-start(bf16[256,2048]{1,0:T(8,128)(2,1)} %pad_maximum_fusion.2.refs_1_), channel_id=1, source_target_pairs={{2,0},{3,1},{0,2},{1,3},{6,4},{7,5},{4,6},{5,7},{10,8},{11,9},{8,1... | collective-permute-start | bytes 3145736 | tf_op jit(solution)/shard_map/ppermute | solution.py:626
  224.9 26.7 %collective-permute-start.27 = (bf16[128,2048]{1,0:T(8,128)(2,1)}, bf16[128,2048]{1,0:T(8,128)(2,1)}, u32[]{:S(2)}, u32[]{:S(2)}) collective-permute-start(bf16[128,2048]{1,0:T(8,128)(2,1)} %pad_maximum_fusion.6.refs_0_), channel_id=1, source_target_pairs={{12,0},{13,1},{14,2},{15,3},{0,4},{1,5},{2,6},{3,7},{4,8},{5,9},{6... | collective-permute-start | bytes 1572872 | tf_op jit(solution)/shard_map/ppermute | solution.py:626
  338.7 59.5 %collective-permute-start.39 = (bf16[2048,768]{1,0:T(8,128)(2,1)S(1)}, bf16[2048,768]{1,0:T(8,128)(2,1)S(1)}, u32[]{:S(2)}, u32[]{:S(2)}) collective-permute-start(bf16[2048,768]{1,0:T(8,128)(2,1)S(1)} %bitcast.39), channel_id=1, source_target_pairs={{1,0},{0,1},{3,2},{2,3},{5,4},{4,5},{7,6},{6,7},{9,8},{8,9},{11,10... | collective-permute-start | bytes 9437192 | tf_op jit(solution)/shard_map/ppermute | solution.py:626
  339.9 58.2 %collective-permute-start.40 = (bf16[512,1152]{1,0:T(8,128)(2,1)}, bf16[512,1152]{1,0:T(8,128)(2,1)S(1)}, u32[]{:S(2)}, u32[]{:S(2)}) collective-permute-start(bf16[512,1152]{1,0:T(8,128)(2,1)} %get-tuple-element.339), channel_id=1, source_target_pairs={{96,0},{112,16},{0,32},{16,48},{32,64},{48,80},{64,96},{80,112},{9... | collective-permute-start | bytes 3538952 | tf_op jit(solution)/shard_map/ppermute | solution.py:630
  340.7 57.4 %collective-permute-start.41 = (bf16[512,1152]{1,0:T(8,128)(2,1)}, bf16[512,1152]{1,0:T(8,128)(2,1)}, u32[]{:S(2)}, u32[]{:S(2)}) collective-permute-start(bf16[512,1152]{1,0:T(8,128)(2,1)} %get-tuple-element.340), channel_id=1, source_target_pairs={{64,0},{80,16},{96,32},{112,48},{0,64},{16,80},{32,96},{48,112},{6... | collective-permute-start | bytes 3538952 | tf_op jit(solution)/shard_map/ppermute | solution.py:630
  343.1 55.0 %collective-permute-start.42 = (bf16[512,1152]{1,0:T(8,128)(2,1)}, bf16[512,1152]{1,0:T(8,128)(2,1)}, u32[]{:S(2)}, u32[]{:S(2)}) collective-permute-start(bf16[512,1152]{1,0:T(8,128)(2,1)} %get-tuple-element.341), channel_id=1, source_target_pairs={{32,0},{48,16},{64,32},{80,48},{96,64},{112,80},{0,96},{16,112},{3... | collective-permute-start | bytes 3538952 | tf_op jit(solution)/shard_map/ppermute | solution.py:630
  399.2 47.5 %collective-permute-start.38 = (bf16[512,2048]{1,0:T(8,128)(2,1)}, bf16[512,2048]{1,0:T(8,128)(2,1)}, u32[]{:S(2)}, u32[]{:S(2)}) collective-permute-start(bf16[512,2048]{1,0:T(8,128)(2,1)} %get-tuple-element.326), channel_id=1, source_target_pairs={{2,0},{3,1},{0,2},{1,3},{6,4},{7,5},{4,6},{5,7},{10,8},{11,9},{8,1... | collective-permute-start | bytes 6291464 | tf_op jit(solution)/shard_map/ppermute | solution.py:626
  412.6 56.6 %all-to-all-start.4 = ((bf16[4,512,640]{2,1,0:T(8,128)(2,1)}), bf16[4,512,640]{2,1,0:T(8,128)(2,1)S(1)}, u32[]{:S(2)}, u32[]{:S(2)}) async-start(bf16[4,512,640]{2,1,0:T(8,128)(2,1)} %get-tuple-element.344), calls=%async_computation.4 | async-start | bytes 5242880 | tf_op jit(solution)/shard_map/all_to_all | solution.py:780
  429.4 39.8 %collective-permute-start.47 = (bf16[256,2048]{1,0:T(8,128)(2,1)}, bf16[256,2048]{1,0:T(8,128)(2,1)}, u32[]{:S(2)}, u32[]{:S(2)}) collective-permute-start(bf16[256,2048]{1,0:T(8,128)(2,1)} %get-tuple-element.366), channel_id=1, source_target_pairs={{2,0},{3,1},{0,2},{1,3},{6,4},{7,5},{4,6},{5,7},{10,8},{11,9},{8,1... | collective-permute-start | bytes 3145736 | tf_op jit(solution)/shard_map/ppermute | solution.py:626
  473.5 28.2 %collective-permute-start.55 = (bf16[256,640]{1,0:T(8,128)(2,1)}, bf16[256,640]{1,0:T(8,128)(2,1)S(1)}, u32[]{:S(2)}, u32[]{:S(2)}) collective-permute-start(bf16[256,640]{1,0:T(8,128)(2,1)} %get-tuple-element.400), channel_id=1, source_target_pairs={{16,0},{0,16},{48,32},{32,48},{80,64},{64,80},{112,96},{96,112},{1... | collective-permute-start | bytes 983048 | tf_op jit(solution)/shard_map/ppermute | solution.py:630
  483.2 31.0 %all-to-all-start.5 = ((bf16[8,448,128]{2,1,0:T(8,128)(2,1)}), bf16[8,448,128]{2,1,0:T(8,128)(2,1)S(1)}, u32[]{:S(2)}, u32[]{:S(2)}) async-start(bf16[8,448,128]{2,1,0:T(8,128)(2,1)} %pad_maximum_fusion.3), calls=%async_computation.5 | async-start | bytes 1835008 | tf_op jit(solution)/shard_map/all_to_all | solution.py:1379
  493.5 37.1 %collective-permute-start.48 = (bf16[128,2048]{1,0:T(8,128)(2,1)}, bf16[128,2048]{1,0:T(8,128)(2,1)}, u32[]{:S(2)}, u32[]{:S(2)}) collective-permute-start(bf16[128,2048]{1,0:T(8,128)(2,1)} %get-tuple-element.375), channel_id=1, source_target_pairs={{12,0},{13,1},{14,2},{15,3},{0,4},{1,5},{2,6},{3,7},{4,8},{5,9},{6... | collective-permute-start | bytes 1572872 | tf_op jit(solution)/shard_map/ppermute | solution.py:626
  494.0 36.6 %collective-permute-start.49 = (bf16[128,2048]{1,0:T(8,128)(2,1)}, bf16[128,2048]{1,0:T(8,128)(2,1)}, u32[]{:S(2)}, u32[]{:S(2)}) collective-permute-start(bf16[128,2048]{1,0:T(8,128)(2,1)} %get-tuple-element.376), channel_id=1, source_target_pairs={{8,0},{9,1},{10,2},{11,3},{12,4},{13,5},{14,6},{15,7},{0,8},{1,9},... | collective-permute-start | bytes 1572872 | tf_op jit(solution)/shard_map/ppermute | solution.py:626
  495.9 34.7 %collective-permute-start.50 = (bf16[128,2048]{1,0:T(8,128)(2,1)}, bf16[128,2048]{1,0:T(8,128)(2,1)}, u32[]{:S(2)}, u32[]{:S(2)}) collective-permute-start(bf16[128,2048]{1,0:T(8,128)(2,1)} %get-tuple-element.377), channel_id=1, source_target_pairs={{4,0},{5,1},{6,2},{7,3},{8,4},{9,5},{10,6},{11,7},{12,8},{13,9},{1... | collective-permute-start | bytes 1572872 | tf_op jit(solution)/shard_map/ppermute | solution.py:626
  (76 other events, 1031.1 us)
Sparse Core Ops, SparseCore 0:
  157.4 68.6 all-gather.2
  338.8 57.7 all-gather.4

commit v3 on v2

--- a/solution.py
+++ b/solution.py
@@ -8,8 +8,8 @@
 
 CHUNK = 128
 BATCH = 4
-ROWS_A = 64
-ROWS_B = 64
+ROWS_A = 80
+ROWS_B = 48
 GATE_ALONE = 9
 VMEM_MAX = 56 * 1024 * 1024
 
@@ -608,6 +608,7 @@
 LANES = 128
 HALF = 384
 GROUP = 256
+SIDE = 64
 
 
 def exchange_perm(count, shifted, sizes):
@@ -672,7 +673,7 @@
 
 def reduce_arrivals(rounds, far, beside=()):
     arrived = [take_zx(rounds[k - 1], -k, 0) for k in (1, 2, 3)] + [take_zx(far, 0, 1)]
-    return lax.optimization_barrier(tuple(arrived) + tuple(beside))[:4]
+    return lax.optimization_barrier(tuple(arrived) + tuple(beside))[:4], arrived[0]
 
 
 def turn_sum_kernel(*refs):
@@ -698,22 +699,42 @@
     return whole_call(turn_sum_kernel, outs, "turn_sum", (), first, *arrived[:3], near, arrived[3])
 
 
+def small_kernel(gain1_ref, gain2_ref, out_gain_ref, params_ref, taps_ref, out_grad_ref, sent_ref, rows_ref):
+    for row in range(8):
+        for half in range(2):
+            lanes = slice(half * LANES, (half + 1) * LANES)
+            place = 2 * row + half
+            rows_ref[place : place + 1] = gain1_ref[row, 0:1, lanes]
+            rows_ref[16 + place : 17 + place] = gain2_ref[:, place * LANES : (place + 1) * LANES]
+    rows_ref[32:40] = out_gain_ref[...]
+    rows_ref[40:48] = params_ref[...]
+    for part in range(3):
+        rows_ref[48 + 4 * part : 52 + 4 * part] = taps_ref[part]
+    rows_ref[60:] = jnp.zeros_like(rows_ref[60:])
+    small = rows_ref[...]
+    high, rest = split(small)
+    low = narrow(small - wide(high) - wide(rest))
+    pieces = jnp.concatenate([high, rest, low], axis=0)
+    for target in range(8):
+        sent_ref[target, :GROUP] = out_grad_ref[target]
+        sent_ref[target, GROUP:] = pieces
+
+
 def side_sum_kernel(near_ref, crossed_ref, *out_refs):
     for k, out_ref in enumerate(out_refs):
         for half in range(2):
-            rows = slice(ROWS_A * (4 * half + k), ROWS_A * (4 * half + k + 1))
+            rows = slice(SIDE * (4 * half + k), SIDE * (4 * half + k + 1))
             total = wide(near_ref[rows]) + wide(crossed_ref[rows])
-            out_ref[ROWS_A * half : ROWS_A * (half + 1)] = total if k == 0 else narrow(total)
-
-
-def ring_sum_kernel(over_ref, *refs):
-    arrived, (kept_ref, sent_ref) = refs[:4], refs[4:]
+            out_ref[SIDE * half : SIDE * (half + 1)] = total if k == 0 else narrow(total)
+
+
+def ring_sum_kernel(over_ref, arrived_ref, kept_ref, sent_ref):
     half = kept_ref.shape[0]
     for target, side in ((kept_ref, over_ref[0]), (sent_ref, 1 - over_ref[0])):
         rows = pl.ds(pl.multiple_of(side * half, 16), half)
-        total = wide(arrived[0][rows])
-        for ref in arrived[1:]:
-            total = total + wide(ref[rows])
+        total = wide(arrived_ref[0, rows])
+        for source in (1, 2, 3):
+            total = total + wide(arrived_ref[source, rows])
         target[...] = total.astype(target.dtype)
 
 
@@ -724,6 +745,54 @@
 
 
 RINGS = [[0, 2, 4, 6], [1, 3, 5, 7]]
+
+
+def pair_kernel(over_ref, value_ref, mate_ref, *out_refs):
+    rows, start = value_ref.shape[0], 0
+    for out_ref in out_refs:
+        lanes = slice(start, start + out_ref.shape[1])
+        start = lanes.stop
+        for source, place in ((value_ref, over_ref[0]), (mate_ref, 1 - over_ref[0])):
+            out_ref[pl.ds(pl.multiple_of(place * rows, 16), rows)] = source[:, lanes]
+
+
+def ordered_pair(value, mate):
+    over = (lax.axis_index("dp") % 2)[None].astype(jnp.int32)
+    outs = [shaped((2 * value.shape[0], columns), value.dtype) for columns in (2 * HALF, HALF)]
+    return whole_call(pair_kernel, outs, "ordered_pair", (over,), value, mate)
+
+
+def ordered_join_kernel(up_ref, *refs):
+    sources, target, sems = refs[:4], refs[4], refs[5]
+    rows = sources[0].shape[0]
+    copies = []
+    for k, ref in enumerate(sources):
+        place = lax.rem(up_ref[0] + k, 4)
+        copies.append(
+            pltpu.make_async_copy(ref, target.at[pl.ds(pl.multiple_of(place * rows, 16), rows)], sems.at[k])
+        )
+        copies[-1].start()
+    for copy in copies:
+        copy.wait()
+
+
+def ordered_join(pieces):
+    anywhere = pl.BlockSpec(memory_space=pl.ANY)
+    rows, columns = pieces[0].shape
+    return pl.pallas_call(
+        ordered_join_kernel,
+        grid_spec=pltpu.PrefetchScalarGridSpec(
+            num_scalar_prefetch=1,
+            grid=(1,),
+            in_specs=[anywhere] * 4,
+            out_specs=whole((4 * rows, columns)),
+            scratch_shapes=[pltpu.SemaphoreType.DMA((4,))],
+        ),
+        out_shape=shaped((4 * rows, columns), pieces[0].dtype),
+        compiler_params=pltpu.CompilerParams(vmem_limit_bytes=VMEM_MAX),
+        cost_estimate=spends(4),
+        name="ordered_join",
+    )((lax.axis_index("dp") // 2)[None].astype(jnp.int32), *pieces)
 
 
 def spread_kernel(over_ref, *refs):
@@ -759,21 +828,10 @@
     return everything.reshape(8 * spread.shape[2], spread.shape[3])
 
 
-def ring_blocks(value):
-    up = lax.axis_index("dp") // 2
-    rows = value.shape[0] // 4
-    blocks = [lax.dynamic_slice_in_dim(value, (up + k) % 4 * rows, rows, 0) for k in range(4)]
-    return lax.optimization_barrier(tuple(blocks))
-
-
-def ring_arrivals(blocks):
-    return [blocks[0]] + [take_yx(blocks[k], -k, 0) for k in (1, 2, 3)]
-
-
 def ring_parts(arrived):
     over = (lax.axis_index("dp") % 2)[None].astype(jnp.int32)
-    half = (arrived[0].shape[0] // 2, arrived[0].shape[1])
-    return whole_call(ring_sum_kernel, [shaped(half), shaped(half, jnp.bfloat16)], "ring_sum", (over,), *arrived)
+    half = (arrived.shape[1] // 2, arrived.shape[2])
+    return whole_call(ring_sum_kernel, [shaped(half), shaped(half, jnp.bfloat16)], "ring_sum", (over,), arrived)
 
 
 def exchange_ring(value):
@@ -936,7 +994,7 @@
         cost_estimate=spends(8),
         name="in_grads",
     )(own, other, draw0, draw1, weights, gain)
-    return grad, part[:, 0]
+    return grad, part
 
 
 def out_grad_kernel(rows_ref, mixed_ref, out_ref):
@@ -984,10 +1042,8 @@
     def _():
         total_ref[...] = wide(rows_ref[...])
 
-    pair = jnp.concatenate([mixed_ref[heads_ref[0, step]], mixed_ref[heads_ref[1, step]]], axis=1)
-    cut = weight_refs[0].shape[0]
-    total_ref[:, :cut] += against(pair, jnp.concatenate([weight_refs[0][...], weight_refs[1][...]], axis=1))
-    total_ref[:, cut:] += against(pair, jnp.concatenate([weight_refs[2][...], weight_refs[3][...]], axis=1))
+    mixed = jnp.concatenate([mixed_ref[heads_ref[i % 2, 2 * step + i // 2]] for i in range(4)], axis=1)
+    total_ref[...] += against(mixed, jnp.concatenate([ref[0] for ref in weight_refs], axis=1))
 
     @pl.when(step == pl.num_programs(0) - 1)
     def _():
@@ -997,21 +1053,22 @@
         normed_ref[...] = narrow(unit * gain_ref[...])
 
 
-def out_weight_specs(out_parts):
-    rows = out_parts[0].shape[0] // 16
-    first = pl.BlockSpec((rows, LANES), lambda step, *_: (step % 4 * 2 + step // 4, 0))
-    second = pl.BlockSpec((rows, LANES), lambda step, *_: (8 + step, 0))
-    return [first, first, second, second]
-
-
-def attend(heads, received, out_parts, rows, gain):
+def out_weight_specs(out_heads):
+    shape = (1,) + out_heads.shape[1:]
+    return [
+        pl.BlockSpec(shape, lambda step, heads_ref, i=i: (heads_ref[i % 2, 2 * step + i // 2], 0, 0))
+        for i in range(4)
+    ]
+
+
+def attend(heads, received, out_heads, rows, gain):
     shape = rows.shape
     return pl.pallas_call(
         attn_kernel,
         grid_spec=pltpu.PrefetchScalarGridSpec(
             num_scalar_prefetch=1,
-            grid=(8,),
-            in_specs=[whole(received.shape)] + out_weight_specs(out_parts) + [whole(shape), whole(gain.shape)],
+            grid=(4,),
+            in_specs=[whole(received.shape)] + out_weight_specs(out_heads) + [whole(shape), whole(gain.shape)],
             out_specs=[whole(shape), whole(shape)],
             scratch_shapes=[pltpu.VMEM(shape, jnp.float32)],
         ),
@@ -1019,7 +1076,7 @@
         compiler_params=pltpu.CompilerParams(vmem_limit_bytes=VMEM_MAX),
         cost_estimate=spends(10),
         name="attend",
-    )(heads, received, *out_parts, *out_parts, rows, gain)
+    )(heads, received, *[out_heads] * 4, rows, gain)
 
 
 def total_of(refs):
@@ -1042,27 +1099,23 @@
         dresid_ref[...] = dresid
         dattn_ref[...] = narrow(dresid)
 
-    cut = weight_refs[0].shape[0]
-    dattn = dattn_ref[...]
-    weights = jnp.concatenate([weight_refs[0][...], weight_refs[1][...]], axis=1)
-    total = plain_product(dattn[:, :cut], weights)
-    weights = jnp.concatenate([weight_refs[2][...], weight_refs[3][...]], axis=1)
-    total = narrow(total + plain_product(dattn[:, cut:], weights))
-    dmixed_ref[heads_ref[0, step]] = total[:, :LANES]
-    dmixed_ref[heads_ref[1, step]] = total[:, LANES:]
-
-
-def middle(heads, pieces, resid, cot, gain, out_parts):
+    weights = jnp.concatenate([ref[0] for ref in weight_refs], axis=1)
+    total = narrow(plain_product(dattn_ref[...], weights))
+    for i in range(4):
+        dmixed_ref[heads_ref[i % 2, 2 * step + i // 2]] = total[:, i * LANES : (i + 1) * LANES]
+
+
+def middle(heads, pieces, resid, cot, gain, out_heads):
     shape = resid.shape
     mixed_shape = (16, shape[0], LANES)
     return pl.pallas_call(
         middle_kernel,
         grid_spec=pltpu.PrefetchScalarGridSpec(
             num_scalar_prefetch=1,
-            grid=(8,),
+            grid=(4,),
             in_specs=[whole(piece.shape) for piece in pieces]
             + [whole(shape), whole(shape), whole(gain.shape)]
-            + out_weight_specs(out_parts),
+            + out_weight_specs(out_heads),
             out_specs=[whole(shape), whole(shape), whole((1, shape[1])), whole(mixed_shape)],
         ),
         out_shape=[shaped(shape), shaped(shape, jnp.bfloat16), shaped((1, shape[1])),
@@ -1070,7 +1123,7 @@
         compiler_params=pltpu.CompilerParams(vmem_limit_bytes=VMEM_MAX),
         cost_estimate=spends(10),
         name="middle",
-    )(heads, *pieces, resid, cot, gain, *out_parts, *out_parts)
+    )(heads, *pieces, resid, cot, gain, *[out_heads] * 4)
 
 
 def leave_kernel(*refs):
@@ -1103,7 +1156,7 @@
             normed_ref[start : start + ref.shape[0]] = ref[...]
             start += ref.shape[0]
         for place, ref in enumerate(cot_refs):
-            cot_ref[ROWS_A * place : ROWS_A * (place + 1)] = ref[...]
+            cot_ref[SIDE * place : SIDE * (place + 1)] = ref[...]
 
     rows = pl.ds(pl.multiple_of(step * size, 16), size)
     normed, cot = normed_ref[rows], cot_ref[rows]
@@ -1135,17 +1188,15 @@
             start += ref.shape[0]
         if joins:
             near_ref, far_ref = fed_refs
-            near_ref[:ROWS_A] = earlier_refs[0][:ROWS_A]
-            far_ref[:ROWS_A] = earlier_refs[0][ROWS_A:]
-            for k in (1, 2, 3):
-                base = 2 * ROWS_A * (k - 1)
-                near_ref[ROWS_A * k : ROWS_A * (k + 1)] = out_ref[base : base + ROWS_A]
-                far_ref[ROWS_A * k : ROWS_A * (k + 1)] = out_ref[base + ROWS_A : base + 2 * ROWS_A]
-            near_ref[4 * ROWS_A :] = earlier_refs[1][...]
-            far_ref[4 * ROWS_A :] = out_ref[6 * ROWS_A :]
+            for k in range(4):
+                first = earlier_refs[0] if k == 0 else out_ref.at[2 * SIDE * (k - 1) : 2 * SIDE * k]
+                near_ref[SIDE * k : SIDE * (k + 1)] = first[:SIDE]
+                far_ref[SIDE * k : SIDE * (k + 1)] = first[SIDE:]
+            near_ref[4 * SIDE :] = earlier_refs[1][...]
+            far_ref[4 * SIDE :] = out_ref[6 * SIDE :]
         else:
-            fed_refs[0][...] = out_ref[: 2 * ROWS_A]
-            fed_refs[1][...] = out_ref[2 * ROWS_A :]
+            fed_refs[0][...] = out_ref[: 2 * SIDE]
+            fed_refs[1][...] = out_ref[2 * SIDE :]
 
 
 def held(shape, place=None):
@@ -1158,13 +1209,12 @@
     shapes = [piece.shape for piece in pieces]
     count = sum(shape[0] for shape in shapes)
     size = count // steps
-    gate_up = held((width, 2 * HALF))
-    down = held((width, HALF), lambda *_: (0, 2))
+    gate_up, down = held((width, 2 * HALF)), held((width, HALF))
 
     def half_block(slot, half):
-        return held((ROWS_A, width), lambda i, heads_ref: (2 * heads_ref[0, slot] + half, 0))
-
-    fed_shapes = [(8 * ROWS_A, width)] * 2 if earlier else shapes
+        return held((SIDE, width), lambda i, heads_ref: (2 * heads_ref[0, slot] + half, 0))
+
+    fed_shapes = [(8 * SIDE, width)] * 2 if earlier else shapes
     row_widths = (2 * HALF, 4 * HALF, width, width)
     outs = pl.pallas_call(
         partial(feed_kernel, tuple(halves), len(pieces), bool(earlier)),
@@ -1184,8 +1234,9 @@
         compiler_params=pltpu.CompilerParams(vmem_limit_bytes=VMEM_MAX),
         cost_estimate=spends(28),
         name="feed",
-    )(heads, *pieces, *[cot] * len(halves), own, own, other, other, *earlier)
-    return outs[:2], outs[2 : 2 + len(shapes)], outs[2 + len(shapes) :]
+    )(heads, *pieces, *[cot] * len(halves), *own, *other, *earlier)
+    feds = len(fed_shapes)
+    return outs[:feds], outs[feds : feds + len(shapes)], outs[feds + len(shapes) :]
 
 
 def join_kernel(*refs):
@@ -1279,59 +1330,55 @@
     cut, used = pack_one.shape[1], 5 * LANES
 
     mate_one = take_yx(pack_one, 0, 1)
-    pair, column = gather_turn(normed1, ROWS_A, beside=(mate_one,))
+    pair, column = gather_turn(normed1, ROWS_A, beside=(mate_one, pack_two))
     pair, column, mate_one = lax.optimization_barrier((pair, column, mate_one))
     mate_two = take_yx(after(pack_two, mate_one), 0, 1)
     mine_one = round_ring(spread_pair(pack_one, mate_one))
     rings, columns = gather_end(pair, column)
     rings, columns, mine_one, mate_two = lax.optimization_barrier((rings, columns, mine_one, mate_two))
-    spread_two = spread_pair(pack_two, mate_two)
+    pair_gu, pair_down = ordered_pair(pack_two, mate_two)
     normed1_own = join(rings + columns)
     normed1_other = from_head(normed1_own, dc=1)
     raw0, raw1 = project(normed1_own, normed1_other, mine_one, used)
     taps = mine_one.reshape(8, GROUP, cut)[:, :12, 4 * LANES + 2 : 4 * LANES + 18]
     taps = wide(taps.transpose(1, 0, 2).reshape(3, 4, LANES))
 
-    mine_two = round_ring(spread_two)
-
-    out_turn = gather_turn(after(mine_one[:, used:], normed1_own), width // 2, beside=(raw0,))
-    raw0, raw1, out_turn = lax.optimization_barrier((raw0, raw1, out_turn))
-    out_rings, out_columns = gather_end(*out_turn)
+    gu_arrived = [take_yx(pair_gu, k, 0) for k in (1, 2, 3)]
+
+    out_heads = lax.all_gather(after(mine_one[:, used:], normed1_own), "head")
     prepared = prepare(place, starts, gate_params, raw0, raw1, taps)
     mixed, kept = mixer_forward(place, prepared, raw0, raw1, out_gain_row)
-    mixed, mine_two, out_rings, out_columns = lax.optimization_barrier((mixed, mine_two, out_rings, out_columns))
-    cot_group = lax.all_gather(after(cotangent, mixed), "head", axis=0, tiled=True)
+    mixed, gu_arrived, out_heads, pair_down = lax.optimization_barrier((mixed, gu_arrived, out_heads, pair_down))
+    down_arrived = [take_yx(pair_down, k, 0) for k in (1, 2, 3)]
+    cot_group = lax.all_gather(after(cotangent, out_heads), "head", axis=0, tiled=True)
     received = lax.all_to_all(mixed, "head", 0, 0, tiled=False)
-    out_own = join(out_rings + out_columns)
-    out_parts = (out_own, from_head(out_own, dc=1))
-    other_two = from_head(mine_two, dc=1)
-    received, other_two = lax.optimization_barrier((received, other_two))
-    resid, normed2 = attend(heads, received, out_parts, tokens, gain2_row)
-    pair, column = gather_turn(normed2, ROWS_A)
+    resid, normed2 = attend(heads, received, out_heads, tokens, gain2_row)
+    gu_arrived, down_arrived = lax.optimization_barrier((gu_arrived, down_arrived, normed2))[:2]
+    own_two = (ordered_join([pair_gu, *gu_arrived]), ordered_join([pair_down, *down_arrived]))
+    pair, column = gather_turn(normed2, SIDE, beside=own_two)
+    other_two = tuple(from_head(after(weights, pair), dc=1) for weights in own_two)
     rings, columns = gather_end(pair, column)
     near_halves = [(0, 0), (4, 0)] + [(k, 1) for k in range(4)]
     far_halves = [half for k in (1, 2, 3) for half in ((k, 0), (4 + k, 0))] + [(4 + k, 1) for k in range(4)]
     fed_early, (dpair, dnear), kept_near = feed(
-        heads, [pair, column], near_halves, cot_group, mine_two, other_two, 1
+        heads, [pair, column], near_halves, cot_group, own_two, other_two, 1
     )
     rings, columns, dpair = lax.optimization_barrier((rings, columns, dpair))
     (fed_near, fed_far), (*drings, dfar), kept_far = feed(
-        heads, rings[1:] + columns[1:], far_halves, cot_group, mine_two, other_two, 2, fed_early
-    )
-
-    parts = reduce_parts(dpair, dnear, reduce_arrivals(drings, dfar))
+        heads, rings[1:] + columns[1:], far_halves, cot_group, own_two, other_two, 2, fed_early
+    )
+
+    parts = reduce_parts(dpair, dnear, reduce_arrivals(drings, dfar)[0])
     feed_own, feed_other = feed_grads(kept_near, kept_far)
     parts, feed_own, feed_other = lax.optimization_barrier((parts, feed_own, feed_other))
     feed_grad = narrow(wide(feed_own) + wide(from_head(feed_other, dc=1)))
     dnormed2_pieces = reduce_end(parts)
-    feed_blocks = ring_blocks(feed_grad)
-    resid_then = after(resid, feed_blocks)
-    feed_blocks = lax.optimization_barrier((feed_blocks, dnormed2_pieces))[0]
-    dresid, dattn, dgain2, dmixed = middle(heads, dnormed2_pieces, resid_then, cotangent, gain2_row, out_parts)
+    resid_then = after(resid, feed_grad)
+    dresid, dattn, dgain2, dmixed = middle(heads, dnormed2_pieces, resid_then, cotangent, gain2_row, out_heads)
     dmixed_mine = lax.all_to_all(dmixed, "head", 0, 0, tiled=False)
     dcore, dstates, dgate, dgain_out = mixer_backward_scan(place, raw0, raw1, out_gain_row, kept, dmixed_mine)
 
-    feed_arrived = ring_arrivals(feed_blocks)
+    feed_arrived = exchange_ring(after(feed_grad, dmixed_mine).reshape(4, 2 * GROUP, 3 * HALF))
     fed_crossed = take_zx(after(fed_far, dcore), 0, 1)
     dattn_group = lax.all_gather(dattn, "head", axis=0, tiled=True)
     weights_other = from_head(after(mine_one, dmixed), dc=1)
@@ -1339,51 +1386,53 @@
     draw0, draw1, dtaps, dparams = mixer_backward(
         place, starts, gate_params, raw0, raw1, taps, kept, dstates, dcore, dgate
     )
-    draw0, draw1, weights_other, feed_arrived = lax.optimization_barrier((draw0, draw1, weights_other, feed_arrived))
+    draw0, draw1, weights_other = lax.optimization_barrier((draw0, draw1, weights_other))
     draw_far = from_head(draw1, dc=1)
     in_grad, gain1_part = in_grads(normed1_own, normed1_other, draw0, draw1, mine_one, gain1_row)
+    draw_far = after(draw_far, in_grad)
+    dnormed1 = unproject(draw0, draw_far, mine_one, weights_other, [(2 * ROWS_A, width)] * 4 + [(4 * ROWS_B, width)] * 2)
+    dnormed1, feed_arrived, dattn_then, in_grad = lax.optimization_barrier(
+        (dnormed1, feed_arrived, dattn_group, in_grad)
+    )
     in_arrived = exchange_ring(in_grad)
-    draw_far = after(draw_far, in_grad)
-    dnormed1 = unproject(draw0, draw_far, mine_one, weights_other, [dpair.shape] * 4 + [dnear.shape] * 2)
-    dnormed1, feed_arrived, dattn_then = lax.optimization_barrier((dnormed1, feed_arrived, dattn_group))
     feed_kept, feed_sent = ring_parts(feed_arrived)
     out_grad = out_grads(dattn_then, mixed.reshape(dattn_group.shape[0], LANES))
-    arrived = reduce_arrivals(
-        dnormed1[1:4], dnormed1[5], beside=(feed_kept, feed_sent, out_grad, fed_crossed)
-    )
-    dnormed1_pieces = reduce_end(reduce_parts(dnormed1[0], dnormed1[4], arrived))
-    fed_crossed, feed_sent = lax.optimization_barrier((fed_crossed, feed_sent, arrived))[:2]
-    half_rows = (ROWS_A + ROWS_B, width)
+    (sent,) = whole_call(
+        small_kernel,
+        shaped((8, GROUP + 192, LANES), jnp.bfloat16),
+        "small",
+        (),
+        gain1_part,
+        dgain2,
+        dgain_out,
+        dparams,
+        dtaps,
+        out_grad,
+        scratch=[pltpu.VMEM((64, LANES), jnp.float32)],
+    )
+    half_rows = (2 * SIDE, width)
+    in_kept, in_sent = ring_parts(in_arrived)
+    arrived, first_arrived = reduce_arrivals(
+        dnormed1[1:4], dnormed1[5], beside=(feed_kept, feed_sent, in_kept, in_sent, sent, fed_crossed)
+    )
+    parts = reduce_parts(dnormed1[0], dnormed1[4], arrived)
+    dnormed1_pieces = reduce_end(parts)
+    fed_crossed, feed_sent, in_sent = lax.optimization_barrier((fed_crossed, feed_sent, in_sent, parts))[:3]
     fed_sums = whole_call(
         side_sum_kernel, [shaped(half_rows)] + [shaped(half_rows, jnp.bfloat16)] * 3, "side_sum", (), fed_near, fed_crossed
     )
     fed_pieces = [fed_sums[0]] + [take_zx(fed_sums[k], -k, 0) for k in (1, 2, 3)]
-    in_kept, in_sent = ring_parts(list(after(in_arrived, *arrived)))
     one_total = in_kept + wide(take_yx(in_sent, 0, 1))
-    small = jnp.concatenate(
-        [
-            gain1_part.reshape(16, LANES),
-            dgain2.reshape(16, LANES),
-            dgain_out,
-            dparams,
-            dtaps.reshape(12, LANES),
-            jnp.zeros((4, LANES), jnp.float32),
-        ],
-        axis=0,
-    )
-    high, rest = split(small)
-    small_rows = jnp.concatenate([high, rest, narrow(small - wide(high) - wide(rest))], axis=0)
-    sent = jnp.concatenate(
-        [out_grad, jnp.broadcast_to(small_rows, (8,) + small_rows.shape)], axis=1
-    )
-    got = lax.all_to_all(after(sent, in_arrived, *arrived), "dp", 0, 0, tiled=False)
+    got = lax.all_to_all(after(sent, in_arrived, first_arrived), "dp", 0, 0, tiled=False)
+    dnormed1_pieces, got = lax.optimization_barrier((dnormed1_pieces, got))
     out_total = jnp.sum(wide(got[:, :GROUP]), axis=0)
-    pieces = wide(got[:, GROUP:]).reshape(8, 3, small.shape[0], LANES)
+    pieces = wide(got[:, GROUP:]).reshape(8, 3, 64, LANES)
     small = jnp.sum(pieces[:, 0] + pieces[:, 1] + pieces[:, 2], axis=0)
     shared = sum_all(small[:40], "head", 16)
     fed_pieces, shared = lax.optimization_barrier((fed_pieces, shared))
     (block_out,) = whole_call(leave_kernel, shaped(rows_shape, jnp.bfloat16), "leave", (), *fed_pieces, resid)
-    feed_total = feed_kept + wide(take_yx(feed_sent, 0, 1))
+    feed_got, shared = lax.optimization_barrier((take_yx(feed_sent, 0, 1), shared))
+    feed_total = feed_kept + wide(feed_got)
 
     gain1_total = shared[:16].reshape(-1)
     gain2_total = shared[16:32].reshape(-1)

time: 552 us -> 513 us (0.929)
  waiting for transfers between devices: 140 us -> 100 us
  starting transfers between devices: 89.6 us -> 108 us
    ppermute x50 -> x42, waiting for transfers between devices: 106 us -> 45.7 us  [from_head(): lax.ppermute(value, 'head', exchange_perm(16, (dz, dx, dc), (4, 2, 2)))]
    all_to_all x1 -> x2, waiting for transfers between devices: 0.01 us -> 13 us  [exchange_ring(): lax.all_to_all(value, 'dp', 0, 0, tiled=False, axis_index_groups=RINGS)]
    ppermute x7 -> x10, waiting for transfers between devices: 10.4 us -> 22.8 us  [from_dp(): return lax.ppermute(value, 'dp', exchange_perm(8, (dy, dx), (4, 2)))]
    ppermute x50 -> x42, starting transfers between devices: 45.8 us -> 57.7 us  [from_head(): lax.ppermute(value, 'head', exchange_perm(16, (dz, dx, dc), (4, 2, 2)))]
    all_to_all x1, waiting for transfers between devices: 15.4 us -> 4.33 us  [body(): received = lax.all_to_all(mixed, 'head', 0, 0, tiled=False)]
    all_gather x1 -> x2, waiting for transfers between devices: 0.38 us -> 9.54 us  [the longest x1 5.28 us: body(): lax.all_gather(after(cotangent, out_heads), 'head', axis=0, tiled=True)]
    pallas_call x0 -> x2, Pallas kernels: none -> 6.4 us  [ordered_join(): pl.pallas_call(ordered_join_kernel, grid_spec=pltpu.PrefetchScalarGridSpe...]
    all_to_all x1 -> x2, starting transfers between devices: 3.67 us -> 9.58 us  [exchange_ring(): lax.all_to_all(value, 'dp', 0, 0, tiled=False, axis_index_groups=RINGS)]
  transfers between devices with their start and end apart: 65 -> 61, of which waited for: 25 -> 22; matrix products, arithmetic and copies ran while one was open for 6% -> 4% of each run, Pallas kernels for 32% -> 34%
where the time goes in v3:
time: 513 us; the launch traced here: 506 us
  Pallas kernels  226 us (44%)
  starting transfers between devices  108 us (21%)
  waiting for transfers between devices  100 us (19%)
  local copies, waits for them, and re-layouts  26.8 us (5%)
  blocking collectives  16.4 us (3%)
  other arithmetic  14.6 us (3%)
  between operations  14.6 us (3%)
    ppermute x42, starting transfers between devices, from_head(): lax.ppermute(value, 'head', exchange_perm(16, (dz, dx, dc), (4, 2, 2)))  57.7 us
    ppermute x42, waiting for transfers between devices, from_head(): lax.ppermute(value, 'head', exchange_perm(16, (dz, dx, dc), (4, 2, 2)))  45.7 us
    pallas_call x2, Pallas kernels, feed(): pl.pallas_call(partial(feed_kernel, tuple(halves), len(pieces), bool(earl...  40.8 us
    pallas_call x10, Pallas kernels, whole_call(): pl.pallas_call(kernel, grid_spec=pltpu.PrefetchScalarGridSpec(num_scalar_...  31.2 us
    pallas_call x1, Pallas kernels, back(): pl.pallas_call(back_kernel, grid_spec=pltpu.PrefetchScalarGridSpec(num_sc...  25.3 us
    ppermute x10, waiting for transfers between devices, from_dp(): return lax.ppermute(value, 'dp', exchange_perm(8, (dy, dx), (4, 2)))  22.8 us
    ppermute x10, starting transfers between devices, from_dp(): return lax.ppermute(value, 'dp', exchange_perm(8, (dy, dx), (4, 2)))  19.5 us
    pallas_call x1, Pallas kernels, prepare(): pl.pallas_call(prepare_kernel, grid_spec=pltpu.PrefetchScalarGridSpec(num...  18.3 us
  transfers between devices with their start and end apart: 61, of which 22 were waited for; matrix products, arithmetic and copies ran while one was open for 4% of the time, Pallas kernels for 34%

profile of v3, /device:TPU:1, one launch (start us, length us, event | category | flops | bytes accessed | tf_op | source)
XLA Modules:
  0.0 506.2 jit_solution(4829763510495776062)
XLA Ops:
  29.1 5.1 %collective-permute-done.2 = bf16[48,2048]{1,0:T(8,128)(2,1)S(1)} collective-permute-done((bf16[48,2048]{1,0:T(8,128)(2,1)S(1)}, bf16[48,2048]{1,0:T(8,128)(2,1)S(1)}, u32[]{:S(2)}, u32[]{:S(2)}) %collective-permute-start.2) | collective-permute-done | bytes 196640 | tf_op jit(solution)/shard_map/ppermute | solution.py:627
  51.8 22.8 %collective-permute-done.9.mate_ref = bf16[256,1152]{1,0:T(8,128)(2,1)S(1)} collective-permute-done((bf16[256,1152]{1,0:T(8,128)(2,1)}, bf16[256,1152]{1,0:T(8,128)(2,1)S(1)}, u32[]{:S(2)}, u32[]{:S(2)}) %collective-permute-start.9) | collective-permute-done | bytes 589856 | tf_op jit(solution)/shard_map/ppermute | solution.py:631
  98.2 11.9 %project.1 = (f32[1024,640]{1,0:T(8,128)}, f32[1024,640]{1,0:T(8,128)}) custom-call(bf16[1024,2048]{1,0:T(8,128)(2,1)} %join.1.own_ref, bf16[1024,2048]{1,0:T(8,128)(2,1)} %collective-permute-done.10.other_ref, bf16[2048,768]{1,0:T(8,128)(2,1)} %bitcast.36), custom_call_target="tpu_custom_call" | custom-call | flops 5000000 | bytes 1024 | tf_op jit(solution)/shard_map/project/pallas_call | solution.py:903
  110.1 18.3 %prepare.1 = (f32[16,8,128]{2,1,0:T(8,128)}, f32[16,128,128]{2,1,0:T(8,128)}, f32[16,128,128]{2,1,0:T(8,128)}, f32[16,128,128]{2,1,0:T(8,128)}, f32[16,128,256]{...) custom-call(s32[3,16]{1,0:T(4,128)} %pad_add_fusion.place_ref, ...), custom_call_target="tpu_custom_call" | custom-call | flops 18000000 | bytes 1024 | tf_op jit(solution)/shard_map/prepare/pallas_call | solution.py:291
  128.3 7.2 %scan_states.1 = (f32[16,128,128]{2,1,0:T(8,128)}, f32[16,128,128]{2,1,0:T(8,128)}, bf16[16,128,128]{2,1,0:T(8,128)(2,1)}) custom-call(s32[3,16]{1,0:T(4,128)} %pad_add_fusion.place_ref, bf16[16,128,256]{2,1,0:T(8,128)(2,1)} %get-tuple-element.230.m_ref, f32[16,128,128]{2,1,0:T(8,128)} %get-tuple-element.231.b_ref, ...), custom_call_target="tpu_custom_call" | custom-call | flops 7000000 | bytes 1024 | tf_op jit(solution)/shard_map/scan_states/pallas_call | solution.py:339
  139.9 5.2 %all-to-all-start.1 = ((bf16[16,128,128]{2,1,0:T(8,128)(2,1)}), bf16[16,128,128]{2,1,0:T(8,128)(2,1)S(1)}, u32[]{:S(2)}, u32[]{:S(2)}) async-start(bf16[16,128,128]{2,1,0:T(8,128)(2,1)} %get-tuple-element.239), calls=%async_computation.1 | async-start | bytes 1048576 | tf_op jit(solution)/shard_map/all_to_all | solution.py:1354
  155.7 8.3 %attend.1 = (f32[128,2048]{1,0:T(8,128)}, bf16[128,2048]{1,0:T(8,128)(2,1)}) custom-call(s32[2,8]{1,0:T(2,128)} %pad_add_fusion.1.heads_ref, bf16[16,128,128]{2,1,0:T(8,128)(2,1)} %copy-done.8, bf16[16,2048,128]{2,1,0:T(8,128)(2,1)} %bitcast.26, bf16[16,2048,128]{2,1,0:T(8,128)(2,1)} %bitcast.27, bf16[16,2048,128]{2,1,0:T(8,128)(2,1)} %bitcast.28, ...), custom_call_target="tpu_custom_call" | custom-call | flops 10000000 | bytes 1024 | tf_op jit(solution)/shard_map/attend/pallas_call | solution.py:1066
  178.6 12.5 %collective-permute-done.16 = bf16[64,2048]{1,0:T(8,128)(2,1)S(1)} collective-permute-done((bf16[64,2048]{1,0:T(8,128)(2,1)S(1)}, bf16[64,2048]{1,0:T(8,128)(2,1)S(1)}, u32[]{:S(2)}, u32[]{:S(2)}) %collective-permute-start.16) | collective-permute-done | bytes 262176 | tf_op jit(solution)/shard_map/ppermute | solution.py:627
  197.9 6.0 %collective-permute-done.26.refs_11_.refs_17_ = bf16[2048,384]{1,0:T(8,128)(2,1)S(1)} collective-permute-done((bf16[2048,384]{1,0:T(8,128)(2,1)S(1)}, bf16[2048,384]{1,0:T(8,128)(2,1)S(1)}, u32[]{:S(2)}, u32[]{:S(2)}) %collective-permute-start.26) | collective-permute-done | bytes 1572896 | tf_op jit(solution)/shard_map/ppermute | solution.py:627
  204.3 5.3 %all-gather.5.cloned.1.call-done.refs_2_.refs_3_.refs_4_.refs_5_.refs_6_.refs_7_.refs_8_.refs_9_.refs_10_.refs_11_.refs_12_.refs_13_ = bf16[2048,2048]{1,0:T(8,128)(2,1)} async-done(((bf16[128,2048]{1,0:T(8,128)(2,1)}), bf16[2048,2048]{1,0:T(8,128)(2,1)}) %all-gather.5.cloned.1.call-update) | async-done | bytes 8388624 | tf_op jit(solution)/shard_map/all_gather | solution.py:1353
  209.6 15.2 %feed.2 = (bf16[128,2048]{1,0:T(8,128)(2,1)}, bf16[256,2048]{1,0:T(8,128)(2,1)}, bf16[128,2048]{1,0:T(8,128)(2,1)}, bf16[256,2048]{1,0:T(8,128)(2,1)}, bf16[384,...) custom-call(s32[2,8]{1,0:T(2,128)} %pad_add_fusion.1.heads_ref, ...), custom_call_target="tpu_custom_call" | custom-call | flops 28000000 | bytes 1024 | tf_op jit(solution)/shard_map/feed/pallas_call | solution.py:1219
  228.5 25.6 %feed.3 = (bf16[512,2048]{1,0:T(8,128)(2,1)}, bf16[512,2048]{1,0:T(8,128)(2,1)}, bf16[128,2048]{1,0:T(8,128)(2,1)}, bf16[128,2048]{1,0:T(8,128)(2,1)}, bf16[128,...) custom-call(s32[2,8]{1,0:T(2,128)} %pad_add_fusion.1.heads_ref, ...), custom_call_target="tpu_custom_call" | custom-call | flops 28000000 | bytes 1024 | tf_op jit(solution)/shard_map/feed/pallas_call | solution.py:1219
  254.9 7.4 %collective-permute-start.27 = (bf16[128,2048]{1,0:T(8,128)(2,1)}, bf16[128,2048]{1,0:T(8,128)(2,1)S(1)}, u32[]{:S(2)}, u32[]{:S(2)}) collective-permute-start(bf16[128,2048]{1,0:T(8,128)(2,1)} %get-tuple-element.273), channel_id=1, source_target_pairs={{12,0},{13,1},{14,2},{15,3},{0,4},{1,5},{2,6},{3,7},{4,8},{5,9},{6... | collective-permute-start | bytes 1572872 | tf_op jit(solution)/shard_map/ppermute | solution.py:627
  264.7 18.0 %feed_grads.1 = (bf16[2048,1152]{1,0:T(8,128)(2,1)}, bf16[2048,1152]{1,0:T(8,128)(2,1)}) custom-call(bf16[384,2048]{1,0:T(8,128)(2,1)} %get-tuple-element.288.refs_0_, bf16[384,2048]{1,0:T(8,128)(2,1)} %get-tuple-element.289.refs_1_, bf16[384,1536]{1,0:T(8,128)(2,1)} %get-tuple-element.290.refs_2_, bf16[384,768]{1,0:T(8,128)(2,1)} %get-tuple-element.291.refs_3_, ...), custom_call_target="tpu_custom_call" | custom-call | flops 12000000 | bytes 1024 | tf_op jit(solution)/shard_map/feed_grads/pallas_call | solution.py:958
  299.2 5.8 %add_convert_fusion = bf16[2048,1152]{1,0:T(8,128)(2,1)} fusion(bf16[2048,1152]{1,0:T(8,128)(2,1)S(1)} %collective-permute-done.35, bf16[2048,1152]{1,0:T(8,128)(2,1)} %get-tuple-element.305), kind=kLoop, calls=%fused_computation | loop fusion | flops 9437184 | bytes 14155776 | tf_op jit(solution)/shard_map/convert_element_type | solution.py:664
  308.6 8.7 %middle.1 = (f32[128,2048]{1,0:T(8,128)}, bf16[128,2048]{1,0:T(8,128)(2,1)}, f32[1,2048]{1,0:T(1,128)}, bf16[16,128,128]{2,1,0:T(8,128)(2,1)}) custom-call(s32[2,8]{1,0:T(2,128)} %pad_add_fusion.1.heads_ref, f32[64,2048]{1,0:T(8,128)} %get-tuple-element.298.refs_0_, bf16[64,2048]{1,0:T(8,128)(2,1)} %copy-done.29, f32[64,2048]{1,0:T(8,128)} %get-tuple-element.300.refs_2_, ...), custom_call_target="tpu_custom_call" | custom-call | flops 10000000 | bytes 1024 | tf_op jit(solution)/shard_map/middle/pallas_call | solution.py:1111
  318.5 16.4 %all_to_all.35.dmixed_ref = bf16[16,128,128]{2,1,0:T(8,128)(2,1)} all-to-all(bf16[16,128,128]{2,1,0:T(8,128)(2,1)} %get-tuple-element.308), channel_id=1, replica_groups=mesh['dp'=8,'head'=16] {'head'}, dimensions={0} | all-to-all | bytes 1048576 | tf_op jit(solution)/shard_map/all_to_all | solution.py:1378
  339.9 7.3 %back_scan.1 = (f32[16,128,128]{2,1,0:T(8,128)}, f32[16,128,128]{2,1,0:T(8,128)}, bf16[16,128,128]{2,1,0:T(8,128)(2,1)}, f32[8,128]{1,0:T(8,128)}) custom-call(s32[3,16]{1,0:T(4,128)} %pad_add_fusion.place_ref, bf16[16,128,256]{2,1,0:T(8,128)(2,1)} %get-tuple-element.270.mt_ref, f32[16,128,128]{2,1,0:T(8,128)} %get-tuple-element.232.r_ref, ...), custom_call_target="tpu_custom_call" | custom-call | flops 7000000 | bytes 1024 | tf_op jit(solution)/shard_map/back_scan/pallas_call | solution.py:399
  347.3 25.3 %back.1 = (bf16[1024,640]{1,0:T(8,128)(2,1)}, bf16[1024,640]{1,0:T(8,128)(2,1)}, f32[3,4,128]{2,1,0:T(4,128)}, f32[8,128]{1,0:T(8,128)}) custom-call(s32[3,16]{1,0:T(4,128)} %pad_add_fusion.place_ref, s32[32]{0:T(128)} %or_convert_fusion.starts_ref, f32[2,1]{1,0:T(2,128)} %copy.73.params_ref, f32[1024,640]{1,0:T(8,128)} %get-tuple-element.228.raw0_ref.gate0_ref, ...), custom_call_target="tpu_custom_call" | custom-call | flops 24000000 | bytes 1024 | tf_op jit(solution)/shard_map/back/pallas_call | solution.py:563
  374.7 13.0 %in_grads.1 = (bf16[4,512,640]{2,1,0:T(8,128)(2,1)}, f32[8,8,256]{2,1,0:T(8,128)}) custom-call(bf16[1024,2048]{1,0:T(8,128)(2,1)} %join.1.own_ref, bf16[1024,2048]{1,0:T(8,128)(2,1)} %collective-permute-done.10.other_ref, bf16[1024,640]{1,0:T(8,128)(2,1)} %get-tuple-element.322.draw0_ref.own_ref, bf16[1024,640]{1,0:T(8,128)(2,1)} %get-tuple-element.323.draw1_ref, ...), custom_call_target="tpu_custom_call" | custom-call | flops 8000000 | bytes 1024 | tf_op jit(solution)/shard_map/in_grads/pallas_call | solution.py:985
  388.8 13.1 %unproject.1 = (bf16[160,2048]{1,0:T(8,128)(2,1)}, bf16[160,2048]{1,0:T(8,128)(2,1)}, bf16[160,2048]{1,0:T(8,128)(2,1)}, bf16[160,2048]{1,0:T(8,128)(2,1)}, bf16...) custom-call(bf16[1024,640]{1,0:T(8,128)(2,1)} %get-tuple-element.322.draw0_ref.own_ref, bf16[1024,640]{1,0:T(8,128)(2,1)} %copy-done.11, ...), custom_call_target="tpu_custom_call" | custom-call | flops 8000000 | bytes 1024 | tf_op jit(solution)/shard_map/unproject/pallas_call | solution.py:925
  414.5 8.5 %out_grads.1.out_grad_ref = bf16[8,256,128]{2,1,0:T(8,128)(2,1)} custom-call(bf16[2048,2048]{1,0:T(8,128)(2,1)} %all-gather.7.cloned.1.call-done.rows_ref, bf16[2048,128]{1,0:T(8,128)(2,1)} %bitcast.41), custom_call_target="tpu_custom_call" | custom-call | flops 6000000 | bytes 1024 | tf_op jit(solution)/shard_map/out_grads/pallas_call | solution.py:1006
  425.1 13.0 %all-to-all-done.4.arrived_ref = bf16[4,512,640]{2,1,0:T(8,128)(2,1)S(1)} async-done(((bf16[4,512,640]{2,1,0:T(8,128)(2,1)}), bf16[4,512,640]{2,1,0:T(8,128)(2,1)S(1)}, u32[]{:S(2)}, u32[]{:S(2)}) %all-to-all-start.4) | async-done | bytes 2621472 | tf_op jit(solution)/shard_map/all_to_all | solution.py:838
  474.0 7.7 %all-to-all-start.6 = ((f32[16,40,128]{2,1,0:T(8,128)}), f32[16,40,128]{2,1,0:T(8,128)S(1)}, u32[]{:S(2)}, u32[]{:S(2)}) async-start(f32[16,40,128]{2,1,0:T(8,128)} %broadcast_in_dim.35), calls=%async_computation.6 | async-start | bytes 655360 | tf_op jit(solution)/shard_map/all_to_all | solution.py:843
  (273 shorter events, 204.0 us)
Async XLA Ops:
  40.2 39.9 %all-to-all-start = ((bf16[4,2,256,768]{3,2,1,0:T(8,128)(2,1)}), bf16[4,2,256,768]{3,2,1,0:T(8,128)(2,1)S(1)}, u32[]{:S(2)}, u32[]{:S(2)}) async-start(bf16[4,2,256,768]{3,2,1,0:T(8,128)(2,1)} %spread_pair.1), calls=%async_computation | async-start | bytes 6291456 | tf_op jit(solution)/shard_map/all_to_all | solution.py:827
  44.3 95.5 %all-gather.9.cloned.1.call-start = ((), (), s32[]{:S(2)}) async-start(), calls=%async_computation.9 | async-start | bytes 8912896 | tf_op jit(solution)/shard_map/all_gather | solution.py:1348
  44.3 34.9 %collective-permute-start.8 = (bf16[192,2048]{1,0:T(8,128)(2,1)}, bf16[192,2048]{1,0:T(8,128)(2,1)}, u32[]{:S(2)}, u32[]{:S(2)}) collective-permute-start(bf16[192,2048]{1,0:T(8,128)(2,1)} %pad_maximum_fusion.1.refs_4_), channel_id=1, source_target_pairs={{2,0},{3,1},{0,2},{1,3},{6,4},{7,5},{4,6},{5,7},{10,8},{11,9},{8,1... | collective-permute-start | bytes 2359304 | tf_op jit(solution)/shard_map/ppermute | solution.py:627
  45.5 29.1 %collective-permute-start.7 = (bf16[160,2048]{1,0:T(8,128)(2,1)}, bf16[160,2048]{1,0:T(8,128)(2,1)S(1)}, u32[]{:S(2)}, u32[]{:S(2)}) collective-permute-start(bf16[160,2048]{1,0:T(8,128)(2,1)} %pad_maximum_fusion.2.refs_0_), channel_id=1, source_target_pairs={{12,0},{13,1},{14,2},{15,3},{0,4},{1,5},{2,6},{3,7},{4,8},{5,9},{6... | collective-permute-start | bytes 1966088 | tf_op jit(solution)/shard_map/ppermute | solution.py:627
  47.1 30.2 %collective-permute-start.6 = (bf16[160,2048]{1,0:T(8,128)(2,1)}, bf16[160,2048]{1,0:T(8,128)(2,1)S(1)}, u32[]{:S(2)}, u32[]{:S(2)}) collective-permute-start(bf16[160,2048]{1,0:T(8,128)(2,1)} %pad_maximum_fusion.2.refs_0_), channel_id=1, source_target_pairs={{8,0},{9,1},{10,2},{11,3},{12,4},{13,5},{14,6},{15,7},{0,8},{1,9},... | collective-permute-start | bytes 1966088 | tf_op jit(solution)/shard_map/ppermute | solution.py:627
  85.6 123.9 %all-gather.5.cloned.1.call-start = ((), (), s32[]{:S(2)}) async-start(), calls=%async_computation.7 | async-start | bytes 8912896 | tf_op jit(solution)/shard_map/all_gather | solution.py:1353
  92.3 43.2 %collective-permute-start.13 = (bf16[512,768]{1,0:T(8,128)(2,1)}, bf16[512,768]{1,0:T(8,128)(2,1)}, u32[]{:S(2)}, u32[]{:S(2)}) collective-permute-start(bf16[512,768]{1,0:T(8,128)(2,1)} %get-tuple-element.236.refs_0_), channel_id=1, source_target_pairs={{96,0},{112,16},{0,32},{16,48},{32,64},{48,80},{64,96},{80,112},{9... | collective-permute-start | bytes 2359304 | tf_op jit(solution)/shard_map/ppermute | solution.py:631
  93.1 42.5 %collective-permute-start.12 = (bf16[512,768]{1,0:T(8,128)(2,1)}, bf16[512,768]{1,0:T(8,128)(2,1)}, u32[]{:S(2)}, u32[]{:S(2)}) collective-permute-start(bf16[512,768]{1,0:T(8,128)(2,1)} %get-tuple-element.236.refs_0_), channel_id=1, source_target_pairs={{64,0},{80,16},{96,32},{112,48},{0,64},{16,80},{32,96},{48,112},{6... | collective-permute-start | bytes 2359304 | tf_op jit(solution)/shard_map/ppermute | solution.py:631
  95.4 40.1 %collective-permute-start.11 = (bf16[512,768]{1,0:T(8,128)(2,1)}, bf16[512,768]{1,0:T(8,128)(2,1)}, u32[]{:S(2)}, u32[]{:S(2)}) collective-permute-start(bf16[512,768]{1,0:T(8,128)(2,1)} %get-tuple-element.236.refs_0_), channel_id=1, source_target_pairs={{32,0},{48,16},{64,32},{80,48},{96,64},{112,80},{0,96},{16,112},{3... | collective-permute-start | bytes 2359304 | tf_op jit(solution)/shard_map/ppermute | solution.py:631
  145.1 256.7 %all-gather.7.cloned.1.call-start = ((), (), s32[]{:S(2)}) async-start(), calls=%async_computation.8 | async-start | bytes 8912896 | tf_op jit(solution)/shard_map/all_gather | solution.py:1383
  195.8 32.7 %collective-permute-start.24 = (bf16[256,2048]{1,0:T(8,128)(2,1)S(1)}, bf16[256,2048]{1,0:T(8,128)(2,1)}, u32[]{:S(2)}, u32[]{:S(2)}) collective-permute-start(bf16[256,2048]{1,0:T(8,128)(2,1)S(1)} %pad_maximum_fusion.refs_1_), channel_id=1, source_target_pairs={{2,0},{3,1},{0,2},{1,3},{6,4},{7,5},{4,6},{5,7},{10,8},{11,9},{8,1... | collective-permute-start | bytes 3145736 | tf_op jit(solution)/shard_map/ppermute | solution.py:627
  196.5 28.3 %collective-permute-start.23 = (bf16[128,2048]{1,0:T(8,128)(2,1)S(1)}, bf16[128,2048]{1,0:T(8,128)(2,1)}, u32[]{:S(2)}, u32[]{:S(2)}) collective-permute-start(bf16[128,2048]{1,0:T(8,128)(2,1)S(1)} %pad_maximum_fusion.3.refs_0_), channel_id=1, source_target_pairs={{12,0},{13,1},{14,2},{15,3},{0,4},{1,5},{2,6},{3,7},{4,8},{5,9},{6... | collective-permute-start | bytes 1572872 | tf_op jit(solution)/shard_map/ppermute | solution.py:627
  196.5 32.0 %collective-permute-start.22 = (bf16[128,2048]{1,0:T(8,128)(2,1)S(1)}, bf16[128,2048]{1,0:T(8,128)(2,1)}, u32[]{:S(2)}, u32[]{:S(2)}) collective-permute-start(bf16[128,2048]{1,0:T(8,128)(2,1)S(1)} %pad_maximum_fusion.3.refs_0_), channel_id=1, source_target_pairs={{8,0},{9,1},{10,2},{11,3},{12,4},{13,5},{14,6},{15,7},{0,8},{1,9},... | collective-permute-start | bytes 1572872 | tf_op jit(solution)/shard_map/ppermute | solution.py:627
  254.1 31.4 %collective-permute-start.30 = (bf16[256,2048]{1,0:T(8,128)(2,1)}, bf16[256,2048]{1,0:T(8,128)(2,1)S(1)}, u32[]{:S(2)}, u32[]{:S(2)}) collective-permute-start(bf16[256,2048]{1,0:T(8,128)(2,1)} %get-tuple-element.276), channel_id=1, source_target_pairs={{2,0},{3,1},{0,2},{1,3},{6,4},{7,5},{4,6},{5,7},{10,8},{11,9},{8,1... | collective-permute-start | bytes 3145736 | tf_op jit(solution)/shard_map/ppermute | solution.py:627
  317.3 55.3 %collective-permute-start.37 = (bf16[2048,768]{1,0:T(8,128)(2,1)S(1)}, bf16[2048,768]{1,0:T(8,128)(2,1)}, u32[]{:S(2)}, u32[]{:S(2)}) collective-permute-start(bf16[2048,768]{1,0:T(8,128)(2,1)S(1)} %bitcast.39), channel_id=1, source_target_pairs={{1,0},{0,1},{3,2},{2,3},{5,4},{4,5},{7,6},{6,7},{9,8},{8,9},{11,10... | collective-permute-start | bytes 9437192 | tf_op jit(solution)/shard_map/ppermute | solution.py:627
  334.9 67.0 %all-to-all-start.3 = ((bf16[4,512,1152]{2,1,0:T(8,128)(2,1)}), bf16[4,512,1152]{2,1,0:T(8,128)(2,1)}, u32[]{:S(2)}, u32[]{:S(2)}) async-start(bf16[4,512,1152]{2,1,0:T(8,128)(2,1)} %bitcast.40), calls=%async_computation.3 | async-start | bytes 9437184 | tf_op jit(solution)/shard_map/all_to_all | solution.py:838
  374.7 67.7 %collective-permute-start.36 = (bf16[512,2048]{1,0:T(8,128)(2,1)}, bf16[512,2048]{1,0:T(8,128)(2,1)}, u32[]{:S(2)}, u32[]{:S(2)}) collective-permute-start(bf16[512,2048]{1,0:T(8,128)(2,1)} %get-tuple-element.310), channel_id=1, source_target_pairs={{2,0},{3,1},{0,2},{1,3},{6,4},{7,5},{4,6},{5,7},{10,8},{11,9},{8,1... | collective-permute-start | bytes 6291464 | tf_op jit(solution)/shard_map/ppermute | solution.py:627
  401.8 36.3 %all-to-all-start.4 = ((bf16[4,512,640]{2,1,0:T(8,128)(2,1)}), bf16[4,512,640]{2,1,0:T(8,128)(2,1)S(1)}, u32[]{:S(2)}, u32[]{:S(2)}) async-start(bf16[4,512,640]{2,1,0:T(8,128)(2,1)} %get-tuple-element.337), calls=%async_computation.4 | async-start | bytes 5242880 | tf_op jit(solution)/shard_map/all_to_all | solution.py:838
  406.4 36.0 %collective-permute-start.42 = (bf16[192,2048]{1,0:T(8,128)(2,1)}, bf16[192,2048]{1,0:T(8,128)(2,1)S(1)}, u32[]{:S(2)}, u32[]{:S(2)}) collective-permute-start(bf16[192,2048]{1,0:T(8,128)(2,1)} %get-tuple-element.343), channel_id=1, source_target_pairs={{2,0},{3,1},{0,2},{1,3},{6,4},{7,5},{4,6},{5,7},{10,8},{11,9},{8,1... | collective-permute-start | bytes 2359304 | tf_op jit(solution)/shard_map/ppermute | solution.py:627
  408.0 34.4 %collective-permute-start.39 = (bf16[160,2048]{1,0:T(8,128)(2,1)}, bf16[160,2048]{1,0:T(8,128)(2,1)}, u32[]{:S(2)}, u32[]{:S(2)}) collective-permute-start(bf16[160,2048]{1,0:T(8,128)(2,1)} %get-tuple-element.340), channel_id=1, source_target_pairs={{12,0},{13,1},{14,2},{15,3},{0,4},{1,5},{2,6},{3,7},{4,8},{5,9},{6... | collective-permute-start | bytes 1966088 | tf_op jit(solution)/shard_map/ppermute | solution.py:627
  408.0 34.4 %collective-permute-start.40 = (bf16[160,2048]{1,0:T(8,128)(2,1)}, bf16[160,2048]{1,0:T(8,128)(2,1)}, u32[]{:S(2)}, u32[]{:S(2)}) collective-permute-start(bf16[160,2048]{1,0:T(8,128)(2,1)} %get-tuple-element.341), channel_id=1, source_target_pairs={{8,0},{9,1},{10,2},{11,3},{12,4},{13,5},{14,6},{15,7},{0,8},{1,9},... | collective-permute-start | bytes 1966088 | tf_op jit(solution)/shard_map/ppermute | solution.py:627
  408.4 34.0 %collective-permute-start.41 = (bf16[160,2048]{1,0:T(8,128)(2,1)}, bf16[160,2048]{1,0:T(8,128)(2,1)}, u32[]{:S(2)}, u32[]{:S(2)}) collective-permute-start(bf16[160,2048]{1,0:T(8,128)(2,1)} %get-tuple-element.342), channel_id=1, source_target_pairs={{4,0},{5,1},{6,2},{7,3},{8,4},{9,5},{10,6},{11,7},{12,8},{13,9},{1... | collective-permute-start | bytes 1966088 | tf_op jit(solution)/shard_map/ppermute | solution.py:627
  460.2 32.0 %collective-permute-start.43 = (bf16[128,2048]{1,0:T(8,128)(2,1)}, bf16[128,2048]{1,0:T(8,128)(2,1)S(1)}, u32[]{:S(2)}, u32[]{:S(2)}) collective-permute-start(bf16[128,2048]{1,0:T(8,128)(2,1)} %get-tuple-element.365), channel_id=1, source_target_pairs={{12,0},{13,1},{14,2},{15,3},{0,4},{1,5},{2,6},{3,7},{4,8},{5,9},{6... | collective-permute-start | bytes 1572872 | tf_op jit(solution)/shard_map/ppermute | solution.py:627
  462.3 29.9 %collective-permute-start.44 = (bf16[128,2048]{1,0:T(8,128)(2,1)}, bf16[128,2048]{1,0:T(8,128)(2,1)}, u32[]{:S(2)}, u32[]{:S(2)}) collective-permute-start(bf16[128,2048]{1,0:T(8,128)(2,1)} %get-tuple-element.366), channel_id=1, source_target_pairs={{8,0},{9,1},{10,2},{11,3},{12,4},{13,5},{14,6},{15,7},{0,8},{1,9},... | collective-permute-start | bytes 1572872 | tf_op jit(solution)/shard_map/ppermute | solution.py:627
  (80 other events, 938.2 us)
Sparse Core Ops, SparseCore 0:
  85.8 54.0 all-gather.8
  141.5 68.0 all-gather.4
  317.4 55.9 all-gather.6

commit v4 on v3

--- a/solution.py
+++ b/solution.py
@@ -7,7 +7,9 @@
 from jax.experimental.pallas import tpu as pltpu
 
 CHUNK = 128
-BATCH = 4
+PREPARE_BATCH = 8
+SCAN_BATCH = 4
+BACK_BATCH = 2
 ROWS_A = 80
 ROWS_B = 48
 GATE_ALONE = 9
@@ -231,8 +233,8 @@
     row_index, col_index = iotas()
     diagonal = (row_index == col_index).astype(jnp.float32)
     stricts, kept = [], []
-    for member in range(BATCH):
-        chunk = pl.program_id(0) * BATCH + member
+    for member in range(PREPARE_BATCH):
+        chunk = pl.program_id(0) * PREPARE_BATCH + member
         starts = start_flags(starts_ref, chunk)
         raw_refs = (raw0_ref, raw1_ref)
         _, pieces = convolved(raw_refs, place_ref, starts, taps_ref, chunk, row_index)
@@ -254,7 +256,7 @@
     inverses = inverse_lower(stricts)
     joined = [mul(inverse, pair) for inverse, (pair, _, _, _) in zip(inverses, kept)]
     both = [mul(stack, join) for join, (_, stack, _, _) in zip(joined, kept)]
-    for member in range(BATCH):
+    for member in range(PREPARE_BATCH):
         _, _, span, faded = kept[member]
         inv_ref[member] = inverses[member]
         uw_ref[member] = joined[member]
@@ -283,16 +285,16 @@
 
 def prepare(place, starts, params, raw0, raw1, taps):
     chunks = place.shape[1]
-    square = (BATCH, CHUNK, CHUNK)
-    wide = (BATCH, CHUNK, 2 * CHUNK)
-    kinds = [((BATCH, 8, CHUNK), jnp.float32), (square, jnp.float32), (square, jnp.float32), (square, jnp.float32),
+    square = (PREPARE_BATCH, CHUNK, CHUNK)
+    wide = (PREPARE_BATCH, CHUNK, 2 * CHUNK)
+    kinds = [((PREPARE_BATCH, 8, CHUNK), jnp.float32), (square, jnp.float32), (square, jnp.float32), (square, jnp.float32),
              (wide, jnp.float32), (wide, jnp.bfloat16), (wide, jnp.bfloat16), (square, jnp.float32),
              (square, jnp.float32), (square, jnp.float32)]
     return pl.pallas_call(
         prepare_kernel,
         grid_spec=pltpu.PrefetchScalarGridSpec(
             num_scalar_prefetch=3,
-            grid=(chunks // BATCH,),
+            grid=(chunks // PREPARE_BATCH,),
             in_specs=[whole(raw0.shape), whole(raw1.shape), whole(taps.shape)],
             out_specs=[per_batch(shape) for shape, _ in kinds],
         ),
@@ -314,8 +316,8 @@
         state_ref[...] = jnp.zeros_like(state_ref)
 
     state = state_ref[...]
-    for member in range(BATCH):
-        chunk = pl.program_id(0) * BATCH + member
+    for member in range(SCAN_BATCH):
+        chunk = pl.program_id(0) * SCAN_BATCH + member
         state_out_ref[member] = state
         pair = right_pair(state)
         core = mul_pairs(left_pair(r_ref[member]), pair) + pu_ref[member]
@@ -334,13 +336,13 @@
 
 def scan_states(place, m, b, r, pu, raw0, raw1, gain):
     chunks = m.shape[0]
-    square = (BATCH, CHUNK, CHUNK)
-    wide = (BATCH, CHUNK, 2 * CHUNK)
+    square = (SCAN_BATCH, CHUNK, CHUNK)
+    wide = (SCAN_BATCH, CHUNK, 2 * CHUNK)
     return pl.pallas_call(
         scan_kernel,
         grid_spec=pltpu.PrefetchScalarGridSpec(
             num_scalar_prefetch=1,
-            grid=(chunks // BATCH,),
+            grid=(chunks // SCAN_BATCH,),
             in_specs=[per_batch(wide), per_batch(square), per_batch(square), per_batch(square),
                       gate_columns(raw0), gate_columns(raw1), whole((1, CHUNK))],
             out_specs=[per_batch(square)] * 3,
@@ -366,8 +368,8 @@
     gain = gain_ref[...]
     dgain = jnp.zeros((8, CHUNK), jnp.float32)
     terms = []
-    for member in reversed(range(BATCH)):
-        chunk = (pl.num_programs(0) - 1 - step) * BATCH + member
+    for member in reversed(range(SCAN_BATCH)):
+        chunk = (pl.num_programs(0) - 1 - step) * SCAN_BATCH + member
         core = core_ref[member]
         raw_gate = gate_rows_of((gate0_ref, gate1_ref), place_ref, chunk)
         dmixed = dmixed_ref[member].astype(jnp.float32)
@@ -393,14 +395,14 @@
 
 def back_scan(place, mt, r, core, raw0, raw1, dmixed, gain):
     chunks = mt.shape[0]
-    square = (BATCH, CHUNK, CHUNK)
-    wide = (BATCH, CHUNK, 2 * CHUNK)
-    turned = partial(per_batch, turned=True, steps=chunks // BATCH)
+    square = (SCAN_BATCH, CHUNK, CHUNK)
+    wide = (SCAN_BATCH, CHUNK, 2 * CHUNK)
+    turned = partial(per_batch, turned=True, steps=chunks // SCAN_BATCH)
     return pl.pallas_call(
         back_scan_kernel,
         grid_spec=pltpu.PrefetchScalarGridSpec(
             num_scalar_prefetch=1,
-            grid=(chunks // BATCH,),
+            grid=(chunks // SCAN_BATCH,),
             in_specs=[turned(wide), turned(square), turned(square),
                       gate_columns(raw0), gate_columns(raw1), turned(square), whole((1, CHUNK))],
             out_specs=[turned(square), turned(square), turned(square), whole((8, CHUNK))],
@@ -433,10 +435,10 @@
         dparams_ref[...] = jnp.zeros_like(dparams_ref)
 
     raw_refs = (raw0_ref, raw1_ref)
-    members = range(BATCH)
+    members = range(BACK_BATCH)
     setups = []
     for member in members:
-        chunk = (pl.num_programs(0) - 1 - step) * BATCH + member
+        chunk = (pl.num_programs(0) - 1 - step) * BACK_BATCH + member
         starts = start_flags(starts_ref, chunk)
         keeps, pieces = convolved(raw_refs, place_ref, starts, taps_ref, chunk, row_index)
         queries, keys_in, values_in, q_scale, k_scale = normed_qkv(pieces)
@@ -507,7 +509,7 @@
         kind = row_index[:8]
         dtotal = jnp.where(kind == 0, turned - flow_rows, 0.0)
         dlog = spread_sum(dtotal, lower.astype(jnp.float32))[0:1]
-        chunk = (pl.num_programs(0) - 1 - step) * BATCH + i
+        chunk = (pl.num_programs(0) - 1 - step) * BACK_BATCH + i
         pair = jnp.transpose(head_rows(raw_refs, place_ref, chunk, 4))[:8]
         inside = pair[0:1] + params_ref[1, 0]
         rate = -jnp.exp(params_ref[0, 0] + jnp.zeros((1, CHUNK), jnp.float32))
@@ -556,16 +558,16 @@
 
 def back(place, starts, params, raw0, raw1, rows, taps, inverse, kkf, inner, joined, states, dstates, dcore, dgate):
     chunks = rows.shape[0]
-    square = (BATCH, CHUNK, CHUNK)
-    wide = (BATCH, CHUNK, 2 * CHUNK)
-    turned = partial(per_batch, turned=True, steps=chunks // BATCH)
+    square = (BACK_BATCH, CHUNK, CHUNK)
+    wide = (BACK_BATCH, CHUNK, 2 * CHUNK)
+    turned = partial(per_batch, turned=True, steps=chunks // BACK_BATCH)
     draw = (2,) + raw0.shape
     return pl.pallas_call(
         back_kernel,
         grid_spec=pltpu.PrefetchScalarGridSpec(
             num_scalar_prefetch=3,
-            grid=(chunks // BATCH,),
-            in_specs=[whole(raw0.shape), whole(raw1.shape), turned((BATCH, 8, CHUNK)), whole(taps.shape),
+            grid=(chunks // BACK_BATCH,),
+            in_specs=[whole(raw0.shape), whole(raw1.shape), turned((BACK_BATCH, 8, CHUNK)), whole(taps.shape),
                       turned(square), turned(square), turned(square), turned(wide), turned(square),
                       turned(square), turned(square), turned(square)],
             out_specs=[whole(raw0.shape), whole(raw0.shape), whole((3, 4, CHUNK)), whole((8, CHUNK))],
@@ -1345,7 +1347,7 @@
 
     gu_arrived = [take_yx(pair_gu, k, 0) for k in (1, 2, 3)]
 
-    out_heads = lax.all_gather(after(mine_one[:, used:], normed1_own), "head")
+    out_heads = lax.all_gather(mine_one[:, used:], "head")
     prepared = prepare(place, starts, gate_params, raw0, raw1, taps)
     mixed, kept = mixer_forward(place, prepared, raw0, raw1, out_gain_row)
     mixed, gu_arrived, out_heads, pair_down = lax.optimization_barrier((mixed, gu_arrived, out_heads, pair_down))
@@ -1412,15 +1414,15 @@
     )
     half_rows = (2 * SIDE, width)
     in_kept, in_sent = ring_parts(in_arrived)
+    fed_sums = whole_call(
+        side_sum_kernel, [shaped(half_rows)] + [shaped(half_rows, jnp.bfloat16)] * 3, "side_sum", (), fed_near, after(fed_crossed, sent)
+    )
     arrived, first_arrived = reduce_arrivals(
-        dnormed1[1:4], dnormed1[5], beside=(feed_kept, feed_sent, in_kept, in_sent, sent, fed_crossed)
+        dnormed1[1:4], dnormed1[5], beside=(feed_kept, feed_sent, in_kept, in_sent, sent, *fed_sums)
     )
     parts = reduce_parts(dnormed1[0], dnormed1[4], arrived)
     dnormed1_pieces = reduce_end(parts)
-    fed_crossed, feed_sent, in_sent = lax.optimization_barrier((fed_crossed, feed_sent, in_sent, parts))[:3]
-    fed_sums = whole_call(
-        side_sum_kernel, [shaped(half_rows)] + [shaped(half_rows, jnp.bfloat16)] * 3, "side_sum", (), fed_near, fed_crossed
-    )
+    fed_sums, feed_sent, in_sent = lax.optimization_barrier((fed_sums, feed_sent, in_sent, parts))[:3]
     fed_pieces = [fed_sums[0]] + [take_zx(fed_sums[k], -k, 0) for k in (1, 2, 3)]
     one_total = in_kept + wide(take_yx(in_sent, 0, 1))
     got = lax.all_to_all(after(sent, in_arrived, first_arrived), "dp", 0, 0, tiled=False)

time: 513 us -> 508 us (level)
    ppermute x42, waiting for transfers between devices: 45.7 us -> 53.7 us  [from_head(): lax.ppermute(value, 'head', exchange_perm(16, (dz, dx, dc), (4, 2, 2)))]
    unnamed x96 -> x94, local copies, waits for them, and re-layouts: 15.9 us -> 16.7 us
  transfers between devices with their start and end apart: 61 -> 61, of which waited for: 22 -> 28; matrix products, arithmetic and copies ran while one was open for 4% -> 4% of each run, Pallas kernels for 34% -> 34%
where the time goes in v4:
time: 508 us; the launch traced here: 500 us
  Pallas kernels  223 us (44%)
  starting transfers between devices  106 us (21%)
  waiting for transfers between devices  98.7 us (19%)
  local copies, waits for them, and re-layouts  27.6 us (5%)
  blocking collectives  16.4 us (3%)
  between operations  14.8 us (3%)
  other arithmetic  14.6 us (3%)
    ppermute x42, starting transfers between devices, from_head(): lax.ppermute(value, 'head', exchange_perm(16, (dz, dx, dc), (4, 2, 2)))  54.4 us
    ppermute x42, waiting for transfers between devices, from_head(): lax.ppermute(value, 'head', exchange_perm(16, (dz, dx, dc), (4, 2, 2)))  53.7 us
    pallas_call x2, Pallas kernels, feed(): pl.pallas_call(partial(feed_kernel, tuple(halves), len(pieces), bool(earl...  41.1 us
    pallas_call x10, Pallas kernels, whole_call(): pl.pallas_call(kernel, grid_spec=pltpu.PrefetchScalarGridSpec(num_scalar_...  31.3 us
    pallas_call x1, Pallas kernels, back(): pl.pallas_call(back_kernel, grid_spec=pltpu.PrefetchScalarGridSpec(num_sc...  24.1 us
    ppermute x10, waiting for transfers between devices, from_dp(): return lax.ppermute(value, 'dp', exchange_perm(8, (dy, dx), (4, 2)))  23.1 us
    ppermute x10, starting transfers between devices, from_dp(): return lax.ppermute(value, 'dp', exchange_perm(8, (dy, dx), (4, 2)))  19.4 us
    pallas_call x1, Pallas kernels, feed_grads(): pl.pallas_call(feed_grad_kernel, grid=(width // GROUP,), in_specs=specs,...  18 us
  transfers between devices with their start and end apart: 61, of which 28 were waited for; matrix products, arithmetic and copies ran while one was open for 4% of the time, Pallas kernels for 34%

profile of v4, /device:TPU:1, one launch (start us, length us, event | category | flops | bytes accessed | tf_op | source)
XLA Modules:
  0.0 500.5 jit_solution(4959652751307207605)
XLA Ops:
  29.1 5.1 %collective-permute-done.2 = bf16[48,2048]{1,0:T(8,128)(2,1)S(1)} collective-permute-done((bf16[48,2048]{1,0:T(8,128)(2,1)S(1)}, bf16[48,2048]{1,0:T(8,128)(2,1)S(1)}, u32[]{:S(2)}, u32[]{:S(2)}) %collective-permute-start.2) | collective-permute-done | bytes 196640 | tf_op jit(solution)/shard_map/ppermute | solution.py:629
  51.8 22.8 %collective-permute-done.9.mate_ref = bf16[256,1152]{1,0:T(8,128)(2,1)S(1)} collective-permute-done((bf16[256,1152]{1,0:T(8,128)(2,1)}, bf16[256,1152]{1,0:T(8,128)(2,1)S(1)}, u32[]{:S(2)}, u32[]{:S(2)}) %collective-permute-start.9) | collective-permute-done | bytes 589856 | tf_op jit(solution)/shard_map/ppermute | solution.py:633
  98.2 12.0 %project.1 = (f32[1024,640]{1,0:T(8,128)}, f32[1024,640]{1,0:T(8,128)}) custom-call(bf16[1024,2048]{1,0:T(8,128)(2,1)} %join.1.own_ref, bf16[1024,2048]{1,0:T(8,128)(2,1)} %collective-permute-done.10.other_ref, bf16[2048,768]{1,0:T(8,128)(2,1)} %bitcast.36), custom_call_target="tpu_custom_call" | custom-call | flops 5000000 | bytes 1024 | tf_op jit(solution)/shard_map/project/pallas_call | solution.py:905
  110.2 15.7 %prepare.1 = (f32[16,8,128]{2,1,0:T(8,128)}, f32[16,128,128]{2,1,0:T(8,128)}, f32[16,128,128]{2,1,0:T(8,128)}, f32[16,128,128]{2,1,0:T(8,128)}, f32[16,128,256]{...) custom-call(s32[3,16]{1,0:T(4,128)} %pad_add_fusion.place_ref, ...), custom_call_target="tpu_custom_call" | custom-call | flops 18000000 | bytes 1024 | tf_op jit(solution)/shard_map/prepare/pallas_call | solution.py:293
  125.9 7.1 %scan_states.1 = (f32[16,128,128]{2,1,0:T(8,128)}, f32[16,128,128]{2,1,0:T(8,128)}, bf16[16,128,128]{2,1,0:T(8,128)(2,1)}) custom-call(s32[3,16]{1,0:T(4,128)} %pad_add_fusion.place_ref, bf16[16,128,256]{2,1,0:T(8,128)(2,1)} %get-tuple-element.233.m_ref, f32[16,128,128]{2,1,0:T(8,128)} %get-tuple-element.234.b_ref, ...), custom_call_target="tpu_custom_call" | custom-call | flops 7000000 | bytes 1024 | tf_op jit(solution)/shard_map/scan_states/pallas_call | solution.py:341
  135.2 5.2 %all-to-all-start.1 = ((bf16[16,128,128]{2,1,0:T(8,128)(2,1)}), bf16[16,128,128]{2,1,0:T(8,128)(2,1)S(1)}, u32[]{:S(2)}, u32[]{:S(2)}) async-start(bf16[16,128,128]{2,1,0:T(8,128)(2,1)} %get-tuple-element.241), calls=%async_computation.1 | async-start | bytes 1048576 | tf_op jit(solution)/shard_map/all_to_all | solution.py:1356
  151.1 8.4 %attend.1 = (f32[128,2048]{1,0:T(8,128)}, bf16[128,2048]{1,0:T(8,128)(2,1)}) custom-call(s32[2,8]{1,0:T(2,128)} %pad_add_fusion.1.heads_ref, bf16[16,128,128]{2,1,0:T(8,128)(2,1)} %copy-done.8, bf16[16,2048,128]{2,1,0:T(8,128)(2,1)} %bitcast.26, bf16[16,2048,128]{2,1,0:T(8,128)(2,1)} %bitcast.27, bf16[16,2048,128]{2,1,0:T(8,128)(2,1)} %bitcast.28, ...), custom_call_target="tpu_custom_call" | custom-call | flops 10000000 | bytes 1024 | tf_op jit(solution)/shard_map/attend/pallas_call | solution.py:1068
  174.1 12.4 %collective-permute-done.16 = bf16[64,2048]{1,0:T(8,128)(2,1)S(1)} collective-permute-done((bf16[64,2048]{1,0:T(8,128)(2,1)S(1)}, bf16[64,2048]{1,0:T(8,128)(2,1)S(1)}, u32[]{:S(2)}, u32[]{:S(2)}) %collective-permute-start.16) | collective-permute-done | bytes 262176 | tf_op jit(solution)/shard_map/ppermute | solution.py:629
  193.7 6.0 %collective-permute-done.26.refs_11_.refs_17_ = bf16[2048,384]{1,0:T(8,128)(2,1)S(1)} collective-permute-done((bf16[2048,384]{1,0:T(8,128)(2,1)S(1)}, bf16[2048,384]{1,0:T(8,128)(2,1)S(1)}, u32[]{:S(2)}, u32[]{:S(2)}) %collective-permute-start.26) | collective-permute-done | bytes 1572896 | tf_op jit(solution)/shard_map/ppermute | solution.py:629
  204.4 15.2 %feed.2 = (bf16[128,2048]{1,0:T(8,128)(2,1)}, bf16[256,2048]{1,0:T(8,128)(2,1)}, bf16[128,2048]{1,0:T(8,128)(2,1)}, bf16[256,2048]{1,0:T(8,128)(2,1)}, bf16[384,...) custom-call(s32[2,8]{1,0:T(2,128)} %pad_add_fusion.1.heads_ref, ...), custom_call_target="tpu_custom_call" | custom-call | flops 28000000 | bytes 1024 | tf_op jit(solution)/shard_map/feed/pallas_call | solution.py:1221
  223.9 25.8 %feed.3 = (bf16[512,2048]{1,0:T(8,128)(2,1)}, bf16[512,2048]{1,0:T(8,128)(2,1)}, bf16[128,2048]{1,0:T(8,128)(2,1)}, bf16[128,2048]{1,0:T(8,128)(2,1)}, bf16[128,...) custom-call(s32[2,8]{1,0:T(2,128)} %pad_add_fusion.1.heads_ref, ...), custom_call_target="tpu_custom_call" | custom-call | flops 28000000 | bytes 1024 | tf_op jit(solution)/shard_map/feed/pallas_call | solution.py:1221
  250.4 7.2 %collective-permute-start.27 = (bf16[128,2048]{1,0:T(8,128)(2,1)}, bf16[128,2048]{1,0:T(8,128)(2,1)S(1)}, u32[]{:S(2)}, u32[]{:S(2)}) collective-permute-start(bf16[128,2048]{1,0:T(8,128)(2,1)} %get-tuple-element.275), channel_id=1, source_target_pairs={{12,0},{13,1},{14,2},{15,3},{0,4},{1,5},{2,6},{3,7},{4,8},{5,9},{6... | collective-permute-start | bytes 1572872 | tf_op jit(solution)/shard_map/ppermute | solution.py:629
  260.0 18.0 %feed_grads.1 = (bf16[2048,1152]{1,0:T(8,128)(2,1)}, bf16[2048,1152]{1,0:T(8,128)(2,1)}) custom-call(bf16[384,2048]{1,0:T(8,128)(2,1)} %get-tuple-element.290.refs_0_, bf16[384,2048]{1,0:T(8,128)(2,1)} %get-tuple-element.291.refs_1_, bf16[384,1536]{1,0:T(8,128)(2,1)} %get-tuple-element.292.refs_2_, bf16[384,768]{1,0:T(8,128)(2,1)} %get-tuple-element.293.refs_3_, ...), custom_call_target="tpu_custom_call" | custom-call | flops 12000000 | bytes 1024 | tf_op jit(solution)/shard_map/feed_grads/pallas_call | solution.py:960
  294.5 5.8 %add_convert_fusion = bf16[2048,1152]{1,0:T(8,128)(2,1)} fusion(bf16[2048,1152]{1,0:T(8,128)(2,1)S(1)} %collective-permute-done.35, bf16[2048,1152]{1,0:T(8,128)(2,1)} %get-tuple-element.307), kind=kLoop, calls=%fused_computation | loop fusion | flops 9437184 | bytes 14155776 | tf_op jit(solution)/shard_map/convert_element_type | solution.py:666
  303.9 8.7 %middle.1 = (f32[128,2048]{1,0:T(8,128)}, bf16[128,2048]{1,0:T(8,128)(2,1)}, f32[1,2048]{1,0:T(1,128)}, bf16[16,128,128]{2,1,0:T(8,128)(2,1)}) custom-call(s32[2,8]{1,0:T(2,128)} %pad_add_fusion.1.heads_ref, f32[64,2048]{1,0:T(8,128)} %get-tuple-element.300.refs_0_, bf16[64,2048]{1,0:T(8,128)(2,1)} %copy-done.28, f32[64,2048]{1,0:T(8,128)} %get-tuple-element.302.refs_2_, ...), custom_call_target="tpu_custom_call" | custom-call | flops 10000000 | bytes 1024 | tf_op jit(solution)/shard_map/middle/pallas_call | solution.py:1113
  313.8 16.4 %all_to_all.35.dmixed_ref = bf16[16,128,128]{2,1,0:T(8,128)(2,1)} all-to-all(bf16[16,128,128]{2,1,0:T(8,128)(2,1)} %get-tuple-element.310), channel_id=1, replica_groups=mesh['dp'=8,'head'=16] {'head'}, dimensions={0} | all-to-all | bytes 1048576 | tf_op jit(solution)/shard_map/all_to_all | solution.py:1380
  330.2 5.0 %all-to-all-start.3 = ((bf16[4,512,1152]{2,1,0:T(8,128)(2,1)}), bf16[4,512,1152]{2,1,0:T(8,128)(2,1)}, u32[]{:S(2)}, u32[]{:S(2)}) async-start(bf16[4,512,1152]{2,1,0:T(8,128)(2,1)} %bitcast.40), calls=%async_computation.3 | async-start | bytes 9437184 | tf_op jit(solution)/shard_map/all_to_all | solution.py:840
  335.3 7.4 %back_scan.1 = (f32[16,128,128]{2,1,0:T(8,128)}, f32[16,128,128]{2,1,0:T(8,128)}, bf16[16,128,128]{2,1,0:T(8,128)(2,1)}, f32[8,128]{1,0:T(8,128)}) custom-call(s32[3,16]{1,0:T(4,128)} %pad_add_fusion.place_ref, bf16[16,128,256]{2,1,0:T(8,128)(2,1)} %get-tuple-element.272.mt_ref, f32[16,128,128]{2,1,0:T(8,128)} %get-tuple-element.235.r_ref, ...), custom_call_target="tpu_custom_call" | custom-call | flops 7000000 | bytes 1024 | tf_op jit(solution)/shard_map/back_scan/pallas_call | solution.py:401
  342.6 24.1 %back.1 = (bf16[1024,640]{1,0:T(8,128)(2,1)}, bf16[1024,640]{1,0:T(8,128)(2,1)}, f32[3,4,128]{2,1,0:T(4,128)}, f32[8,128]{1,0:T(8,128)}) custom-call(s32[3,16]{1,0:T(4,128)} %pad_add_fusion.place_ref, s32[32]{0:T(128)} %or_convert_fusion.starts_ref, f32[2,1]{1,0:T(2,128)} %copy.73.params_ref, f32[1024,640]{1,0:T(8,128)} %get-tuple-element.231.raw0_ref.gate0_ref, ...), custom_call_target="tpu_custom_call" | custom-call | flops 24000000 | bytes 1024 | tf_op jit(solution)/shard_map/back/pallas_call | solution.py:565
  368.8 13.0 %in_grads.1 = (bf16[4,512,640]{2,1,0:T(8,128)(2,1)}, f32[8,8,256]{2,1,0:T(8,128)}) custom-call(bf16[1024,2048]{1,0:T(8,128)(2,1)} %join.1.own_ref, bf16[1024,2048]{1,0:T(8,128)(2,1)} %collective-permute-done.10.other_ref, bf16[1024,640]{1,0:T(8,128)(2,1)} %get-tuple-element.324.draw0_ref.own_ref, bf16[1024,640]{1,0:T(8,128)(2,1)} %get-tuple-element.325.draw1_ref, ...), custom_call_target="tpu_custom_call" | custom-call | flops 8000000 | bytes 1024 | tf_op jit(solution)/shard_map/in_grads/pallas_call | solution.py:987
  382.9 13.1 %unproject.1 = (bf16[160,2048]{1,0:T(8,128)(2,1)}, bf16[160,2048]{1,0:T(8,128)(2,1)}, bf16[160,2048]{1,0:T(8,128)(2,1)}, bf16[160,2048]{1,0:T(8,128)(2,1)}, bf16...) custom-call(bf16[1024,640]{1,0:T(8,128)(2,1)} %get-tuple-element.324.draw0_ref.own_ref, bf16[1024,640]{1,0:T(8,128)(2,1)} %copy-done.11, ...), custom_call_target="tpu_custom_call" | custom-call | flops 8000000 | bytes 1024 | tf_op jit(solution)/shard_map/unproject/pallas_call | solution.py:927
  404.8 8.5 %out_grads.1.out_grad_ref = bf16[8,256,128]{2,1,0:T(8,128)(2,1)} custom-call(bf16[2048,2048]{1,0:T(8,128)(2,1)} %all-gather.7.cloned.1.call-done.rows_ref, bf16[2048,128]{1,0:T(8,128)(2,1)} %bitcast.41), custom_call_target="tpu_custom_call" | custom-call | flops 6000000 | bytes 1024 | tf_op jit(solution)/shard_map/out_grads/pallas_call | solution.py:1008
  424.0 8.1 %all-to-all-done.4.arrived_ref = bf16[4,512,640]{2,1,0:T(8,128)(2,1)S(1)} async-done(((bf16[4,512,640]{2,1,0:T(8,128)(2,1)}), bf16[4,512,640]{2,1,0:T(8,128)(2,1)S(1)}, u32[]{:S(2)}, u32[]{:S(2)}) %all-to-all-start.4) | async-done | bytes 2621472 | tf_op jit(solution)/shard_map/all_to_all | solution.py:840
  468.1 9.5 %all-to-all-start.6 = ((f32[16,40,128]{2,1,0:T(8,128)}), f32[16,40,128]{2,1,0:T(8,128)S(1)}, u32[]{:S(2)}, u32[]{:S(2)}) async-start(f32[16,40,128]{2,1,0:T(8,128)} %broadcast_in_dim.35), calls=%async_computation.6 | async-start | bytes 655360 | tf_op jit(solution)/shard_map/all_to_all | solution.py:845
  (271 shorter events, 205.2 us)
Async XLA Ops:
  40.2 39.9 %all-to-all-start = ((bf16[4,2,256,768]{3,2,1,0:T(8,128)(2,1)}), bf16[4,2,256,768]{3,2,1,0:T(8,128)(2,1)S(1)}, u32[]{:S(2)}, u32[]{:S(2)}) async-start(bf16[4,2,256,768]{3,2,1,0:T(8,128)(2,1)} %spread_pair.1), calls=%async_computation | async-start | bytes 6291456 | tf_op jit(solution)/shard_map/all_to_all | solution.py:829
  44.3 90.9 %all-gather.9.cloned.1.call-start = ((), (), s32[]{:S(2)}) async-start(), calls=%async_computation.9 | async-start | bytes 8912896 | tf_op jit(solution)/shard_map/all_gather | solution.py:1350
  44.3 34.9 %collective-permute-start.8 = (bf16[192,2048]{1,0:T(8,128)(2,1)}, bf16[192,2048]{1,0:T(8,128)(2,1)}, u32[]{:S(2)}, u32[]{:S(2)}) collective-permute-start(bf16[192,2048]{1,0:T(8,128)(2,1)} %pad_maximum_fusion.1.refs_4_), channel_id=1, source_target_pairs={{2,0},{3,1},{0,2},{1,3},{6,4},{7,5},{4,6},{5,7},{10,8},{11,9},{8,1... | collective-permute-start | bytes 2359304 | tf_op jit(solution)/shard_map/ppermute | solution.py:629
  45.5 29.1 %collective-permute-start.7 = (bf16[160,2048]{1,0:T(8,128)(2,1)}, bf16[160,2048]{1,0:T(8,128)(2,1)S(1)}, u32[]{:S(2)}, u32[]{:S(2)}) collective-permute-start(bf16[160,2048]{1,0:T(8,128)(2,1)} %pad_maximum_fusion.2.refs_0_), channel_id=1, source_target_pairs={{12,0},{13,1},{14,2},{15,3},{0,4},{1,5},{2,6},{3,7},{4,8},{5,9},{6... | collective-permute-start | bytes 1966088 | tf_op jit(solution)/shard_map/ppermute | solution.py:629
  47.1 30.2 %collective-permute-start.6 = (bf16[160,2048]{1,0:T(8,128)(2,1)}, bf16[160,2048]{1,0:T(8,128)(2,1)S(1)}, u32[]{:S(2)}, u32[]{:S(2)}) collective-permute-start(bf16[160,2048]{1,0:T(8,128)(2,1)} %pad_maximum_fusion.2.refs_0_), channel_id=1, source_target_pairs={{8,0},{9,1},{10,2},{11,3},{12,4},{13,5},{14,6},{15,7},{0,8},{1,9},... | collective-permute-start | bytes 1966088 | tf_op jit(solution)/shard_map/ppermute | solution.py:629
  81.0 123.4 %all-gather.5.cloned.1.call-start = ((), (), s32[]{:S(2)}) async-start(), calls=%async_computation.7 | async-start | bytes 8912896 | tf_op jit(solution)/shard_map/all_gather | solution.py:1355
  92.3 40.8 %collective-permute-start.13 = (bf16[512,768]{1,0:T(8,128)(2,1)}, bf16[512,768]{1,0:T(8,128)(2,1)}, u32[]{:S(2)}, u32[]{:S(2)}) collective-permute-start(bf16[512,768]{1,0:T(8,128)(2,1)} %get-tuple-element.239.refs_0_), channel_id=1, source_target_pairs={{96,0},{112,16},{0,32},{16,48},{32,64},{48,80},{64,96},{80,112},{9... | collective-permute-start | bytes 2359304 | tf_op jit(solution)/shard_map/ppermute | solution.py:633
  93.0 40.0 %collective-permute-start.12 = (bf16[512,768]{1,0:T(8,128)(2,1)}, bf16[512,768]{1,0:T(8,128)(2,1)}, u32[]{:S(2)}, u32[]{:S(2)}) collective-permute-start(bf16[512,768]{1,0:T(8,128)(2,1)} %get-tuple-element.239.refs_0_), channel_id=1, source_target_pairs={{64,0},{80,16},{96,32},{112,48},{0,64},{16,80},{32,96},{48,112},{6... | collective-permute-start | bytes 2359304 | tf_op jit(solution)/shard_map/ppermute | solution.py:633
  95.4 37.7 %collective-permute-start.11 = (bf16[512,768]{1,0:T(8,128)(2,1)}, bf16[512,768]{1,0:T(8,128)(2,1)}, u32[]{:S(2)}, u32[]{:S(2)}) collective-permute-start(bf16[512,768]{1,0:T(8,128)(2,1)} %get-tuple-element.239.refs_0_), channel_id=1, source_target_pairs={{32,0},{48,16},{64,32},{80,48},{96,64},{112,80},{0,96},{16,112},{3... | collective-permute-start | bytes 2359304 | tf_op jit(solution)/shard_map/ppermute | solution.py:633
  140.5 255.5 %all-gather.7.cloned.1.call-start = ((), (), s32[]{:S(2)}) async-start(), calls=%async_computation.8 | async-start | bytes 8912896 | tf_op jit(solution)/shard_map/all_gather | solution.py:1385
  191.7 32.2 %collective-permute-start.24 = (bf16[256,2048]{1,0:T(8,128)(2,1)S(1)}, bf16[256,2048]{1,0:T(8,128)(2,1)}, u32[]{:S(2)}, u32[]{:S(2)}) collective-permute-start(bf16[256,2048]{1,0:T(8,128)(2,1)S(1)} %pad_maximum_fusion.refs_1_), channel_id=1, source_target_pairs={{2,0},{3,1},{0,2},{1,3},{6,4},{7,5},{4,6},{5,7},{10,8},{11,9},{8,1... | collective-permute-start | bytes 3145736 | tf_op jit(solution)/shard_map/ppermute | solution.py:629
  192.3 31.6 %collective-permute-start.22 = (bf16[128,2048]{1,0:T(8,128)(2,1)S(1)}, bf16[128,2048]{1,0:T(8,128)(2,1)}, u32[]{:S(2)}, u32[]{:S(2)}) collective-permute-start(bf16[128,2048]{1,0:T(8,128)(2,1)S(1)} %pad_maximum_fusion.3.refs_0_), channel_id=1, source_target_pairs={{8,0},{9,1},{10,2},{11,3},{12,4},{13,5},{14,6},{15,7},{0,8},{1,9},... | collective-permute-start | bytes 1572872 | tf_op jit(solution)/shard_map/ppermute | solution.py:629
  249.7 31.2 %collective-permute-start.30 = (bf16[256,2048]{1,0:T(8,128)(2,1)}, bf16[256,2048]{1,0:T(8,128)(2,1)S(1)}, u32[]{:S(2)}, u32[]{:S(2)}) collective-permute-start(bf16[256,2048]{1,0:T(8,128)(2,1)} %get-tuple-element.278), channel_id=1, source_target_pairs={{2,0},{3,1},{0,2},{1,3},{6,4},{7,5},{4,6},{5,7},{10,8},{11,9},{8,1... | collective-permute-start | bytes 3145736 | tf_op jit(solution)/shard_map/ppermute | solution.py:629
  312.7 54.0 %collective-permute-start.37 = (bf16[2048,768]{1,0:T(8,128)(2,1)S(1)}, bf16[2048,768]{1,0:T(8,128)(2,1)}, u32[]{:S(2)}, u32[]{:S(2)}) collective-permute-start(bf16[2048,768]{1,0:T(8,128)(2,1)S(1)} %bitcast.39), channel_id=1, source_target_pairs={{1,0},{0,1},{3,2},{2,3},{5,4},{4,5},{7,6},{6,7},{9,8},{8,9},{11,10... | collective-permute-start | bytes 9437192 | tf_op jit(solution)/shard_map/ppermute | solution.py:629
  330.2 65.7 %all-to-all-start.3 = ((bf16[4,512,1152]{2,1,0:T(8,128)(2,1)}), bf16[4,512,1152]{2,1,0:T(8,128)(2,1)}, u32[]{:S(2)}, u32[]{:S(2)}) async-start(bf16[4,512,1152]{2,1,0:T(8,128)(2,1)} %bitcast.40), calls=%async_computation.3 | async-start | bytes 9437184 | tf_op jit(solution)/shard_map/all_to_all | solution.py:840
  368.8 47.5 %collective-permute-start.36 = (bf16[512,2048]{1,0:T(8,128)(2,1)}, bf16[512,2048]{1,0:T(8,128)(2,1)}, u32[]{:S(2)}, u32[]{:S(2)}) collective-permute-start(bf16[512,2048]{1,0:T(8,128)(2,1)} %get-tuple-element.312), channel_id=1, source_target_pairs={{2,0},{3,1},{0,2},{1,3},{6,4},{7,5},{4,6},{5,7},{10,8},{11,9},{8,1... | collective-permute-start | bytes 6291464 | tf_op jit(solution)/shard_map/ppermute | solution.py:629
  395.9 36.2 %all-to-all-start.4 = ((bf16[4,512,640]{2,1,0:T(8,128)(2,1)}), bf16[4,512,640]{2,1,0:T(8,128)(2,1)S(1)}, u32[]{:S(2)}, u32[]{:S(2)}) async-start(bf16[4,512,640]{2,1,0:T(8,128)(2,1)} %get-tuple-element.350), calls=%async_computation.4 | async-start | bytes 5242880 | tf_op jit(solution)/shard_map/all_to_all | solution.py:840
  400.4 36.0 %collective-permute-start.42 = (bf16[192,2048]{1,0:T(8,128)(2,1)}, bf16[192,2048]{1,0:T(8,128)(2,1)S(1)}, u32[]{:S(2)}, u32[]{:S(2)}) collective-permute-start(bf16[192,2048]{1,0:T(8,128)(2,1)} %get-tuple-element.356), channel_id=1, source_target_pairs={{2,0},{3,1},{0,2},{1,3},{6,4},{7,5},{4,6},{5,7},{10,8},{11,9},{8,1... | collective-permute-start | bytes 2359304 | tf_op jit(solution)/shard_map/ppermute | solution.py:629
  401.9 34.6 %collective-permute-start.39 = (bf16[160,2048]{1,0:T(8,128)(2,1)}, bf16[160,2048]{1,0:T(8,128)(2,1)}, u32[]{:S(2)}, u32[]{:S(2)}) collective-permute-start(bf16[160,2048]{1,0:T(8,128)(2,1)} %get-tuple-element.353), channel_id=1, source_target_pairs={{12,0},{13,1},{14,2},{15,3},{0,4},{1,5},{2,6},{3,7},{4,8},{5,9},{6... | collective-permute-start | bytes 1966088 | tf_op jit(solution)/shard_map/ppermute | solution.py:629
  401.9 34.6 %collective-permute-start.40 = (bf16[160,2048]{1,0:T(8,128)(2,1)}, bf16[160,2048]{1,0:T(8,128)(2,1)}, u32[]{:S(2)}, u32[]{:S(2)}) collective-permute-start(bf16[160,2048]{1,0:T(8,128)(2,1)} %get-tuple-element.354), channel_id=1, source_target_pairs={{8,0},{9,1},{10,2},{11,3},{12,4},{13,5},{14,6},{15,7},{0,8},{1,9},... | collective-permute-start | bytes 1966088 | tf_op jit(solution)/shard_map/ppermute | solution.py:629
  402.2 34.3 %collective-permute-start.41 = (bf16[160,2048]{1,0:T(8,128)(2,1)}, bf16[160,2048]{1,0:T(8,128)(2,1)}, u32[]{:S(2)}, u32[]{:S(2)}) collective-permute-start(bf16[160,2048]{1,0:T(8,128)(2,1)} %get-tuple-element.355), channel_id=1, source_target_pairs={{4,0},{5,1},{6,2},{7,3},{8,4},{9,5},{10,6},{11,7},{12,8},{13,9},{1... | collective-permute-start | bytes 1966088 | tf_op jit(solution)/shard_map/ppermute | solution.py:629
  450.6 35.7 %collective-permute-start.43 = (bf16[128,2048]{1,0:T(8,128)(2,1)}, bf16[128,2048]{1,0:T(8,128)(2,1)S(1)}, u32[]{:S(2)}, u32[]{:S(2)}) collective-permute-start(bf16[128,2048]{1,0:T(8,128)(2,1)} %get-tuple-element.371), channel_id=1, source_target_pairs={{12,0},{13,1},{14,2},{15,3},{0,4},{1,5},{2,6},{3,7},{4,8},{5,9},{6... | collective-permute-start | bytes 1572872 | tf_op jit(solution)/shard_map/ppermute | solution.py:629
  453.4 32.9 %collective-permute-start.44 = (bf16[128,2048]{1,0:T(8,128)(2,1)}, bf16[128,2048]{1,0:T(8,128)(2,1)}, u32[]{:S(2)}, u32[]{:S(2)}) collective-permute-start(bf16[128,2048]{1,0:T(8,128)(2,1)} %get-tuple-element.372), channel_id=1, source_target_pairs={{8,0},{9,1},{10,2},{11,3},{12,4},{13,5},{14,6},{15,7},{0,8},{1,9},... | collective-permute-start | bytes 1572872 | tf_op jit(solution)/shard_map/ppermute | solution.py:629
  457.9 28.4 %collective-permute-start.45 = (bf16[128,2048]{1,0:T(8,128)(2,1)}, bf16[128,2048]{1,0:T(8,128)(2,1)}, u32[]{:S(2)}, u32[]{:S(2)}) collective-permute-start(bf16[128,2048]{1,0:T(8,128)(2,1)} %get-tuple-element.373), channel_id=1, source_target_pairs={{4,0},{5,1},{6,2},{7,3},{8,4},{9,5},{10,6},{11,7},{12,8},{13,9},{1... | collective-permute-start | bytes 1572872 | tf_op jit(solution)/shard_map/ppermute | solution.py:629
  (79 other events, 915.0 us)
Sparse Core Ops, SparseCore 0:
  81.1 54.0 all-gather.8
  136.9 67.4 all-gather.4
  312.8 55.9 all-gather.6

commit v5 on v4

--- a/solution.py
+++ b/solution.py
@@ -1422,7 +1422,8 @@
     )
     parts = reduce_parts(dnormed1[0], dnormed1[4], arrived)
     dnormed1_pieces = reduce_end(parts)
-    fed_sums, feed_sent, in_sent = lax.optimization_barrier((fed_sums, feed_sent, in_sent, parts))[:3]
+    fed_sums, feed_sent = lax.optimization_barrier((fed_sums, feed_sent, parts))[:2]
+    in_sent = after(in_sent, *dnormed1_pieces)
     fed_pieces = [fed_sums[0]] + [take_zx(fed_sums[k], -k, 0) for k in (1, 2, 3)]
     one_total = in_kept + wide(take_yx(in_sent, 0, 1))
     got = lax.all_to_all(after(sent, in_arrived, first_arrived), "dp", 0, 0, tiled=False)

time: 508 us -> 513 us (level)
    unnamed x94 -> x90, local copies, waits for them, and re-layouts: 16.7 us -> 16 us
  transfers between devices with their start and end apart: 61 -> 61, of which waited for: 28 -> 25; matrix products, arithmetic and copies ran while one was open for 4% -> 4% of each run, Pallas kernels for 34% -> 34%
where the time goes in v5:
time: 513 us; the launch traced here: 506 us
  Pallas kernels  223 us (43%)
  starting transfers between devices  110 us (21%)
  waiting for transfers between devices  100 us (19%)
  local copies, waits for them, and re-layouts  26.9 us (5%)
  blocking collectives  16.4 us (3%)
  other arithmetic  15.5 us (3%)
  between operations  14.8 us (3%)
    ppermute x42, starting transfers between devices, from_head(): lax.ppermute(value, 'head', exchange_perm(16, (dz, dx, dc), (4, 2, 2)))  58.5 us
    ppermute x42, waiting for transfers between devices, from_head(): lax.ppermute(value, 'head', exchange_perm(16, (dz, dx, dc), (4, 2, 2)))  52.7 us
    pallas_call x2, Pallas kernels, feed(): pl.pallas_call(partial(feed_kernel, tuple(halves), len(pieces), bool(earl...  41 us
    pallas_call x10, Pallas kernels, whole_call(): pl.pallas_call(kernel, grid_spec=pltpu.PrefetchScalarGridSpec(num_scalar_...  31.3 us
    pallas_call x1, Pallas kernels, back(): pl.pallas_call(back_kernel, grid_spec=pltpu.PrefetchScalarGridSpec(num_sc...  24.1 us
    ppermute x10, waiting for transfers between devices, from_dp(): return lax.ppermute(value, 'dp', exchange_perm(8, (dy, dx), (4, 2)))  22.8 us
    ppermute x10, starting transfers between devices, from_dp(): return lax.ppermute(value, 'dp', exchange_perm(8, (dy, dx), (4, 2)))  18.9 us
    pallas_call x1, Pallas kernels, feed_grads(): pl.pallas_call(feed_grad_kernel, grid=(width // GROUP,), in_specs=specs,...  18 us
  transfers between devices with their start and end apart: 61, of which 25 were waited for; matrix products, arithmetic and copies ran while one was open for 4% of the time, Pallas kernels for 34%

profile of v5, /device:TPU:1, one launch (start us, length us, event | category | flops | bytes accessed | tf_op | source)
XLA Modules:
  0.0 506.3 jit_solution(16380418228439243218)
XLA Ops:
  29.1 5.1 %collective-permute-done.2 = bf16[48,2048]{1,0:T(8,128)(2,1)S(1)} collective-permute-done((bf16[48,2048]{1,0:T(8,128)(2,1)S(1)}, bf16[48,2048]{1,0:T(8,128)(2,1)S(1)}, u32[]{:S(2)}, u32[]{:S(2)}) %collective-permute-start.2) | collective-permute-done | bytes 196640 | tf_op jit(solution)/shard_map/ppermute | solution.py:629
  51.8 22.8 %collective-permute-done.9.mate_ref = bf16[256,1152]{1,0:T(8,128)(2,1)S(1)} collective-permute-done((bf16[256,1152]{1,0:T(8,128)(2,1)}, bf16[256,1152]{1,0:T(8,128)(2,1)S(1)}, u32[]{:S(2)}, u32[]{:S(2)}) %collective-permute-start.9) | collective-permute-done | bytes 589856 | tf_op jit(solution)/shard_map/ppermute | solution.py:633
  98.2 12.0 %project.1 = (f32[1024,640]{1,0:T(8,128)}, f32[1024,640]{1,0:T(8,128)}) custom-call(bf16[1024,2048]{1,0:T(8,128)(2,1)} %join.1.own_ref, bf16[1024,2048]{1,0:T(8,128)(2,1)} %collective-permute-done.10.other_ref, bf16[2048,768]{1,0:T(8,128)(2,1)} %bitcast.36), custom_call_target="tpu_custom_call" | custom-call | flops 5000000 | bytes 1024 | tf_op jit(solution)/shard_map/project/pallas_call | solution.py:905
  110.2 15.7 %prepare.1 = (f32[16,8,128]{2,1,0:T(8,128)}, f32[16,128,128]{2,1,0:T(8,128)}, f32[16,128,128]{2,1,0:T(8,128)}, f32[16,128,128]{2,1,0:T(8,128)}, f32[16,128,256]{...) custom-call(s32[3,16]{1,0:T(4,128)} %pad_add_fusion.place_ref, ...), custom_call_target="tpu_custom_call" | custom-call | flops 18000000 | bytes 1024 | tf_op jit(solution)/shard_map/prepare/pallas_call | solution.py:293
  125.9 7.1 %scan_states.1 = (f32[16,128,128]{2,1,0:T(8,128)}, f32[16,128,128]{2,1,0:T(8,128)}, bf16[16,128,128]{2,1,0:T(8,128)(2,1)}) custom-call(s32[3,16]{1,0:T(4,128)} %pad_add_fusion.place_ref, bf16[16,128,256]{2,1,0:T(8,128)(2,1)} %get-tuple-element.233.m_ref, f32[16,128,128]{2,1,0:T(8,128)} %get-tuple-element.234.b_ref, ...), custom_call_target="tpu_custom_call" | custom-call | flops 7000000 | bytes 1024 | tf_op jit(solution)/shard_map/scan_states/pallas_call | solution.py:341
  135.2 5.2 %all-to-all-start.1 = ((bf16[16,128,128]{2,1,0:T(8,128)(2,1)}), bf16[16,128,128]{2,1,0:T(8,128)(2,1)S(1)}, u32[]{:S(2)}, u32[]{:S(2)}) async-start(bf16[16,128,128]{2,1,0:T(8,128)(2,1)} %get-tuple-element.241), calls=%async_computation.1 | async-start | bytes 1048576 | tf_op jit(solution)/shard_map/all_to_all | solution.py:1356
  151.0 8.4 %attend.1 = (f32[128,2048]{1,0:T(8,128)}, bf16[128,2048]{1,0:T(8,128)(2,1)}) custom-call(s32[2,8]{1,0:T(2,128)} %pad_add_fusion.1.heads_ref, bf16[16,128,128]{2,1,0:T(8,128)(2,1)} %copy-done.8, bf16[16,2048,128]{2,1,0:T(8,128)(2,1)} %bitcast.26, bf16[16,2048,128]{2,1,0:T(8,128)(2,1)} %bitcast.27, bf16[16,2048,128]{2,1,0:T(8,128)(2,1)} %bitcast.28, ...), custom_call_target="tpu_custom_call" | custom-call | flops 10000000 | bytes 1024 | tf_op jit(solution)/shard_map/attend/pallas_call | solution.py:1068
  174.0 12.5 %collective-permute-done.16 = bf16[64,2048]{1,0:T(8,128)(2,1)S(1)} collective-permute-done((bf16[64,2048]{1,0:T(8,128)(2,1)S(1)}, bf16[64,2048]{1,0:T(8,128)(2,1)S(1)}, u32[]{:S(2)}, u32[]{:S(2)}) %collective-permute-start.16) | collective-permute-done | bytes 262176 | tf_op jit(solution)/shard_map/ppermute | solution.py:629
  193.7 6.0 %collective-permute-done.26.refs_11_.refs_17_ = bf16[2048,384]{1,0:T(8,128)(2,1)S(1)} collective-permute-done((bf16[2048,384]{1,0:T(8,128)(2,1)S(1)}, bf16[2048,384]{1,0:T(8,128)(2,1)S(1)}, u32[]{:S(2)}, u32[]{:S(2)}) %collective-permute-start.26) | collective-permute-done | bytes 1572896 | tf_op jit(solution)/shard_map/ppermute | solution.py:629
  204.4 15.2 %feed.2 = (bf16[128,2048]{1,0:T(8,128)(2,1)}, bf16[256,2048]{1,0:T(8,128)(2,1)}, bf16[128,2048]{1,0:T(8,128)(2,1)}, bf16[256,2048]{1,0:T(8,128)(2,1)}, bf16[384,...) custom-call(s32[2,8]{1,0:T(2,128)} %pad_add_fusion.1.heads_ref, ...), custom_call_target="tpu_custom_call" | custom-call | flops 28000000 | bytes 1024 | tf_op jit(solution)/shard_map/feed/pallas_call | solution.py:1221
  223.8 25.8 %feed.3 = (bf16[512,2048]{1,0:T(8,128)(2,1)}, bf16[512,2048]{1,0:T(8,128)(2,1)}, bf16[128,2048]{1,0:T(8,128)(2,1)}, bf16[128,2048]{1,0:T(8,128)(2,1)}, bf16[128,...) custom-call(s32[2,8]{1,0:T(2,128)} %pad_add_fusion.1.heads_ref, ...), custom_call_target="tpu_custom_call" | custom-call | flops 28000000 | bytes 1024 | tf_op jit(solution)/shard_map/feed/pallas_call | solution.py:1221
  250.4 7.1 %collective-permute-start.27 = (bf16[128,2048]{1,0:T(8,128)(2,1)}, bf16[128,2048]{1,0:T(8,128)(2,1)S(1)}, u32[]{:S(2)}, u32[]{:S(2)}) collective-permute-start(bf16[128,2048]{1,0:T(8,128)(2,1)} %get-tuple-element.275), channel_id=1, source_target_pairs={{12,0},{13,1},{14,2},{15,3},{0,4},{1,5},{2,6},{3,7},{4,8},{5,9},{6... | collective-permute-start | bytes 1572872 | tf_op jit(solution)/shard_map/ppermute | solution.py:629
  259.9 18.0 %feed_grads.1 = (bf16[2048,1152]{1,0:T(8,128)(2,1)}, bf16[2048,1152]{1,0:T(8,128)(2,1)}) custom-call(bf16[384,2048]{1,0:T(8,128)(2,1)} %get-tuple-element.290.refs_0_, bf16[384,2048]{1,0:T(8,128)(2,1)} %get-tuple-element.291.refs_1_, bf16[384,1536]{1,0:T(8,128)(2,1)} %get-tuple-element.292.refs_2_, bf16[384,768]{1,0:T(8,128)(2,1)} %get-tuple-element.293.refs_3_, ...), custom_call_target="tpu_custom_call" | custom-call | flops 12000000 | bytes 1024 | tf_op jit(solution)/shard_map/feed_grads/pallas_call | solution.py:960
  294.5 5.8 %add_convert_fusion = bf16[2048,1152]{1,0:T(8,128)(2,1)} fusion(bf16[2048,1152]{1,0:T(8,128)(2,1)S(1)} %collective-permute-done.35, bf16[2048,1152]{1,0:T(8,128)(2,1)} %get-tuple-element.307), kind=kLoop, calls=%fused_computation | loop fusion | flops 9437184 | bytes 14155776 | tf_op jit(solution)/shard_map/convert_element_type | solution.py:666
  303.9 8.7 %middle.1 = (f32[128,2048]{1,0:T(8,128)}, bf16[128,2048]{1,0:T(8,128)(2,1)}, f32[1,2048]{1,0:T(1,128)}, bf16[16,128,128]{2,1,0:T(8,128)(2,1)}) custom-call(s32[2,8]{1,0:T(2,128)} %pad_add_fusion.1.heads_ref, f32[64,2048]{1,0:T(8,128)} %get-tuple-element.300.refs_0_, bf16[64,2048]{1,0:T(8,128)(2,1)} %copy-done.28, f32[64,2048]{1,0:T(8,128)} %get-tuple-element.302.refs_2_, ...), custom_call_target="tpu_custom_call" | custom-call | flops 10000000 | bytes 1024 | tf_op jit(solution)/shard_map/middle/pallas_call | solution.py:1113
  313.8 16.4 %all_to_all.35.dmixed_ref = bf16[16,128,128]{2,1,0:T(8,128)(2,1)} all-to-all(bf16[16,128,128]{2,1,0:T(8,128)(2,1)} %get-tuple-element.310), channel_id=1, replica_groups=mesh['dp'=8,'head'=16] {'head'}, dimensions={0} | all-to-all | bytes 1048576 | tf_op jit(solution)/shard_map/all_to_all | solution.py:1380
  335.2 7.4 %back_scan.1 = (f32[16,128,128]{2,1,0:T(8,128)}, f32[16,128,128]{2,1,0:T(8,128)}, bf16[16,128,128]{2,1,0:T(8,128)(2,1)}, f32[8,128]{1,0:T(8,128)}) custom-call(s32[3,16]{1,0:T(4,128)} %pad_add_fusion.place_ref, bf16[16,128,256]{2,1,0:T(8,128)(2,1)} %get-tuple-element.272.mt_ref, f32[16,128,128]{2,1,0:T(8,128)} %get-tuple-element.235.r_ref, ...), custom_call_target="tpu_custom_call" | custom-call | flops 7000000 | bytes 1024 | tf_op jit(solution)/shard_map/back_scan/pallas_call | solution.py:401
  342.5 24.1 %back.1 = (bf16[1024,640]{1,0:T(8,128)(2,1)}, bf16[1024,640]{1,0:T(8,128)(2,1)}, f32[3,4,128]{2,1,0:T(4,128)}, f32[8,128]{1,0:T(8,128)}) custom-call(s32[3,16]{1,0:T(4,128)} %pad_add_fusion.place_ref, s32[32]{0:T(128)} %or_convert_fusion.starts_ref, f32[2,1]{1,0:T(2,128)} %copy.73.params_ref, f32[1024,640]{1,0:T(8,128)} %get-tuple-element.231.raw0_ref.gate0_ref, ...), custom_call_target="tpu_custom_call" | custom-call | flops 24000000 | bytes 1024 | tf_op jit(solution)/shard_map/back/pallas_call | solution.py:565
  368.7 13.0 %in_grads.1 = (bf16[4,512,640]{2,1,0:T(8,128)(2,1)}, f32[8,8,256]{2,1,0:T(8,128)}) custom-call(bf16[1024,2048]{1,0:T(8,128)(2,1)} %join.1.own_ref, bf16[1024,2048]{1,0:T(8,128)(2,1)} %collective-permute-done.10.other_ref, bf16[1024,640]{1,0:T(8,128)(2,1)} %get-tuple-element.324.draw0_ref.own_ref, bf16[1024,640]{1,0:T(8,128)(2,1)} %get-tuple-element.325.draw1_ref, ...), custom_call_target="tpu_custom_call" | custom-call | flops 8000000 | bytes 1024 | tf_op jit(solution)/shard_map/in_grads/pallas_call | solution.py:987
  382.8 13.1 %unproject.1 = (bf16[160,2048]{1,0:T(8,128)(2,1)}, bf16[160,2048]{1,0:T(8,128)(2,1)}, bf16[160,2048]{1,0:T(8,128)(2,1)}, bf16[160,2048]{1,0:T(8,128)(2,1)}, bf16...) custom-call(bf16[1024,640]{1,0:T(8,128)(2,1)} %get-tuple-element.324.draw0_ref.own_ref, bf16[1024,640]{1,0:T(8,128)(2,1)} %copy-done.11, ...), custom_call_target="tpu_custom_call" | custom-call | flops 8000000 | bytes 1024 | tf_op jit(solution)/shard_map/unproject/pallas_call | solution.py:927
  404.7 8.5 %out_grads.1.out_grad_ref = bf16[8,256,128]{2,1,0:T(8,128)(2,1)} custom-call(bf16[2048,2048]{1,0:T(8,128)(2,1)} %all-gather.7.cloned.1.call-done.rows_ref, bf16[2048,128]{1,0:T(8,128)(2,1)} %bitcast.41), custom_call_target="tpu_custom_call" | custom-call | flops 6000000 | bytes 1024 | tf_op jit(solution)/shard_map/out_grads/pallas_call | solution.py:1008
  424.0 8.0 %all-to-all-done.4.arrived_ref = bf16[4,512,640]{2,1,0:T(8,128)(2,1)S(1)} async-done(((bf16[4,512,640]{2,1,0:T(8,128)(2,1)}), bf16[4,512,640]{2,1,0:T(8,128)(2,1)S(1)}, u32[]{:S(2)}, u32[]{:S(2)}) %all-to-all-start.4) | async-done | bytes 2621472 | tf_op jit(solution)/shard_map/all_to_all | solution.py:840
  444.8 8.7 %collective-permute-done.47.refs_3_ = bf16[48,2048]{1,0:T(8,128)(2,1)} collective-permute-done((bf16[48,2048]{1,0:T(8,128)(2,1)}, bf16[48,2048]{1,0:T(8,128)(2,1)}, u32[]{:S(2)}, u32[]{:S(2)}) %collective-permute-start.47) | collective-permute-done | bytes 196640 | tf_op jit(solution)/shard_map/ppermute | solution.py:629
  473.7 10.1 %all-to-all-start.6 = ((f32[16,40,128]{2,1,0:T(8,128)}), f32[16,40,128]{2,1,0:T(8,128)S(1)}, u32[]{:S(2)}, u32[]{:S(2)}) async-start(f32[16,40,128]{2,1,0:T(8,128)} %broadcast_in_dim.35), calls=%async_computation.6 | async-start | bytes 655360 | tf_op jit(solution)/shard_map/all_to_all | solution.py:845
  (267 shorter events, 206.9 us)
Async XLA Ops:
  40.1 39.9 %all-to-all-start = ((bf16[4,2,256,768]{3,2,1,0:T(8,128)(2,1)}), bf16[4,2,256,768]{3,2,1,0:T(8,128)(2,1)S(1)}, u32[]{:S(2)}, u32[]{:S(2)}) async-start(bf16[4,2,256,768]{3,2,1,0:T(8,128)(2,1)} %spread_pair.1), calls=%async_computation | async-start | bytes 6291456 | tf_op jit(solution)/shard_map/all_to_all | solution.py:829
  44.3 90.8 %all-gather.9.cloned.1.call-start = ((), (), s32[]{:S(2)}) async-start(), calls=%async_computation.9 | async-start | bytes 8912896 | tf_op jit(solution)/shard_map/all_gather | solution.py:1350
  44.3 34.9 %collective-permute-start.8 = (bf16[192,2048]{1,0:T(8,128)(2,1)}, bf16[192,2048]{1,0:T(8,128)(2,1)}, u32[]{:S(2)}, u32[]{:S(2)}) collective-permute-start(bf16[192,2048]{1,0:T(8,128)(2,1)} %pad_maximum_fusion.1.refs_4_), channel_id=1, source_target_pairs={{2,0},{3,1},{0,2},{1,3},{6,4},{7,5},{4,6},{5,7},{10,8},{11,9},{8,1... | collective-permute-start | bytes 2359304 | tf_op jit(solution)/shard_map/ppermute | solution.py:629
  45.5 29.1 %collective-permute-start.7 = (bf16[160,2048]{1,0:T(8,128)(2,1)}, bf16[160,2048]{1,0:T(8,128)(2,1)S(1)}, u32[]{:S(2)}, u32[]{:S(2)}) collective-permute-start(bf16[160,2048]{1,0:T(8,128)(2,1)} %pad_maximum_fusion.2.refs_0_), channel_id=1, source_target_pairs={{12,0},{13,1},{14,2},{15,3},{0,4},{1,5},{2,6},{3,7},{4,8},{5,9},{6... | collective-permute-start | bytes 1966088 | tf_op jit(solution)/shard_map/ppermute | solution.py:629
  47.1 30.2 %collective-permute-start.6 = (bf16[160,2048]{1,0:T(8,128)(2,1)}, bf16[160,2048]{1,0:T(8,128)(2,1)S(1)}, u32[]{:S(2)}, u32[]{:S(2)}) collective-permute-start(bf16[160,2048]{1,0:T(8,128)(2,1)} %pad_maximum_fusion.2.refs_0_), channel_id=1, source_target_pairs={{8,0},{9,1},{10,2},{11,3},{12,4},{13,5},{14,6},{15,7},{0,8},{1,9},... | collective-permute-start | bytes 1966088 | tf_op jit(solution)/shard_map/ppermute | solution.py:629
  81.0 123.4 %all-gather.5.cloned.1.call-start = ((), (), s32[]{:S(2)}) async-start(), calls=%async_computation.7 | async-start | bytes 8912896 | tf_op jit(solution)/shard_map/all_gather | solution.py:1355
  92.3 40.8 %collective-permute-start.13 = (bf16[512,768]{1,0:T(8,128)(2,1)}, bf16[512,768]{1,0:T(8,128)(2,1)}, u32[]{:S(2)}, u32[]{:S(2)}) collective-permute-start(bf16[512,768]{1,0:T(8,128)(2,1)} %get-tuple-element.239.refs_0_), channel_id=1, source_target_pairs={{96,0},{112,16},{0,32},{16,48},{32,64},{48,80},{64,96},{80,112},{9... | collective-permute-start | bytes 2359304 | tf_op jit(solution)/shard_map/ppermute | solution.py:633
  93.0 40.1 %collective-permute-start.12 = (bf16[512,768]{1,0:T(8,128)(2,1)}, bf16[512,768]{1,0:T(8,128)(2,1)}, u32[]{:S(2)}, u32[]{:S(2)}) collective-permute-start(bf16[512,768]{1,0:T(8,128)(2,1)} %get-tuple-element.239.refs_0_), channel_id=1, source_target_pairs={{64,0},{80,16},{96,32},{112,48},{0,64},{16,80},{32,96},{48,112},{6... | collective-permute-start | bytes 2359304 | tf_op jit(solution)/shard_map/ppermute | solution.py:633
  95.4 37.7 %collective-permute-start.11 = (bf16[512,768]{1,0:T(8,128)(2,1)}, bf16[512,768]{1,0:T(8,128)(2,1)}, u32[]{:S(2)}, u32[]{:S(2)}) collective-permute-start(bf16[512,768]{1,0:T(8,128)(2,1)} %get-tuple-element.239.refs_0_), channel_id=1, source_target_pairs={{32,0},{48,16},{64,32},{80,48},{96,64},{112,80},{0,96},{16,112},{3... | collective-permute-start | bytes 2359304 | tf_op jit(solution)/shard_map/ppermute | solution.py:633
  140.4 255.4 %all-gather.7.cloned.1.call-start = ((), (), s32[]{:S(2)}) async-start(), calls=%async_computation.8 | async-start | bytes 8912896 | tf_op jit(solution)/shard_map/all_gather | solution.py:1385
  191.6 32.2 %collective-permute-start.24 = (bf16[256,2048]{1,0:T(8,128)(2,1)S(1)}, bf16[256,2048]{1,0:T(8,128)(2,1)}, u32[]{:S(2)}, u32[]{:S(2)}) collective-permute-start(bf16[256,2048]{1,0:T(8,128)(2,1)S(1)} %pad_maximum_fusion.refs_1_), channel_id=1, source_target_pairs={{2,0},{3,1},{0,2},{1,3},{6,4},{7,5},{4,6},{5,7},{10,8},{11,9},{8,1... | collective-permute-start | bytes 3145736 | tf_op jit(solution)/shard_map/ppermute | solution.py:629
  192.3 31.6 %collective-permute-start.22 = (bf16[128,2048]{1,0:T(8,128)(2,1)S(1)}, bf16[128,2048]{1,0:T(8,128)(2,1)}, u32[]{:S(2)}, u32[]{:S(2)}) collective-permute-start(bf16[128,2048]{1,0:T(8,128)(2,1)S(1)} %pad_maximum_fusion.3.refs_0_), channel_id=1, source_target_pairs={{8,0},{9,1},{10,2},{11,3},{12,4},{13,5},{14,6},{15,7},{0,8},{1,9},... | collective-permute-start | bytes 1572872 | tf_op jit(solution)/shard_map/ppermute | solution.py:629
  249.7 31.2 %collective-permute-start.30 = (bf16[256,2048]{1,0:T(8,128)(2,1)}, bf16[256,2048]{1,0:T(8,128)(2,1)S(1)}, u32[]{:S(2)}, u32[]{:S(2)}) collective-permute-start(bf16[256,2048]{1,0:T(8,128)(2,1)} %get-tuple-element.278), channel_id=1, source_target_pairs={{2,0},{3,1},{0,2},{1,3},{6,4},{7,5},{4,6},{5,7},{10,8},{11,9},{8,1... | collective-permute-start | bytes 3145736 | tf_op jit(solution)/shard_map/ppermute | solution.py:629
  312.6 54.0 %collective-permute-start.37 = (bf16[2048,768]{1,0:T(8,128)(2,1)S(1)}, bf16[2048,768]{1,0:T(8,128)(2,1)}, u32[]{:S(2)}, u32[]{:S(2)}) collective-permute-start(bf16[2048,768]{1,0:T(8,128)(2,1)S(1)} %bitcast.39), channel_id=1, source_target_pairs={{1,0},{0,1},{3,2},{2,3},{5,4},{4,5},{7,6},{6,7},{9,8},{8,9},{11,10... | collective-permute-start | bytes 9437192 | tf_op jit(solution)/shard_map/ppermute | solution.py:629
  330.1 65.7 %all-to-all-start.3 = ((bf16[4,512,1152]{2,1,0:T(8,128)(2,1)}), bf16[4,512,1152]{2,1,0:T(8,128)(2,1)}, u32[]{:S(2)}, u32[]{:S(2)}) async-start(bf16[4,512,1152]{2,1,0:T(8,128)(2,1)} %bitcast.40), calls=%async_computation.3 | async-start | bytes 9437184 | tf_op jit(solution)/shard_map/all_to_all | solution.py:840
  368.7 47.5 %collective-permute-start.36 = (bf16[512,2048]{1,0:T(8,128)(2,1)}, bf16[512,2048]{1,0:T(8,128)(2,1)}, u32[]{:S(2)}, u32[]{:S(2)}) collective-permute-start(bf16[512,2048]{1,0:T(8,128)(2,1)} %get-tuple-element.312), channel_id=1, source_target_pairs={{2,0},{3,1},{0,2},{1,3},{6,4},{7,5},{4,6},{5,7},{10,8},{11,9},{8,1... | collective-permute-start | bytes 6291464 | tf_op jit(solution)/shard_map/ppermute | solution.py:629
  395.9 36.1 %all-to-all-start.4 = ((bf16[4,512,640]{2,1,0:T(8,128)(2,1)}), bf16[4,512,640]{2,1,0:T(8,128)(2,1)S(1)}, u32[]{:S(2)}, u32[]{:S(2)}) async-start(bf16[4,512,640]{2,1,0:T(8,128)(2,1)} %get-tuple-element.356), calls=%async_computation.4 | async-start | bytes 5242880 | tf_op jit(solution)/shard_map/all_to_all | solution.py:840
  400.3 36.0 %collective-permute-start.42 = (bf16[192,2048]{1,0:T(8,128)(2,1)}, bf16[192,2048]{1,0:T(8,128)(2,1)S(1)}, u32[]{:S(2)}, u32[]{:S(2)}) collective-permute-start(bf16[192,2048]{1,0:T(8,128)(2,1)} %get-tuple-element.354), channel_id=1, source_target_pairs={{2,0},{3,1},{0,2},{1,3},{6,4},{7,5},{4,6},{5,7},{10,8},{11,9},{8,1... | collective-permute-start | bytes 2359304 | tf_op jit(solution)/shard_map/ppermute | solution.py:629
  401.8 34.5 %collective-permute-start.39 = (bf16[160,2048]{1,0:T(8,128)(2,1)}, bf16[160,2048]{1,0:T(8,128)(2,1)}, u32[]{:S(2)}, u32[]{:S(2)}) collective-permute-start(bf16[160,2048]{1,0:T(8,128)(2,1)} %get-tuple-element.351), channel_id=1, source_target_pairs={{12,0},{13,1},{14,2},{15,3},{0,4},{1,5},{2,6},{3,7},{4,8},{5,9},{6... | collective-permute-start | bytes 1966088 | tf_op jit(solution)/shard_map/ppermute | solution.py:629
  401.8 34.5 %collective-permute-start.40 = (bf16[160,2048]{1,0:T(8,128)(2,1)}, bf16[160,2048]{1,0:T(8,128)(2,1)}, u32[]{:S(2)}, u32[]{:S(2)}) collective-permute-start(bf16[160,2048]{1,0:T(8,128)(2,1)} %get-tuple-element.352), channel_id=1, source_target_pairs={{8,0},{9,1},{10,2},{11,3},{12,4},{13,5},{14,6},{15,7},{0,8},{1,9},... | collective-permute-start | bytes 1966088 | tf_op jit(solution)/shard_map/ppermute | solution.py:629
  402.1 34.2 %collective-permute-start.41 = (bf16[160,2048]{1,0:T(8,128)(2,1)}, bf16[160,2048]{1,0:T(8,128)(2,1)}, u32[]{:S(2)}, u32[]{:S(2)}) collective-permute-start(bf16[160,2048]{1,0:T(8,128)(2,1)} %get-tuple-element.353), channel_id=1, source_target_pairs={{4,0},{5,1},{6,2},{7,3},{8,4},{9,5},{10,6},{11,7},{12,8},{13,9},{1... | collective-permute-start | bytes 1966088 | tf_op jit(solution)/shard_map/ppermute | solution.py:629
  459.5 32.6 %collective-permute-start.43 = (bf16[128,2048]{1,0:T(8,128)(2,1)}, bf16[128,2048]{1,0:T(8,128)(2,1)S(1)}, u32[]{:S(2)}, u32[]{:S(2)}) collective-permute-start(bf16[128,2048]{1,0:T(8,128)(2,1)} %get-tuple-element.371), channel_id=1, source_target_pairs={{12,0},{13,1},{14,2},{15,3},{0,4},{1,5},{2,6},{3,7},{4,8},{5,9},{6... | collective-permute-start | bytes 1572872 | tf_op jit(solution)/shard_map/ppermute | solution.py:629
  460.2 32.0 %collective-permute-start.44 = (bf16[128,2048]{1,0:T(8,128)(2,1)}, bf16[128,2048]{1,0:T(8,128)(2,1)}, u32[]{:S(2)}, u32[]{:S(2)}) collective-permute-start(bf16[128,2048]{1,0:T(8,128)(2,1)} %get-tuple-element.372), channel_id=1, source_target_pairs={{8,0},{9,1},{10,2},{11,3},{12,4},{13,5},{14,6},{15,7},{0,8},{1,9},... | collective-permute-start | bytes 1572872 | tf_op jit(solution)/shard_map/ppermute | solution.py:629
  464.2 27.9 %collective-permute-start.50 = (bf16[256,1152]{1,0:T(8,128)(2,1)}, bf16[256,1152]{1,0:T(8,128)(2,1)S(1)}, u32[]{:S(2)}, u32[]{:S(2)}) collective-permute-start(bf16[256,1152]{1,0:T(8,128)(2,1)} %get-tuple-element.387), channel_id=1, source_target_pairs={{16,0},{0,16},{48,32},{32,48},{80,64},{64,80},{112,96},{96,112},{1... | collective-permute-start | bytes 1769480 | tf_op jit(solution)/shard_map/ppermute | solution.py:633
  (77 other events, 938.1 us)
Sparse Core Ops, SparseCore 0:
  81.1 54.0 all-gather.8
  136.9 67.4 all-gather.4
  312.7 55.9 all-gather.6
